TPU v7x, 32 devices: a whole 2x2x4 slice. The times are simulated.
32 devices in a mesh: row: 16 (over z, x, core), col: 2 (over y).
Axes of the slice: x: 2, y: 2, z: 4, core: 2. Of those that a mesh axis runs over, the one named last changes fastest.
Arguments:
- errors: bfloat16 [4096, 8192], P('col', 'row'), may hold values from -0.375 to 0.375
- inputs: bfloat16 [4096, 8192], P('row', 'col'), may hold values from -6 to 6
- weight: float32 [8192, 8192], P('row', 'col'), may hold values from -3 to 3
- weight_moment_one: bfloat16 [8192, 8192], P('row', 'col'), may hold values from -3 to 3
- weight_moment_two: bfloat16 [8192, 8192], P('row', 'col'), may hold values from 0.049804688 to 2
- feedback: float32 [2, 4096, 8192], P(None, 'row', 'col'), may hold values from -3 to 3
- feedback_moment_one: bfloat16 [2, 4096, 8192], P(None, 'row', 'col'), may hold values from -3 to 3
- feedback_moment_two: bfloat16 [2, 4096, 8192], P(None, 'row', 'col'), may hold values from 0.049804688 to 2
Outputs:
- new_weight: float32 [8192, 8192], P('row', 'col')
- new_weight_moment_one: bfloat16 [8192, 8192], P('row', 'col')
- new_weight_moment_two: bfloat16 [8192, 8192], P('row', 'col')
- weight_copy: bfloat16 [8192, 8192], P('row', 'col')
- new_feedback: float32 [2, 4096, 8192], P(None, 'row', 'col')
- new_feedback_moment_one: bfloat16 [2, 4096, 8192], P(None, 'row', 'col')
- new_feedback_moment_two: bfloat16 [2, 4096, 8192], P(None, 'row', 'col')
- feedback_copy: bfloat16 [2, 4096, 8192], P(None, 'row', 'col')
All inputs are finite; a program needn't handle non-finite values.
Results may differ from a plain program's by a relative error of at most 0.001.
Values may be sent and summed in bfloat16 or wider, within the bound.
No kernel may reach another device: no remote copies, remote signals or barrier semaphores. Data moves between devices by JAX's collectives and lax.ppermute only.
A program may use at most 192 MiB of HBM per device.

v0:
```python
import jax
import jax.numpy as jnp
from jax import lax
from jax.sharding import PartitionSpec as P

beta_one = 0.9
beta_two = 0.999
learn_rate = 0.02
decay_rate = 0.1
epsilon = 1e-08
bias_one = 1.0
bias_two = 0.63230458


def adam_update(master, moment_one, moment_two, gradient):
    first_new = beta_one * moment_one.astype(jnp.float32) + (1.0 - beta_one) * gradient
    second_new = beta_two * moment_two.astype(jnp.float32) + (1.0 - beta_two) * gradient * gradient
    update = first_new / bias_one / (jnp.sqrt(second_new / bias_two) + epsilon)
    master_new = master * (1.0 - learn_rate * decay_rate) - learn_rate * update
    return (
        master_new,
        first_new.astype(jnp.bfloat16),
        second_new.astype(jnp.bfloat16),
        master_new.astype(jnp.bfloat16),
    )


def token_product(left_rows, right_rows):
    return lax.dot_general(
        left_rows, right_rows, (((0,), (0,)), ((), ())), preferred_element_type=jnp.float32
    )


def shards(
    errors,
    inputs,
    weight,
    weight_moment_one,
    weight_moment_two,
    feedback,
    feedback_moment_one,
    feedback_moment_two,
):
    whole_inputs = lax.all_gather(inputs, "row", axis=0, tiled=True)
    gradient = token_product(lax.all_gather(errors, "col", axis=0, tiled=True), whole_inputs)
    w_master, w_first, w_second, w_copy = adam_update(
        weight, weight_moment_one, weight_moment_two, gradient
    )
    moved = lax.all_to_all(
        lax.all_to_all(gradient.T, "row", split_axis=0, concat_axis=1, tiled=True),
        "col",
        split_axis=1,
        concat_axis=0,
        tiled=True,
    )
    flipped = moved.reshape(feedback.shape)
    b_master, b_first, b_second, b_copy = adam_update(
        feedback, feedback_moment_one, feedback_moment_two, flipped
    )
    return (w_master, w_first, w_second, w_copy, b_master, b_first, b_second, b_copy)


def solution(mesh):
    return jax.shard_map(
        shards,
        mesh=mesh,
        in_specs=(
            P("col", "row"),
            P("row", "col"),
            P("row", "col"),
            P("row", "col"),
            P("row", "col"),
            P(None, "row", "col"),
            P(None, "row", "col"),
            P(None, "row", "col"),
        ),
        out_specs=(
            P("row", "col"),
            P("row", "col"),
            P("row", "col"),
            P("row", "col"),
            P(None, "row", "col"),
            P(None, "row", "col"),
            P(None, "row", "col"),
            P(None, "row", "col"),
        ),
        check_vma=False,
    )
```

profile of v0, /device:TPU:20, one launch (start us, length us, event | category | flops | bytes accessed | tf_op | source)
XLA Modules:
  0.0 611.1 jit_solution(5688584084527015114)
XLA Ops:
  7.2 0.0 all-gather.3.cloned.1.call-start
  7.2 0.7 all-gather.3.cloned.1.call-update
  7.9 0.0 all-gather.5.cloned.1.call-start
  7.9 0.7 all-gather.5.cloned.1.call-update
  8.7 57.8 %all-gather.3.cloned.1.call-done = bf16[4096,512]{1,0:T(8,128)(2,1)} async-done(((bf16[2048,512]{1,0:T(8,128)(2,1)}), bf16[4096,512]{1,0:T(8,128)(2,1)}) %all-gather.3.cloned.1.call-update) | async-done | bytes 4194320 | tf_op jit(solution)/shard_map/all_gather | solution.py:45
  66.4 170.6 %all-gather.5.cloned.1.call-done = bf16[4096,4096]{1,0:T(8,128)(2,1)} async-done(((bf16[256,4096]{1,0:T(8,128)(2,1)}), bf16[4096,4096]{1,0:T(8,128)(2,1)}) %all-gather.5.cloned.1.call-update) | async-done | bytes 33554448 | tf_op jit(solution)/shard_map/all_gather | solution.py:44
  237.0 33.1 %fusion.8 = (bf16[512,4096]{1,0:T(8,128)(2,1)}, f32[512,4096]{1,0:T(8,128)}, bf16[512,4096]{1,0:T(8,128)(2,1)}, bf16[512,4096]{1,0:T(8,128)(2,1)}, f32[512,4096]{1,0:T(8,128)S(1)}) fusion(bf16[512,4096]{1,0:T(8,128)(2,1)} %param.12, bf16[512,4096]{1,0:T(8,128)(2,1)} %param.11, f32[512,4096]{1,0:T(8,128)} %param.10, ...), kind=kOutput, calls=%fused_computation.15 | convolution fusion | flops 17217617920 | bytes 83886080 | tf_op jit(solution)/shard_map/dot_general | solution.py:29
  270.1 0.9 copy.26
  271.0 187.8 %all_to_all.32 = f32[16,256,512]{1,2,0:T(8,128)} all-to-all(f32[16,256,512]{1,2,0:T(8,128)S(1)} %bitcast.25), channel_id=1, replica_groups=mesh['row'=16,'col'=2] {'row'}, dimensions={0} | all-to-all | bytes 16777216 | tf_op jit(solution)/shard_map/all_to_all | solution.py:50
  458.8 7.5 %all-to-all-start.1 = ((f32[256,2,4096]{0,2,1:T(8,128)}), f32[256,2,4096]{0,2,1:T(8,128)}, u32[]{:S(2)}, u32[]{:S(2)}) async-start(f32[256,2,4096]{0,2,1:T(8,128)} %bitcast.24), calls=%async_computation.1 | async-start | bytes 16777216 | tf_op jit(solution)/shard_map/all_to_all | solution.py:49
  466.3 6.3 %copy.17 = bf16[2,256,4096]{1,2,0:T(8,128)(2,1)} copy(bf16[2,256,4096]{2,1,0:T(8,128)(2,1)} %param.14) | data formatting | bytes 8388608 | tf_op args[6]
  472.6 6.3 %copy.19 = bf16[2,256,4096]{1,2,0:T(8,128)(2,1)} copy(bf16[2,256,4096]{2,1,0:T(8,128)(2,1)} %param.15) | data formatting | bytes 8388608 | tf_op args[7]
  478.9 8.9 %copy.16 = f32[2,256,4096]{1,2,0:T(8,128)} copy(f32[2,256,4096]{2,1,0:T(8,128)} %param.13) | data formatting | bytes 16777216 | tf_op args[5]
  487.8 69.0 %all-to-all-done.1 = f32[256,2,4096]{0,2,1:T(8,128)} async-done(((f32[256,2,4096]{0,2,1:T(8,128)}), f32[256,2,4096]{0,2,1:T(8,128)}, u32[]{:S(2)}, u32[]{:S(2)}) %all-to-all-start.1) | async-done | bytes 8388640 | tf_op jit(solution)/shard_map/all_to_all | solution.py:49
  556.8 19.6 %fusion.7 = (bf16[2,256,4096]{1,2,0:T(8,128)(2,1)}, f32[2,256,4096]{1,2,0:T(8,128)}, bf16[2,256,4096]{1,2,0:T(8,128)(2,1)}, bf16[2,256,4096]{1,2,0:T(8,128)(2,1)}) fusion(bf16[2,256,4096]{1,2,0:T(8,128)(2,1)} %copy.19, f32[256,2,4096]{0,2,1:T(8,128)} %all-to-all-done.1, bf16[2,256,4096]{1,2,0:T(8,128)(2,1)} %copy.17, f32[2,256,4096]{1,2,0:T(8,128)} %copy.16), kind=kLoop, calls=%fused_computation.14 | loop fusion | flops 37748736 | bytes 46137344 | tf_op jit(solution)/shard_map/convert_element_type | solution.py:24
  576.4 6.3 %copy.23 = bf16[2,256,4096]{2,1,0:T(8,128)(2,1)} copy(bf16[2,256,4096]{1,2,0:T(8,128)(2,1)} %get-tuple-element.16) | data formatting | bytes 8388608
  582.7 6.3 %copy.22 = bf16[2,256,4096]{2,1,0:T(8,128)(2,1)} copy(bf16[2,256,4096]{1,2,0:T(8,128)(2,1)} %get-tuple-element.20) | data formatting | bytes 8388608
  589.0 6.3 %copy.21 = bf16[2,256,4096]{2,1,0:T(8,128)(2,1)} copy(bf16[2,256,4096]{1,2,0:T(8,128)(2,1)} %get-tuple-element.21) | data formatting | bytes 8388608
  595.3 8.9 %copy.20 = f32[2,256,4096]{2,1,0:T(8,128)} copy(f32[2,256,4096]{1,2,0:T(8,128)} %get-tuple-element.17) | data formatting | bytes 16777216
Async XLA Ops:
  7.2 59.3 %all-gather.3.cloned.1.call-start = ((), (), s32[]{:S(2)}) async-start(), calls=%async_computation.2 | async-start | bytes 6291456 | tf_op jit(solution)/shard_map/all_gather | solution.py:45
  7.9 229.1 %all-gather.5.cloned.1.call-start = ((), (), s32[]{:S(2)}) async-start(), calls=%async_computation.3 | async-start | bytes 35651584 | tf_op jit(solution)/shard_map/all_gather | solution.py:44
  458.8 98.0 %all-to-all-start.1 = ((f32[256,2,4096]{0,2,1:T(8,128)}), f32[256,2,4096]{0,2,1:T(8,128)}, u32[]{:S(2)}, u32[]{:S(2)}) async-start(f32[256,2,4096]{0,2,1:T(8,128)} %bitcast.24), calls=%async_computation.1 | async-start | bytes 16777216 | tf_op jit(solution)/shard_map/all_to_all | solution.py:49
Sparse Core Ops, SparseCore 0:
  9.5 56.8 all-gather.2
  68.0 168.9 all-gather.4
where the time goes:
time: 615 us; the launch traced here: 611 us
  waiting for transfers between devices  299 us (49%)
  blocking collectives  188 us (31%)
  local copies, waits for them, and re-layouts  50.3 us (8%)
  matrix products  33.1 us (5%)
  other arithmetic  19.6 us (3%)
  between operations  14.1 us (2%)
  starting transfers between devices  7.55 us (1%)
    all_to_all x1, blocking collectives, shards(): lax.all_to_all(gradient.T, 'row', split_axis=0, concat_axis=1, tiled=True)  188 us
    all_gather x1, waiting for transfers between devices, shards(): whole_inputs = lax.all_gather(inputs, 'row', axis=0, tiled=True)  171 us
    all_to_all x1, waiting for transfers between devices, shards(): lax.all_to_all(lax.all_to_all(gradient.T, 'row', split_axis=0, concat_axi...  69 us
    all_gather x1, waiting for transfers between devices, shards(): lax.all_gather(errors, 'col', axis=0, tiled=True)  57.8 us
    unnamed x7, local copies, waits for them, and re-layouts  49.4 us
    dot_general x1, matrix products, token_product(): lax.dot_general(left_rows, right_rows, (((0,), (0,)), ((), ())), preferre...  33.1 us
    convert_element_type x1, other arithmetic, adam_update(): master_new.astype(jnp.bfloat16)  19.6 us
  transfers between devices with their start and end apart: 3, of which 3 were waited for; matrix products, arithmetic and copies ran while one was open for 4% of the time, Pallas kernels for 0%

commit v1 on v0

v1 whole, which is shorter than its diff:
```python
import functools

import jax
import jax.numpy as jnp
from jax import lax
from jax.experimental import pallas as pl
from jax.experimental.pallas import tpu as pltpu
from jax.sharding import PartitionSpec as P

beta_one = 0.9
beta_two = 0.999
learn_rate = 0.02
decay_rate = 0.1
epsilon = 1e-08
bias_one = 1.0
bias_two = 0.63230458

POWER = 11
HEAD = 11.5

QUAD = 4


def adam_update(master, moment_one, moment_two, gradient):
    first_new = beta_one * moment_one.astype(jnp.float32) + (1.0 - beta_one) * gradient
    second_new = beta_two * moment_two.astype(jnp.float32) + (1.0 - beta_two) * gradient * gradient
    update = first_new / bias_one / (jnp.sqrt(second_new / bias_two) + epsilon)
    master_new = master * (1.0 - learn_rate * decay_rate) - learn_rate * update
    return (
        master_new,
        first_new.astype(jnp.bfloat16),
        second_new.astype(jnp.bfloat16),
        master_new.astype(jnp.bfloat16),
    )


def encode(gradient, inverse):
    u = gradient * inverse
    u2 = u * u
    u4 = u2 * u2
    return (u4 * u4 * u2 * u).astype(jnp.bfloat16)


def decode(code, scale):
    y = code.astype(jnp.float32)
    size = jnp.exp(jnp.log(jnp.abs(y)) * (1.0 / POWER)) * scale
    return jnp.where(y > 0.0, size, jnp.where(y < 0.0, -size, 0.0))


def my_place():
    row = lax.axis_index("row")
    return row // QUAD, row % QUAD, lax.axis_index("col")


def scalar_spec():
    return pl.BlockSpec(memory_space=pltpu.SMEM)


def any_specs(n):
    return [pl.BlockSpec(memory_space=pl.ANY)] * n


def product_kernel(line, n_col, tokens, outputs, error_at, n_errors, inverse_ref, *refs):
    share = line // n_col
    candidates, refs = refs[: 2 * line - 1], refs[2 * line - 1 :]
    errors, refs = refs[:n_errors], refs[n_errors:]
    to_line, to_quad, refs = refs[:line], refs[line : line + QUAD], refs[line + QUAD :]
    held, turned, whole, code, in_sem, error_sem, out_sem = refs
    layer, quarter, column = my_place()
    depth = QUAD * tokens
    width = held.shape[1]
    rows = width // line

    for n in range(line):
        source = (column ^ (n // share)) * share + n % share
        for i, candidate in enumerate(candidates):
            copy = pltpu.make_async_copy(candidate, held.at[pl.ds(n * depth, depth)], in_sem.at[n])
            pl.when(source - layer == i - (line - 1))(copy.start)
    for q in range(QUAD):
        for n in range(line):
            for d in range(QUAD):
                ref, start = error_at(n // share, q, n % share, quarter ^ d, column)
                pltpu.make_async_copy(
                    errors[ref].at[pl.ds(pl.multiple_of(start, tokens), tokens)],
                    whole.at[pl.ds(n * depth + d * tokens, tokens), pl.ds(q * outputs, outputs)],
                    error_sem.at[q],
                ).start()
    for n in range(line):
        part = held.at[pl.ds(n * depth, depth)]
        pltpu.make_async_copy(part, part, in_sem.at[n]).wait()

    step = 256 if width % 256 == 0 else width
    for w in range(width // step):

        @pl.loop(0, line * depth // 256)
        def _(i):
            at = pl.multiple_of(i * 256, 256)
            turned[:, pl.ds(at, 256)] = held[pl.ds(at, 256), pl.ds(w * step, step)].T

        for q in range(QUAD):
            part = whole.at[:, pl.ds(q * outputs, outputs)]
            if w == 0:
                pltpu.make_async_copy(part, part, error_sem.at[q]).wait()
            gradient = jnp.dot(turned[...], part[...], preferred_element_type=jnp.float32)
            code[pl.ds(w * step, step), pl.ds(q * outputs, outputs)] = encode(gradient, inverse_ref[0])

    copies = []
    for j in range(line):
        to = ((layer % share) * n_col + column) ^ j
        copies.append((code.at[pl.ds(pl.multiple_of(to * rows, 16), rows)], to_line[j]))
    for d in range(QUAD):
        copies.append((code.at[:, pl.ds(d * outputs, outputs)], to_quad[d]))
    copies = [pltpu.make_async_copy(a, b, out_sem.at[i]) for i, (a, b) in enumerate(copies)]
    for copy in copies:
        copy.start()
    for copy in copies:
        copy.wait()


def product(line, n_col, tokens, outputs, error_at, inverse, candidates, errors):
    width = candidates[0].shape[1]
    whole = (line * QUAD * tokens, QUAD * outputs)
    return pl.pallas_call(
        functools.partial(product_kernel, line, n_col, tokens, outputs, error_at, len(errors)),
        out_shape=[jax.ShapeDtypeStruct((width // line, QUAD * outputs), jnp.bfloat16)] * line
        + [jax.ShapeDtypeStruct((width, outputs), jnp.bfloat16)] * QUAD,
        in_specs=[scalar_spec()] + any_specs(len(candidates) + len(errors)),
        out_specs=any_specs(line + QUAD),
        scratch_shapes=[
            pltpu.VMEM((line * QUAD * tokens, width), jnp.bfloat16),
            pltpu.VMEM((256 if width % 256 == 0 else width, line * QUAD * tokens), jnp.bfloat16),
            pltpu.VMEM(whole, jnp.bfloat16),
            pltpu.VMEM((width, QUAD * outputs), jnp.bfloat16),
            pltpu.SemaphoreType.DMA((line,)),
            pltpu.SemaphoreType.DMA((QUAD,)),
            pltpu.SemaphoreType.DMA((line + QUAD,)),
        ],
        compiler_params=pltpu.CompilerParams(vmem_limit_bytes=56 * 2**20),
        cost_estimate=pl.CostEstimate(
            flops=2 * width * whole[0] * whole[1], bytes_accessed=2 * whole[0] * (whole[1] + width), transcendentals=0
        ),
        name="product",
    )(inverse, *candidates, *errors)


def weight_kernel(line, lows, scale_ref, *refs):
    n = len(lows)
    pieces, refs = refs[: n * QUAD], refs[n * QUAD :]
    master, one, two = refs[:3]
    outs, (held, sem) = refs[3:7], refs[7:]
    _, quarter, _ = my_place()

    @pl.when(pl.program_id(0) == 0)
    def _():
        copies = []
        for p, low in enumerate(lows):
            for d in range(QUAD):
                rows = pieces[p * QUAD + d].shape[0] // line
                for h in range(line):
                    copies.append(
                        pltpu.make_async_copy(
                            pieces[p * QUAD + d].at[pl.ds(h * rows, rows)],
                            held.at[h, quarter ^ d, pl.ds(low, rows)],
                            sem.at[len(copies)],
                        )
                    )
        for copy in copies:
            copy.start()
        for copy in copies:
            copy.wait()

    code = held[pl.program_id(0)]
    gradient = decode(code.reshape(code.shape[0] * code.shape[1], code.shape[2]), scale_ref[0]).T
    for out, value in zip(outs, adam_update(master[...], one[...], two[...], gradient)):
        out[...] = value


def weight_update(line, lows, scale, pieces, master, one, two):
    outputs, columns = master.shape
    tile = pl.BlockSpec((outputs, columns // line), lambda h: (0, h))
    return pl.pallas_call(
        functools.partial(weight_kernel, line, lows),
        grid=(line,),
        out_shape=[
            jax.ShapeDtypeStruct(master.shape, t) for t in (jnp.float32, jnp.bfloat16, jnp.bfloat16, jnp.bfloat16)
        ],
        in_specs=[scalar_spec()] + any_specs(len(pieces)) + [tile] * 3,
        out_specs=[tile] * 4,
        scratch_shapes=[
            pltpu.VMEM((line, QUAD, columns // line // QUAD, outputs), jnp.bfloat16),
            pltpu.SemaphoreType.DMA((len(lows) * QUAD * line,)),
        ],
        compiler_params=pltpu.CompilerParams(vmem_limit_bytes=56 * 2**20),
        cost_estimate=pl.CostEstimate(flops=0, bytes_accessed=20 * master.size, transcendentals=3 * master.size),
        name="weight_update",
    )(scale, *pieces, master, one, two)


def feedback_kernel(line, n_col, n_held, scale_ref, *refs):
    share = line // n_col
    pieces, refs = refs[:line], refs[line:]
    (master, one, two), refs = refs[:3], refs[3 + n_held :]
    outs, (held, sem) = refs[:4], refs[4:]
    layer, quarter, _ = my_place()
    outputs = held.shape[-1]

    @pl.when((pl.program_id(0) == 0) & (pl.program_id(1) == 0))
    def _():
        copies = []
        for j in range(line):
            source = layer ^ j
            for d in range(QUAD):
                copies.append(
                    pltpu.make_async_copy(
                        pieces[j].at[:, pl.ds(d * outputs, outputs)],
                        held.at[source % n_col, source // n_col, quarter ^ d],
                        sem.at[len(copies)],
                    )
                )
        for copy in copies:
            copy.start()
        for copy in copies:
            copy.wait()

    rows = master.shape[1]
    at = pl.ds(pl.multiple_of(pl.program_id(1) * rows, 16), rows)
    for s in range(share):
        for q in range(QUAD):
            lanes = pl.ds((s * QUAD + q) * outputs, outputs)
            gradient = decode(held[pl.program_id(0), s, q, at, :], scale_ref[0])
            values = adam_update(master[0, :, lanes], one[0, :, lanes], two[0, :, lanes], gradient)
            for out, value in zip(outs, values):
                out[0, :, lanes] = value


def feedback_update(line, n_col, low, scale, pieces, master, one, two, held):
    groups, _, width = master.shape
    span = pieces[0].shape[0]
    rows = 32 if span % 32 == 0 and low % 32 == 0 else 16
    tile = pl.BlockSpec((1, rows, width), lambda g, t: (g, low // rows + t, 0))
    return pl.pallas_call(
        functools.partial(feedback_kernel, line, n_col, len(held)),
        grid=(groups, span // rows),
        out_shape=[
            jax.ShapeDtypeStruct(master.shape, t) for t in (jnp.float32, jnp.bfloat16, jnp.bfloat16, jnp.bfloat16)
        ],
        in_specs=[scalar_spec()] + any_specs(line) + [tile] * 3 + any_specs(len(held)),
        out_specs=[tile] * 4,
        scratch_shapes=[
            pltpu.VMEM((n_col, line // n_col, QUAD, span, pieces[0].shape[1] // QUAD), jnp.bfloat16),
            pltpu.SemaphoreType.DMA((line * QUAD,)),
        ],
        input_output_aliases={1 + line + 3 + i: i for i in range(len(held))},
        compiler_params=pltpu.CompilerParams(vmem_limit_bytes=56 * 2**20),
        cost_estimate=pl.CostEstimate(
            flops=0, bytes_accessed=20 * groups * span * width, transcendentals=3 * groups * span * width
        ),
        name="feedback_update",
    )(scale, *pieces, master, one, two, *held)


def make(n_row, n_col):
    line = n_row // QUAD
    share = line // n_col

    def permute(x, move):
        pairs = []
        for r in range(n_row):
            for c in range(n_col):
                to = move(r // QUAD, r % QUAD, c)
                if to is not None:
                    pairs.append((r * n_col + c, (to[0] * QUAD + to[1]) * n_col + to[2]))
        return lax.ppermute(x, ("row", "col"), pairs)

    def along_quad(x, d):
        return permute(x, lambda h, q, c: (h, q ^ d, c))

    def along_col(x, d):
        return permute(x, lambda h, q, c: (h, q, c ^ d))

    def up(x, k):
        return permute(x, lambda h, q, c: (h + 1, q, c) if k <= h < line - 1 else None)

    def down(x, k):
        return permute(x, lambda h, q, c: (h - 1, q, c) if 0 < h < line - k else None)

    def gather_errors(errors, tokens):
        if n_col != 2:
            mine = lax.all_gather(errors, "col", axis=0, tiled=True)
            pieces = [mine] + [along_quad(mine, d) for d in range(1, QUAD)]

            def error_at(dc, dq, s, q, column):
                return dq, (((column ^ dc) * share + s) * QUAD + q) * tokens

            return pieces, error_at
        half = errors.shape[0] // 2
        by_col, by_x = along_col(errors, 1), along_quad(errors, 2)
        by_both = along_quad(by_col[:half], 2), along_col(by_x[half:], 1)
        near = [errors, by_col, by_x, *by_both]
        pieces = near + [along_quad(piece, 1) for piece in near]

        def error_at(dc, dq, s, q, column):
            core, x = dq % 2, dq // 2
            if dc and x and share > 1:
                late = s // (share // 2)
                return core * 5 + 3 + late, ((s - late * (share // 2)) * QUAD + q) * tokens
            return core * 5 + x * 2 + dc, (s * QUAD + q) * tokens

        return pieces, error_at

    def shards(
        errors,
        inputs,
        weight,
        weight_moment_one,
        weight_moment_two,
        feedback,
        feedback_moment_one,
        feedback_moment_two,
    ):
        layer, quarter, column = my_place()
        tokens = inputs.shape[0]
        block = inputs.shape[1] // n_row
        outputs = errors.shape[1]
        split = block * 3 // 4 // 16 * 16
        parts = ((0, split), (split, block))

        largest = jnp.stack([jnp.max(jnp.abs(errors)), jnp.max(jnp.abs(inputs))]).astype(jnp.float32)
        largest = lax.all_gather(jnp.broadcast_to(largest[:, None], (2, 128)), ("row", "col"), axis=0)
        largest = jnp.max(largest, axis=(0, 2))
        bound = largest[0] * largest[1] * (n_row * tokens)
        bound = jnp.where(bound > 0.0, bound, 1.0)
        inverse, scale = (2.0**HEAD / bound)[None], (bound * 2.0**-HEAD)[None]

        columns = inputs.reshape(tokens, line, QUAD, block)

        def of(q):
            taken = lax.dynamic_index_in_dim(columns, q, 2, keepdims=False)
            return jnp.concatenate([taken[:, :, a:b].reshape(tokens, -1) for a, b in parts], axis=1)

        own = [of(quarter)] + [along_quad(of(quarter ^ d), d) for d in range(1, QUAD)]
        gathered = []
        for a, b in parts:
            start = jnp.concatenate([piece[:, line * a : line * b] for piece in own], axis=0)
            ups, downs = [start], [start]
            for k in range(line - 1):
                ups.append(up(ups[-1], k))
                downs.append(down(downs[-1], k))
            gathered.append(ups[:0:-1] + downs)
        pieces, error_at = gather_errors(errors, tokens)

        for_weight, new_feedback = [], []
        for (a, b), candidates in zip(parts, gathered):
            codes = product(line, n_col, tokens, outputs, error_at, inverse, candidates, pieces)
            for_feedback = [
                permute(code, lambda h, q, c: (((h % share) * n_col + c) ^ j, q, h // share))
                for j, code in enumerate(codes[:line])
            ]
            for_weight += [along_quad(code, d) if d else code for d, code in enumerate(codes[line:])]
            new_feedback = feedback_update(
                line,
                n_col,
                a,
                scale,
                for_feedback,
                feedback,
                feedback_moment_one,
                feedback_moment_two,
                new_feedback,
            )
        new_weight = weight_update(
            line, tuple(a for a, _ in parts), scale, for_weight, weight, weight_moment_one, weight_moment_two
        )
        return (*new_weight, *new_feedback)

    return shards


def solution(mesh):
    forward, backward = P("row", "col"), P(None, "row", "col")
    return jax.shard_map(
        make(mesh.shape["row"], mesh.shape["col"]),
        mesh=mesh,
        in_specs=(P("col", "row"), forward, forward, forward, forward, backward, backward, backward),
        out_specs=(forward,) * 4 + (backward,) * 4,
        check_vma=False,
    )
```

time: 615 us -> 429 us (0.70)
  the two profiles are of different devices: /device:TPU:20 before, /device:TPU:1 now
where the time goes in v1:
time: 429 us; the launch traced here: 427 us
  waiting for transfers between devices  162 us (38%)
  starting transfers between devices  90.1 us (21%)
  Pallas kernels  89.7 us (21%)
  blocking collectives  50.1 us (12%)
  local copies, waits for them, and re-layouts  25.4 us (6%)
  other arithmetic  6.23 us (1%)
    ppermute x38, waiting for transfers between devices, permute(): return lax.ppermute(x, ('row', 'col'), pairs)  162 us
    ppermute x38, starting transfers between devices, permute(): return lax.ppermute(x, ('row', 'col'), pairs)  90.1 us
    unnamed x1, blocking collectives  50.1 us
    pallas_call x2, Pallas kernels, product(): pl.pallas_call(functools.partial(product_kernel, line, n_col, tokens, out...  43.9 us
    pallas_call x2, Pallas kernels, feedback_update(): pl.pallas_call(functools.partial(feedback_kernel, line, n_col, len(held))...  25.3 us
    pallas_call x1, Pallas kernels, weight_update(): pl.pallas_call(functools.partial(weight_kernel, line, lows), grid=(line,)...  20.5 us
  transfers between devices with their start and end apart: 38, of which 11 were waited for; matrix products, arithmetic and copies ran while one was open for 5% of the time, Pallas kernels for 16%

profile of v1, /device:TPU:1, one launch (start us, length us, event | category | flops | bytes accessed | tf_op | source)
XLA Modules:
  0.0 426.7 jit_solution(6087761694837479607)
XLA Ops:
  0.7 3.3 copy.58
  5.1 1.2 copy.61
  9.9 2.7 collective-permute-start.1
  12.6 1.2 copy.71
  17.1 1.7 collective-permute-start.9
  20.3 4.9 %collective-permute-done.1 = bf16[256,1024]{1,0:T(8,128)(2,1)} collective-permute-done((bf16[256,1024]{1,0:T(8,128)(2,1)}, bf16[256,1024]{1,0:T(8,128)(2,1)}, u32[]{:S(2)}, u32[]{:S(2)}) %collective-permute-start.1) | collective-permute-done | bytes 524320 | tf_op jit(solution)/shard_map/ppermute | solution.py:273
  26.1 10.5 %collective-permute-done.2 = bf16[256,1024]{1,0:T(8,128)(2,1)} collective-permute-done((bf16[256,1024]{1,0:T(8,128)(2,1)}, bf16[256,1024]{1,0:T(8,128)(2,1)}, u32[]{:S(2)}, u32[]{:S(2)}) %collective-permute-start.2) | collective-permute-done | bytes 524320 | tf_op jit(solution)/shard_map/ppermute | solution.py:273
  37.6 4.3 collective-permute-start.21
  43.0 1.3 collective-permute-start.24
  48.4 3.9 collective-permute-done.21.refs_2_
  53.2 4.8 %collective-permute-done.24.refs_4_ = bf16[1024,256]{1,0:T(8,128)(2,1)} collective-permute-done((bf16[1024,256]{1,0:T(8,128)(2,1)S(1)}, bf16[1024,256]{1,0:T(8,128)(2,1)}, u32[]{:S(2)}, u32[]{:S(2)}) %collective-permute-start.24) | collective-permute-done | bytes 524320 | tf_op jit(solution)/shard_map/ppermute | solution.py:273
  57.9 2.6 collective-permute-start.3
  60.5 1.3 collective-permute-start.6
  61.8 2.6 collective-permute-done.9.refs_8_
  64.4 1.3 collective-permute-start.25
  65.7 1.3 slice.82
  67.0 46.5 %collective-permute-done.25.refs_5_ = bf16[1024,256]{1,0:T(8,128)(2,1)S(1)} collective-permute-done((bf16[1024,256]{1,0:T(8,128)(2,1)}, bf16[1024,256]{1,0:T(8,128)(2,1)S(1)}, u32[]{:S(2)}, u32[]{:S(2)}) %collective-permute-start.25) | collective-permute-done | bytes 524320 | tf_op jit(solution)/shard_map/ppermute | solution.py:273
  115.4 1.3 slice.83
  116.8 1.3 collective-permute-start.12
  118.1 1.8 collective-permute-start.4
  119.9 1.3 collective-permute-start.7
  121.2 1.3 collective-permute-start.26
  122.5 12.2 %collective-permute-done.11.refs_10_ = bf16[1024,512]{1,0:T(8,128)(2,1)S(1)} collective-permute-done((bf16[1024,512]{1,0:T(8,128)(2,1)S(1)}, bf16[1024,512]{1,0:T(8,128)(2,1)S(1)}, u32[]{:S(2)}, u32[]{:S(2)}) %collective-permute-start.11) | collective-permute-done | bytes 1048608 | tf_op jit(solution)/shard_map/ppermute | solution.py:273
  134.7 4.4 %collective-permute-start.16 = (bf16[1024,512]{1,0:T(8,128)(2,1)S(1)}, bf16[1024,512]{1,0:T(8,128)(2,1)S(1)}, u32[]{:S(2)}, u32[]{:S(2)}) collective-permute-start(bf16[1024,512]{1,0:T(8,128)(2,1)S(1)} %collective-permute-done.11.refs_10_), channel_id=1, source_target_pairs={{0,2},{1,3},{2,0},{3,1},{4,6},{5,7},{6,4},{7,5},{8,10},{9,11},{10,... | collective-permute-start | bytes 3145736 | tf_op jit(solution)/shard_map/ppermute | solution.py:273
  139.1 27.9 %collective-permute-done.26.refs_6_ = bf16[1024,256]{1,0:T(8,128)(2,1)S(1)} collective-permute-done((bf16[1024,256]{1,0:T(8,128)(2,1)S(1)}, bf16[1024,256]{1,0:T(8,128)(2,1)S(1)}, u32[]{:S(2)}, u32[]{:S(2)}) %collective-permute-start.26) | collective-permute-done | bytes 524320 | tf_op jit(solution)/shard_map/ppermute | solution.py:273
  167.0 5.0 %collective-permute-start.14 = (bf16[2048,512]{1,0:T(8,128)(2,1)}, bf16[2048,512]{1,0:T(8,128)(2,1)}, u32[]{:S(2)}, u32[]{:S(2)}) collective-permute-start(bf16[2048,512]{1,0:T(8,128)(2,1)} %collective-permute-done.9.refs_8_), channel_id=1, source_target_pairs={{0,2},{1,3},{2,0},{3,1},{4,6},{5,7},{6,4},{7,5},{8,10},{9,11},{10,... | collective-permute-start | bytes 6291464 | tf_op jit(solution)/shard_map/ppermute | solution.py:273
  172.0 1.8 collective-permute-start.5
  173.8 1.3 collective-permute-start.8
  179.1 1.5 fusion
  180.6 50.1 %all-reduce = f32[64]{0:T(128)S(1)} all-reduce(f32[64]{0:T(128)S(1)} %fusion), channel_id=3, replica_groups=mesh['row'=16,'col'=2] {'row','col'}, use_global_device_ids=true, to_apply=%add | all-reduce | flops 64 | bytes 512
  233.1 14.5 %product.3 = (bf16[64,2048]{1,0:T(8,128)(2,1)}, bf16[64,2048]{1,0:T(8,128)(2,1)}, bf16[64,2048]{1,0:T(8,128)(2,1)}, bf16[64,2048]{1,0:T(8,128)(2,1)}, bf16[256,5...) custom-call(f32[1]{0:T(128)} %bitcast.4.inverse_ref, ...), custom_call_target="tpu_custom_call" | custom-call | flops 4294967296 | bytes 18874368 | tf_op jit(solution)/shard_map/product/pallas_call | solution.py:123
  247.7 1.7 collective-permute-start.30
  249.4 29.4 %product.2 = (bf16[192,2048]{1,0:T(8,128)(2,1)}, bf16[192,2048]{1,0:T(8,128)(2,1)}, bf16[192,2048]{1,0:T(8,128)(2,1)}, bf16[192,2048]{1,0:T(8,128)(2,1)}, bf16[7...) custom-call(f32[1]{0:T(128)} %bitcast.4.inverse_ref, ...), custom_call_target="tpu_custom_call" | custom-call | flops 12884901888 | bytes 23068672 | tf_op jit(solution)/shard_map/product/pallas_call | solution.py:123
  278.8 1.8 collective-permute-start.34
  280.6 3.5 collective-permute-start.35
  284.2 2.0 collective-permute-start.32
  286.2 4.3 collective-permute-start.33
  290.5 19.5 %collective-permute-done.31.refs_1_ = bf16[64,2048]{1,0:T(8,128)(2,1)S(1)} collective-permute-done((bf16[64,2048]{1,0:T(8,128)(2,1)S(1)}, bf16[64,2048]{1,0:T(8,128)(2,1)S(1)}, u32[]{:S(2)}, u32[]{:S(2)}) %collective-permute-start.31) | collective-permute-done | bytes 262176 | tf_op jit(solution)/shard_map/ppermute | solution.py:273
  310.6 2.7 collective-permute-start.27
  313.3 25.1 %collective-permute-start.36 = (bf16[192,2048]{1,0:T(8,128)(2,1)}, bf16[192,2048]{1,0:T(8,128)(2,1)}, u32[]{:S(2)}, u32[]{:S(2)}) collective-permute-start(bf16[192,2048]{1,0:T(8,128)(2,1)} %get-tuple-element.54), channel_id=1, source_target_pairs={{0,16},{1,24},{2,18},{3,26},{4,20},{5,28},{6,22},{7,30},{8,0},{9,8... | collective-permute-start | bytes 2359304 | tf_op jit(solution)/shard_map/ppermute | solution.py:273
  338.5 4.9 %collective-permute-start.37 = (bf16[192,2048]{1,0:T(8,128)(2,1)}, bf16[192,2048]{1,0:T(8,128)(2,1)}, u32[]{:S(2)}, u32[]{:S(2)}) collective-permute-start(bf16[192,2048]{1,0:T(8,128)(2,1)} %get-tuple-element.55), channel_id=1, source_target_pairs={{0,24},{1,16},{2,26},{3,18},{4,28},{5,20},{6,30},{7,22},{8,8},{9,0... | collective-permute-start | bytes 2359304 | tf_op jit(solution)/shard_map/ppermute | solution.py:273
  346.5 24.9 %collective-permute-done.36.refs_2_ = bf16[192,2048]{1,0:T(8,128)(2,1)} collective-permute-done((bf16[192,2048]{1,0:T(8,128)(2,1)}, bf16[192,2048]{1,0:T(8,128)(2,1)}, u32[]{:S(2)}, u32[]{:S(2)}) %collective-permute-start.36) | collective-permute-done | bytes 786464 | tf_op jit(solution)/shard_map/ppermute | solution.py:273
  371.4 1.2 collective-permute-start.28
  372.6 4.6 %collective-permute-done.37.refs_3_ = bf16[192,2048]{1,0:T(8,128)(2,1)} collective-permute-done((bf16[192,2048]{1,0:T(8,128)(2,1)}, bf16[192,2048]{1,0:T(8,128)(2,1)}, u32[]{:S(2)}, u32[]{:S(2)}) %collective-permute-start.37) | collective-permute-done | bytes 786464 | tf_op jit(solution)/shard_map/ppermute | solution.py:273
  377.2 2.3 collective-permute-start.29
  379.5 17.8 %feedback_update.2 = (f32[2,256,4096]{2,1,0:T(8,128)}, bf16[2,256,4096]{2,1,0:T(8,128)(2,1)}, bf16[2,256,4096]{2,1,0:T(8,128)(2,1)}, bf16[2,256,4096]{2,1,0:T(8,128)(2,1)}) custom-call(f32[1]{0:T(128)} %bitcast.3.scale_ref, bf16[192,2048]{1,0:T(8,128)(2,1)} %copy-done.6, bf16[192,2048]{1,0:T(8,128)(2,1)} %copy-done.7, ...), custom_call_target="tpu_custom_call" | custom-call | bytes 31457280 | tf_op jit(solution)/shard_map/feedback_update/pallas_call | solution.py:241
  397.3 7.5 %feedback_update.3 = (f32[2,256,4096]{2,1,0:T(8,128)}, bf16[2,256,4096]{2,1,0:T(8,128)(2,1)}, bf16[2,256,4096]{2,1,0:T(8,128)(2,1)}, bf16[2,256,4096]{2,1,0:T(8,128)(2,1)}) custom-call(f32[1]{0:T(128)} %bitcast.3.scale_ref, bf16[64,2048]{1,0:T(8,128)(2,1)} %copy-done.14, ...), custom_call_target="tpu_custom_call", output_to_operand_aliasing={{0}: (8, {}), {1}: (9, {}), {2}: (10, {}), {3}: (11, {})} | custom-call | bytes 10485760 | tf_op jit(solution)/shard_map/feedback_update/pallas_call | solution.py:241
  406.0 20.5 %weight_update.1 = (f32[512,4096]{1,0:T(8,128)}, bf16[512,4096]{1,0:T(8,128)(2,1)}, bf16[512,4096]{1,0:T(8,128)(2,1)}, bf16[512,4096]{1,0:T(8,128)(2,1)}) custom-call(f32[1]{0:T(128)} %bitcast.3.scale_ref, bf16[768,512]{1,0:T(8,128)(2,1)} %get-tuple-element.36.refs_0_, bf16[768,512]{1,0:T(8,128)(2,1)} %copy-done.8, bf16[768,512]{1,0:T(8,128)(2,1)} %copy-done.9, ...), custom_call_target="tpu_custom_call" | custom-call | bytes 41943040 | tf_op jit(solution)/shard_map/weight_update/pallas_call | solution.py:181
  (131 shorter events, 29.2 us)
Async XLA Ops:
  8.0 11.3 %collective-permute-start = (bf16[256,1024]{1,0:T(8,128)(2,1)}, bf16[256,1024]{1,0:T(8,128)(2,1)}, u32[]{:S(2)}, u32[]{:S(2)}) collective-permute-start(bf16[256,1024]{1,0:T(8,128)(2,1)} %pad_maximum_fusion.1), channel_id=1, source_target_pairs={{0,2},{1,3},{2,0},{3,1},{4,6},{5,7},{6,4},{7,5},{8,10},{9,11},{10,... | collective-permute-start | bytes 1572872 | tf_op jit(solution)/shard_map/ppermute | solution.py:273
  9.9 15.3 %collective-permute-start.1 = (bf16[256,1024]{1,0:T(8,128)(2,1)}, bf16[256,1024]{1,0:T(8,128)(2,1)}, u32[]{:S(2)}, u32[]{:S(2)}) collective-permute-start(bf16[256,1024]{1,0:T(8,128)(2,1)} %pad_maximum_fusion.2), channel_id=1, source_target_pairs={{0,4},{1,5},{2,6},{3,7},{4,0},{5,1},{6,2},{7,3},{8,12},{9,13},{10,... | collective-permute-start | bytes 1572872 | tf_op jit(solution)/shard_map/ppermute | solution.py:273
  17.1 19.5 %collective-permute-start.2 = (bf16[256,1024]{1,0:T(8,128)(2,1)}, bf16[256,1024]{1,0:T(8,128)(2,1)}, u32[]{:S(2)}, u32[]{:S(2)}) collective-permute-start(bf16[256,1024]{1,0:T(8,128)(2,1)} %pad_maximum_fusion.3), channel_id=1, source_target_pairs={{0,6},{1,7},{2,4},{3,5},{4,2},{5,3},{6,0},{7,1},{8,14},{9,15},{10,... | collective-permute-start | bytes 1572872 | tf_op jit(solution)/shard_map/ppermute | solution.py:273
  17.1 47.3 %collective-permute-start.9 = (bf16[2048,512]{1,0:T(8,128)(2,1)S(1)}, bf16[2048,512]{1,0:T(8,128)(2,1)}, u32[]{:S(2)}, u32[]{:S(2)}) collective-permute-start(bf16[2048,512]{1,0:T(8,128)(2,1)S(1)} %copy-done), channel_id=1, source_target_pairs={{0,1},{1,0},{2,3},{3,2},{4,5},{5,4},{6,7},{7,6},{8,9},{9,8},{10,11... | collective-permute-start | bytes 6291464 | tf_op jit(solution)/shard_map/ppermute | solution.py:273
  37.6 14.8 %collective-permute-start.21 = (bf16[1024,256]{1,0:T(8,128)(2,1)S(1)}, bf16[1024,256]{1,0:T(8,128)(2,1)}, u32[]{:S(2)}, u32[]{:S(2)}) collective-permute-start(bf16[1024,256]{1,0:T(8,128)(2,1)S(1)} %pad_maximum_fusion.4.refs_3_), channel_id=1, source_target_pairs={{0,8},{1,9},{2,10},{3,11},{4,12},{5,13},{6,14},{7,15},{8,16},{9,17... | collective-permute-start | bytes 1572872 | tf_op jit(solution)/shard_map/ppermute | solution.py:273
  41.8 72.9 %collective-permute-start.10 = (bf16[2048,512]{1,0:T(8,128)(2,1)S(1)}, bf16[2048,512]{1,0:T(8,128)(2,1)}, u32[]{:S(2)}, u32[]{:S(2)}) collective-permute-start(bf16[2048,512]{1,0:T(8,128)(2,1)S(1)} %copy-done), channel_id=1, source_target_pairs={{0,4},{1,5},{2,6},{3,7},{4,0},{5,1},{6,2},{7,3},{8,12},{9,13},{10,... | collective-permute-start | bytes 6291464 | tf_op jit(solution)/shard_map/ppermute | solution.py:273
  43.0 14.9 %collective-permute-start.24 = (bf16[1024,256]{1,0:T(8,128)(2,1)S(1)}, bf16[1024,256]{1,0:T(8,128)(2,1)}, u32[]{:S(2)}, u32[]{:S(2)}) collective-permute-start(bf16[1024,256]{1,0:T(8,128)(2,1)S(1)} %pad_maximum_fusion.4.refs_3_), channel_id=1, source_target_pairs={{8,0},{9,1},{10,2},{11,3},{12,4},{13,5},{14,6},{15,7},{16,8},{17,9... | collective-permute-start | bytes 1572872 | tf_op jit(solution)/shard_map/ppermute | solution.py:273
  44.3 75.6 %collective-permute-start.13 = (bf16[2048,512]{1,0:T(8,128)(2,1)S(1)}, bf16[2048,512]{1,0:T(8,128)(2,1)}, u32[]{:S(2)}, u32[]{:S(2)}) collective-permute-start(bf16[2048,512]{1,0:T(8,128)(2,1)S(1)} %copy-done), channel_id=1, source_target_pairs={{0,2},{1,3},{2,0},{3,1},{4,6},{5,7},{6,4},{7,5},{8,10},{9,11},{10,... | collective-permute-start | bytes 6291464 | tf_op jit(solution)/shard_map/ppermute | solution.py:273
  52.4 8.2 %collective-permute-start.22 = (bf16[1024,256]{1,0:T(8,128)(2,1)}, bf16[1024,256]{1,0:T(8,128)(2,1)S(1)}, u32[]{:S(2)}, u32[]{:S(2)}) collective-permute-start(bf16[1024,256]{1,0:T(8,128)(2,1)} %collective-permute-done.21.refs_2_), channel_id=1, source_target_pairs={{8,16},{9,17},{10,18},{11,19},{12,20},{13,21},{14,22},{15,23},{16,... | collective-permute-start | bytes 1572872 | tf_op jit(solution)/shard_map/ppermute | solution.py:273
  53.2 66.7 %copy-start.3 = (bf16[1024,768]{1,0:T(8,128)(2,1)}, bf16[1024,768]{1,0:T(8,128)(2,1)S(1)}, u32[]{:S(2)}) copy-start(bf16[1024,768]{1,0:T(8,128)(2,1)S(1)} %pad_maximum_fusion.refs_3_) | copy-start | bytes 4718596
  57.9 58.8 %collective-permute-start.3 = (bf16[1024,768]{1,0:T(8,128)(2,1)S(1)}, bf16[1024,768]{1,0:T(8,128)(2,1)S(1)}, u32[]{:S(2)}, u32[]{:S(2)}) collective-permute-start(bf16[1024,768]{1,0:T(8,128)(2,1)S(1)} %pad_maximum_fusion.refs_3_), channel_id=1, source_target_pairs={{0,8},{1,9},{2,10},{3,11},{4,12},{5,13},{6,14},{7,15},{8,16},{9,17... | collective-permute-start | bytes 4718600 | tf_op jit(solution)/shard_map/ppermute | solution.py:273
  60.5 116.0 %copy-start.10 = (bf16[1024,256]{1,0:T(8,128)(2,1)}, bf16[1024,256]{1,0:T(8,128)(2,1)S(1)}, u32[]{:S(2)}) copy-start(bf16[1024,256]{1,0:T(8,128)(2,1)S(1)} %collective-permute-done.22.refs_1_) | copy-start | bytes 1572868
  60.5 57.5 %collective-permute-start.6 = (bf16[1024,768]{1,0:T(8,128)(2,1)S(1)}, bf16[1024,768]{1,0:T(8,128)(2,1)S(1)}, u32[]{:S(2)}, u32[]{:S(2)}) collective-permute-start(bf16[1024,768]{1,0:T(8,128)(2,1)S(1)} %pad_maximum_fusion.refs_3_), channel_id=1, source_target_pairs={{8,0},{9,1},{10,2},{11,3},{12,4},{13,5},{14,6},{15,7},{16,8},{17,9... | collective-permute-start | bytes 4718600 | tf_op jit(solution)/shard_map/ppermute | solution.py:273
  64.4 49.1 %collective-permute-start.25 = (bf16[1024,256]{1,0:T(8,128)(2,1)}, bf16[1024,256]{1,0:T(8,128)(2,1)S(1)}, u32[]{:S(2)}, u32[]{:S(2)}) collective-permute-start(bf16[1024,256]{1,0:T(8,128)(2,1)} %collective-permute-done.24.refs_4_), channel_id=1, source_target_pairs={{8,0},{9,1},{10,2},{11,3},{12,4},{13,5},{14,6},{15,7},{16,8},{17,9... | collective-permute-start | bytes 1572872 | tf_op jit(solution)/shard_map/ppermute | solution.py:273
  113.5 63.0 %copy-start.11 = (bf16[1024,256]{1,0:T(8,128)(2,1)}, bf16[1024,256]{1,0:T(8,128)(2,1)S(1)}, u32[]{:S(2)}) copy-start(bf16[1024,256]{1,0:T(8,128)(2,1)S(1)} %collective-permute-done.25.refs_5_) | copy-start | bytes 1572868
  113.5 21.2 %collective-permute-start.11 = (bf16[1024,512]{1,0:T(8,128)(2,1)S(1)}, bf16[1024,512]{1,0:T(8,128)(2,1)S(1)}, u32[]{:S(2)}, u32[]{:S(2)}) collective-permute-start(bf16[1024,512]{1,0:T(8,128)(2,1)S(1)} %slice.82), channel_id=1, source_target_pairs={{0,4},{1,5},{2,6},{3,7},{4,0},{5,1},{6,2},{7,3},{8,12},{9,13},{10,... | collective-permute-start | bytes 3145736 | tf_op jit(solution)/shard_map/ppermute | solution.py:273
  114.7 6.5 %collective-permute-start.23 = (bf16[1024,256]{1,0:T(8,128)(2,1)S(1)}, bf16[1024,256]{1,0:T(8,128)(2,1)S(1)}, u32[]{:S(2)}, u32[]{:S(2)}) collective-permute-start(bf16[1024,256]{1,0:T(8,128)(2,1)S(1)} %collective-permute-done.22.refs_1_), channel_id=1, source_target_pairs={{16,24},{17,25},{18,26},{19,27},{20,28},{21,29},{22,30},{23,31}} | collective-permute-start | bytes 1572872 | tf_op jit(solution)/shard_map/ppermute | solution.py:273
  116.7 59.8 %copy-start.19 = (bf16[1024,768]{1,0:T(8,128)(2,1)}, bf16[1024,768]{1,0:T(8,128)(2,1)S(1)}, u32[]{:S(2)}) copy-start(bf16[1024,768]{1,0:T(8,128)(2,1)S(1)} %collective-permute-done.3.refs_2_) | copy-start | bytes 4718596
  116.8 55.2 %collective-permute-start.12 = (bf16[1024,512]{1,0:T(8,128)(2,1)S(1)}, bf16[1024,512]{1,0:T(8,128)(2,1)}, u32[]{:S(2)}, u32[]{:S(2)}) collective-permute-start(bf16[1024,512]{1,0:T(8,128)(2,1)S(1)} %slice.83), channel_id=1, source_target_pairs={{0,1},{1,0},{2,3},{3,2},{4,5},{5,4},{6,7},{7,6},{8,9},{9,8},{10,11... | collective-permute-start | bytes 3145736 | tf_op jit(solution)/shard_map/ppermute | solution.py:273
  118.1 58.5 %copy-start.20 = (bf16[1024,768]{1,0:T(8,128)(2,1)}, bf16[1024,768]{1,0:T(8,128)(2,1)S(1)}, u32[]{:S(2)}) copy-start(bf16[1024,768]{1,0:T(8,128)(2,1)S(1)} %collective-permute-done.6.refs_4_) | copy-start | bytes 4718596
  118.1 53.9 %collective-permute-start.4 = (bf16[1024,768]{1,0:T(8,128)(2,1)S(1)}, bf16[1024,768]{1,0:T(8,128)(2,1)}, u32[]{:S(2)}, u32[]{:S(2)}) collective-permute-start(bf16[1024,768]{1,0:T(8,128)(2,1)S(1)} %collective-permute-done.3.refs_2_), channel_id=1, source_target_pairs={{8,16},{9,17},{10,18},{11,19},{12,20},{13,21},{14,22},{15,23},{16,... | collective-permute-start | bytes 4718600 | tf_op jit(solution)/shard_map/ppermute | solution.py:273
  119.9 54.0 %collective-permute-start.7 = (bf16[1024,768]{1,0:T(8,128)(2,1)S(1)}, bf16[1024,768]{1,0:T(8,128)(2,1)}, u32[]{:S(2)}, u32[]{:S(2)}) collective-permute-start(bf16[1024,768]{1,0:T(8,128)(2,1)S(1)} %collective-permute-done.6.refs_4_), channel_id=1, source_target_pairs={{8,0},{9,1},{10,2},{11,3},{12,4},{13,5},{14,6},{15,7},{16,8},{17,9... | collective-permute-start | bytes 4718600 | tf_op jit(solution)/shard_map/ppermute | solution.py:273
  121.2 55.4 %copy-start.12 = (bf16[1024,256]{1,0:T(8,128)(2,1)}, bf16[1024,256]{1,0:T(8,128)(2,1)S(1)}, u32[]{:S(2)}) copy-start(bf16[1024,256]{1,0:T(8,128)(2,1)S(1)} %collective-permute-done.23.refs_0_) | copy-start | bytes 1572868
  121.2 45.7 %collective-permute-start.26 = (bf16[1024,256]{1,0:T(8,128)(2,1)S(1)}, bf16[1024,256]{1,0:T(8,128)(2,1)S(1)}, u32[]{:S(2)}, u32[]{:S(2)}) collective-permute-start(bf16[1024,256]{1,0:T(8,128)(2,1)S(1)} %collective-permute-done.25.refs_5_), channel_id=1, source_target_pairs={{8,0},{9,1},{10,2},{11,3},{12,4},{13,5},{14,6},{15,7}} | collective-permute-start | bytes 1572872 | tf_op jit(solution)/shard_map/ppermute | solution.py:273
  134.7 98.4 %copy-start.4 = (bf16[1024,512]{1,0:T(8,128)(2,1)}, bf16[1024,512]{1,0:T(8,128)(2,1)S(1)}, u32[]{:S(2)}) copy-start(bf16[1024,512]{1,0:T(8,128)(2,1)S(1)} %collective-permute-done.11.refs_10_) | copy-start | bytes 3145732
  134.7 40.4 %collective-permute-start.16 = (bf16[1024,512]{1,0:T(8,128)(2,1)S(1)}, bf16[1024,512]{1,0:T(8,128)(2,1)S(1)}, u32[]{:S(2)}, u32[]{:S(2)}) collective-permute-start(bf16[1024,512]{1,0:T(8,128)(2,1)S(1)} %collective-permute-done.11.refs_10_), channel_id=1, source_target_pairs={{0,2},{1,3},{2,0},{3,1},{4,6},{5,7},{6,4},{7,5},{8,10},{9,11},{10,... | collective-permute-start | bytes 3145736 | tf_op jit(solution)/shard_map/ppermute | solution.py:273
  167.0 66.1 %collective-permute-start.14 = (bf16[2048,512]{1,0:T(8,128)(2,1)}, bf16[2048,512]{1,0:T(8,128)(2,1)}, u32[]{:S(2)}, u32[]{:S(2)}) collective-permute-start(bf16[2048,512]{1,0:T(8,128)(2,1)} %collective-permute-done.9.refs_8_), channel_id=1, source_target_pairs={{0,2},{1,3},{2,0},{3,1},{4,6},{5,7},{6,4},{7,5},{8,10},{9,11},{10,... | collective-permute-start | bytes 6291464 | tf_op jit(solution)/shard_map/ppermute | solution.py:273
  171.9 61.1 %collective-permute-start.15 = (bf16[2048,512]{1,0:T(8,128)(2,1)}, bf16[2048,512]{1,0:T(8,128)(2,1)}, u32[]{:S(2)}, u32[]{:S(2)}) collective-permute-start(bf16[2048,512]{1,0:T(8,128)(2,1)} %collective-permute-done.10.refs_9_), channel_id=1, source_target_pairs={{0,2},{1,3},{2,0},{3,1},{4,6},{5,7},{6,4},{7,5},{8,10},{9,11},{10,... | collective-permute-start | bytes 6291464 | tf_op jit(solution)/shard_map/ppermute | solution.py:273
  172.0 77.4 %collective-permute-start.5 = (bf16[1024,768]{1,0:T(8,128)(2,1)}, bf16[1024,768]{1,0:T(8,128)(2,1)}, u32[]{:S(2)}, u32[]{:S(2)}) collective-permute-start(bf16[1024,768]{1,0:T(8,128)(2,1)} %collective-permute-done.4.refs_1_), channel_id=1, source_target_pairs={{16,24},{17,25},{18,26},{19,27},{20,28},{21,29},{22,30},{23,31}} | collective-permute-start | bytes 4718600 | tf_op jit(solution)/shard_map/ppermute | solution.py:273
  173.8 75.5 %collective-permute-start.8 = (bf16[1024,768]{1,0:T(8,128)(2,1)}, bf16[1024,768]{1,0:T(8,128)(2,1)}, u32[]{:S(2)}, u32[]{:S(2)}) collective-permute-start(bf16[1024,768]{1,0:T(8,128)(2,1)} %collective-permute-done.7.refs_5_), channel_id=1, source_target_pairs={{8,0},{9,1},{10,2},{11,3},{12,4},{13,5},{14,6},{15,7}} | collective-permute-start | bytes 4718600 | tf_op jit(solution)/shard_map/ppermute | solution.py:273
  176.1 56.9 %collective-permute-start.17 = (bf16[1024,512]{1,0:T(8,128)(2,1)}, bf16[1024,512]{1,0:T(8,128)(2,1)}, u32[]{:S(2)}, u32[]{:S(2)}) collective-permute-start(bf16[1024,512]{1,0:T(8,128)(2,1)} %collective-permute-done.12.refs_11_), channel_id=1, source_target_pairs={{0,2},{1,3},{2,0},{3,1},{4,6},{5,7},{6,4},{7,5},{8,10},{9,11},{10,... | collective-permute-start | bytes 3145736 | tf_op jit(solution)/shard_map/ppermute | solution.py:273
  247.6 38.6 %copy-start.22 = (bf16[64,2048]{1,0:T(8,128)(2,1)S(1)}, bf16[64,2048]{1,0:T(8,128)(2,1)}, u32[]{:S(2)}) copy-start(bf16[64,2048]{1,0:T(8,128)(2,1)} %get-tuple-element.51) | copy-start | bytes 786436
  247.6 63.0 %copy-start.21 = (bf16[256,512]{1,0:T(8,128)(2,1)S(1)}, bf16[256,512]{1,0:T(8,128)(2,1)}, u32[]{:S(2)}) copy-start(bf16[256,512]{1,0:T(8,128)(2,1)} %get-tuple-element.41) | copy-start | bytes 786436
  247.7 38.5 %collective-permute-start.30 = (bf16[64,2048]{1,0:T(8,128)(2,1)}, bf16[64,2048]{1,0:T(8,128)(2,1)S(1)}, u32[]{:S(2)}, u32[]{:S(2)}) collective-permute-start(bf16[64,2048]{1,0:T(8,128)(2,1)} %get-tuple-element.48), channel_id=1, source_target_pairs={{0,0},{1,8},{2,2},{3,10},{4,4},{5,12},{6,6},{7,14},{8,16},{9,24},{... | collective-permute-start | bytes 786440 | tf_op jit(solution)/shard_map/ppermute | solution.py:273
  278.8 66.0 %collective-permute-start.34 = (bf16[192,2048]{1,0:T(8,128)(2,1)}, bf16[192,2048]{1,0:T(8,128)(2,1)S(1)}, u32[]{:S(2)}, u32[]{:S(2)}) collective-permute-start(bf16[192,2048]{1,0:T(8,128)(2,1)} %get-tuple-element.52), channel_id=1, source_target_pairs={{0,0},{1,8},{2,2},{3,10},{4,4},{5,12},{6,6},{7,14},{8,16},{9,24},{... | collective-permute-start | bytes 2359304 | tf_op jit(solution)/shard_map/ppermute | solution.py:273
  280.6 65.2 %collective-permute-start.35 = (bf16[192,2048]{1,0:T(8,128)(2,1)}, bf16[192,2048]{1,0:T(8,128)(2,1)S(1)}, u32[]{:S(2)}, u32[]{:S(2)}) collective-permute-start(bf16[192,2048]{1,0:T(8,128)(2,1)} %get-tuple-element.53), channel_id=1, source_target_pairs={{0,8},{1,0},{2,10},{3,2},{4,12},{5,4},{6,14},{7,6},{8,24},{9,16},{... | collective-permute-start | bytes 2359304 | tf_op jit(solution)/shard_map/ppermute | solution.py:273
  284.1 25.9 %collective-permute-start.31 = (bf16[64,2048]{1,0:T(8,128)(2,1)S(1)}, bf16[64,2048]{1,0:T(8,128)(2,1)S(1)}, u32[]{:S(2)}, u32[]{:S(2)}) collective-permute-start(bf16[64,2048]{1,0:T(8,128)(2,1)S(1)} %copy-done.24), channel_id=1, source_target_pairs={{0,8},{1,0},{2,10},{3,2},{4,12},{5,4},{6,14},{7,6},{8,24},{9,16},{... | collective-permute-start | bytes 786440 | tf_op jit(solution)/shard_map/ppermute | solution.py:273
  284.2 29.2 %collective-permute-start.32 = (bf16[64,2048]{1,0:T(8,128)(2,1)S(1)}, bf16[64,2048]{1,0:T(8,128)(2,1)S(1)}, u32[]{:S(2)}, u32[]{:S(2)}) collective-permute-start(bf16[64,2048]{1,0:T(8,128)(2,1)S(1)} %copy-done.23), channel_id=1, source_target_pairs={{0,16},{1,24},{2,18},{3,26},{4,20},{5,28},{6,22},{7,30},{8,0},{9,8... | collective-permute-start | bytes 786440 | tf_op jit(solution)/shard_map/ppermute | solution.py:273
  286.2 111.1 %copy-start.14 = (bf16[64,2048]{1,0:T(8,128)(2,1)}, bf16[64,2048]{1,0:T(8,128)(2,1)S(1)}, u32[]{:S(2)}) copy-start(bf16[64,2048]{1,0:T(8,128)(2,1)S(1)} %collective-permute-done.30.refs_0_) | copy-start | bytes 786436
  286.2 52.3 %collective-permute-start.33 = (bf16[64,2048]{1,0:T(8,128)(2,1)S(1)}, bf16[64,2048]{1,0:T(8,128)(2,1)S(1)}, u32[]{:S(2)}, u32[]{:S(2)}) collective-permute-start(bf16[64,2048]{1,0:T(8,128)(2,1)S(1)} %copy-done.22), channel_id=1, source_target_pairs={{0,24},{1,16},{2,26},{3,18},{4,28},{5,20},{6,30},{7,22},{8,8},{9,0... | collective-permute-start | bytes 786440 | tf_op jit(solution)/shard_map/ppermute | solution.py:273
  310.6 32.8 %collective-permute-start.27 = (bf16[256,512]{1,0:T(8,128)(2,1)S(1)}, bf16[256,512]{1,0:T(8,128)(2,1)S(1)}, u32[]{:S(2)}, u32[]{:S(2)}) collective-permute-start(bf16[256,512]{1,0:T(8,128)(2,1)S(1)} %copy-done.21), channel_id=1, source_target_pairs={{0,2},{1,3},{2,0},{3,1},{4,6},{5,7},{6,4},{7,5},{8,10},{9,11},{10,... | collective-permute-start | bytes 786440 | tf_op jit(solution)/shard_map/ppermute | solution.py:273
  313.3 58.1 %collective-permute-start.36 = (bf16[192,2048]{1,0:T(8,128)(2,1)}, bf16[192,2048]{1,0:T(8,128)(2,1)}, u32[]{:S(2)}, u32[]{:S(2)}) collective-permute-start(bf16[192,2048]{1,0:T(8,128)(2,1)} %get-tuple-element.54), channel_id=1, source_target_pairs={{0,16},{1,24},{2,18},{3,26},{4,20},{5,28},{6,22},{7,30},{8,0},{9,8... | collective-permute-start | bytes 2359304 | tf_op jit(solution)/shard_map/ppermute | solution.py:273
  338.5 38.7 %collective-permute-start.37 = (bf16[192,2048]{1,0:T(8,128)(2,1)}, bf16[192,2048]{1,0:T(8,128)(2,1)}, u32[]{:S(2)}, u32[]{:S(2)}) collective-permute-start(bf16[192,2048]{1,0:T(8,128)(2,1)} %get-tuple-element.55), channel_id=1, source_target_pairs={{0,24},{1,16},{2,26},{3,18},{4,28},{5,20},{6,30},{7,22},{8,8},{9,0... | collective-permute-start | bytes 2359304 | tf_op jit(solution)/shard_map/ppermute | solution.py:273
  344.1 60.7 %collective-permute-start.18 = (bf16[768,512]{1,0:T(8,128)(2,1)}, bf16[768,512]{1,0:T(8,128)(2,1)S(1)}, u32[]{:S(2)}, u32[]{:S(2)}) collective-permute-start(bf16[768,512]{1,0:T(8,128)(2,1)} %get-tuple-element.37), channel_id=1, source_target_pairs={{0,2},{1,3},{2,0},{3,1},{4,6},{5,7},{6,4},{7,5},{8,10},{9,11},{10,... | collective-permute-start | bytes 2359304 | tf_op jit(solution)/shard_map/ppermute | solution.py:273
  344.8 60.1 %collective-permute-start.19 = (bf16[768,512]{1,0:T(8,128)(2,1)}, bf16[768,512]{1,0:T(8,128)(2,1)S(1)}, u32[]{:S(2)}, u32[]{:S(2)}) collective-permute-start(bf16[768,512]{1,0:T(8,128)(2,1)} %get-tuple-element.38), channel_id=1, source_target_pairs={{0,4},{1,5},{2,6},{3,7},{4,0},{5,1},{6,2},{7,3},{8,12},{9,13},{10,... | collective-permute-start | bytes 2359304 | tf_op jit(solution)/shard_map/ppermute | solution.py:273
  345.8 59.0 %collective-permute-start.20 = (bf16[768,512]{1,0:T(8,128)(2,1)}, bf16[768,512]{1,0:T(8,128)(2,1)}, u32[]{:S(2)}, u32[]{:S(2)}) collective-permute-start(bf16[768,512]{1,0:T(8,128)(2,1)} %get-tuple-element.39), channel_id=1, source_target_pairs={{0,6},{1,7},{2,4},{3,5},{4,2},{5,3},{6,0},{7,1},{8,14},{9,15},{10,... | collective-permute-start | bytes 2359304 | tf_op jit(solution)/shard_map/ppermute | solution.py:273
  371.4 33.4 %collective-permute-start.28 = (bf16[256,512]{1,0:T(8,128)(2,1)}, bf16[256,512]{1,0:T(8,128)(2,1)}, u32[]{:S(2)}, u32[]{:S(2)}) collective-permute-start(bf16[256,512]{1,0:T(8,128)(2,1)} %get-tuple-element.42), channel_id=1, source_target_pairs={{0,4},{1,5},{2,6},{3,7},{4,0},{5,1},{6,2},{7,3},{8,12},{9,13},{10,... | collective-permute-start | bytes 786440 | tf_op jit(solution)/shard_map/ppermute | solution.py:273
  377.2 27.6 %collective-permute-start.29 = (bf16[256,512]{1,0:T(8,128)(2,1)}, bf16[256,512]{1,0:T(8,128)(2,1)}, u32[]{:S(2)}, u32[]{:S(2)}) collective-permute-start(bf16[256,512]{1,0:T(8,128)(2,1)} %get-tuple-element.43), channel_id=1, source_target_pairs={{0,6},{1,7},{2,4},{3,5},{4,2},{5,3},{6,0},{7,1},{8,14},{9,15},{10,... | collective-permute-start | bytes 786440 | tf_op jit(solution)/shard_map/ppermute | solution.py:273
  (15 other events, 215.8 us)

commit v2 on v1

v2 whole, which is shorter than its diff:
```python
import functools
import math

import jax
import jax.numpy as jnp
from jax import lax
from jax.experimental import pallas as pl
from jax.experimental.pallas import tpu as pltpu
from jax.sharding import PartitionSpec as P

beta_one = 0.9
beta_two = 0.999
learn_rate = 0.02
decay_rate = 0.1
epsilon = 1e-08
bias_one = 1.0
bias_two = 0.63230458

POWER = 13
HEAD = 9.7

BRIEF = pl.CostEstimate(flops=0, bytes_accessed=0, transcendentals=0)

QUAD = 4


def adam_update(master, moment_one, moment_two, gradient):
    first_new = beta_one * moment_one.astype(jnp.float32) + (1.0 - beta_one) * gradient
    second_new = beta_two * moment_two.astype(jnp.float32) + (1.0 - beta_two) * gradient * gradient
    corrected = second_new * (1.0 / bias_two)
    divisor = corrected * lax.rsqrt(corrected) + epsilon
    inverse = pl.reciprocal(divisor, approx=True)
    inverse = inverse * (2.0 - divisor * inverse)
    master_new = master * (1.0 - learn_rate * decay_rate) - (learn_rate / bias_one) * first_new * inverse
    return (
        master_new,
        first_new.astype(jnp.bfloat16),
        second_new.astype(jnp.bfloat16),
        master_new.astype(jnp.bfloat16),
    )


def encode(gradient, inverse):
    u = gradient * inverse
    u2 = u * u
    u4 = u2 * u2
    return (u4 * u4 * u4 * u).astype(jnp.bfloat16)


def decode(code, scale):
    y = code.astype(jnp.float32)
    size = jnp.exp2(jnp.log(jnp.abs(y)) * (1.0 / (POWER * math.log(2.0)))) * scale
    return jnp.where(y < 0.0, -size, size)


def slot(layer, column, share):
    return column * share + (layer + column) % share


def unslot(index, share):
    return index // share, (index + index // share * (share - 1)) % share


def my_place():
    row = lax.axis_index("row")
    return row // QUAD, row % QUAD, lax.axis_index("col")


def scalar_spec():
    return pl.BlockSpec(memory_space=pltpu.SMEM)


def any_specs(n):
    return [pl.BlockSpec(memory_space=pl.ANY)] * n


def after(value, *others):
    return lax.optimization_barrier((value, *others))[0]


def pack_kernel(line, x_ref, *outs):
    _, quarter, _ = my_place()
    block = x_ref.shape[1] // (line * QUAD)
    for d, out in enumerate(outs):
        for h in range(line):
            start = pl.multiple_of((h * QUAD + (quarter ^ d)) * block, block)
            out[:, pl.ds(h * block, block)] = x_ref[:, pl.ds(start, block)]


def pack(line, x):
    return pl.pallas_call(
        functools.partial(pack_kernel, line),
        out_shape=[jax.ShapeDtypeStruct((x.shape[0], x.shape[1] // QUAD), x.dtype)] * QUAD,
        in_specs=[pl.BlockSpec(memory_space=pltpu.VMEM)],
        out_specs=[pl.BlockSpec(memory_space=pltpu.VMEM)] * QUAD,
        compiler_params=pltpu.CompilerParams(vmem_limit_bytes=32 * 2**20),
        cost_estimate=BRIEF,
        name="pack",
    )(x)


def product_kernel(line, n_col, tokens, outputs, depths, inverse_ref, *refs):
    share = line // n_col
    reach = 2 * line - 1
    candidates, refs = refs[: len(depths) * reach], refs[len(depths) * reach :]
    errors, refs = refs[0], refs[1:]
    to_line, to_quad, refs = refs[:line], refs[line : line + QUAD], refs[line + QUAD :]
    held, turned, whole, code, in_sem, error_sem, out_sem = refs
    layer, quarter, column = my_place()
    depth = QUAD * tokens
    width = held.shape[1]
    rows = width // line

    for n in range(line):
        source = (column ^ (n // share)) * share + n % share
        start = n * depth
        for g, slab in enumerate(depths):
            for i, candidate in enumerate(candidates[g * reach : (g + 1) * reach]):
                copy = pltpu.make_async_copy(candidate, held.at[pl.ds(start, slab)], in_sem.at[n])
                pl.when(source - layer == i - (line - 1))(copy.start)
            start += slab
    for q in range(QUAD):
        for n in range(line):
            for d in range(QUAD):
                start = (column ^ (n // share)) * QUAD + (quarter ^ q)
                start = ((start * share + n % share) * QUAD + (quarter ^ d)) * tokens
                pltpu.make_async_copy(
                    errors.at[pl.ds(pl.multiple_of(start, tokens), tokens)],
                    whole.at[pl.ds(n * depth + d * tokens, tokens), pl.ds(q * outputs, outputs)],
                    error_sem.at[q],
                ).start()
    for n in range(line):
        part = held.at[pl.ds(n * depth, depth)]
        pltpu.make_async_copy(part, part, in_sem.at[n]).wait()

        @pl.loop(n * depth // 256, (n + 1) * depth // 256)
        def _(i):
            at = pl.multiple_of(i * 256, 256)
            turned[:, pl.ds(at, 256)] = held[pl.ds(at, 256), :].T

    copies = []
    for q in range(QUAD):
        lanes = pl.ds(q * outputs, outputs)
        part = whole.at[:, lanes]
        pltpu.make_async_copy(part, part, error_sem.at[q]).wait()
        gradient = jnp.dot(turned[...], part[...], preferred_element_type=jnp.float32)
        code[:, lanes] = encode(gradient, inverse_ref[0])
        ready = [(code.at[:, lanes], to_quad[q])]
        for j in range(line):
            to = slot(layer, column, share) ^ j
            at = pl.ds(pl.multiple_of(to * rows, 16), rows)
            ready.append((code.at[at, lanes], to_line[j].at[:, lanes]))
        for source, target in ready:
            copies.append(pltpu.make_async_copy(source, target, out_sem.at[len(copies)]))
            copies[-1].start()
    for copy in copies:
        copy.wait()


def product(line, n_col, tokens, outputs, inverse, groups, errors):
    width = groups[0][0].shape[1]
    whole = (line * QUAD * tokens, QUAD * outputs)
    depths = [group[0].shape[0] for group in groups]
    candidates = [candidate for group in groups for candidate in group]
    return pl.pallas_call(
        functools.partial(product_kernel, line, n_col, tokens, outputs, depths),
        out_shape=[jax.ShapeDtypeStruct((width // line, QUAD * outputs), jnp.bfloat16)] * line
        + [jax.ShapeDtypeStruct((width, outputs), jnp.bfloat16)] * QUAD,
        in_specs=[scalar_spec()] + any_specs(len(candidates) + 1),
        out_specs=any_specs(line + QUAD),
        scratch_shapes=[
            pltpu.VMEM((line * QUAD * tokens, width), jnp.bfloat16),
            pltpu.VMEM((width, line * QUAD * tokens), jnp.bfloat16),
            pltpu.VMEM(whole, jnp.bfloat16),
            pltpu.VMEM((width, QUAD * outputs), jnp.bfloat16),
            pltpu.SemaphoreType.DMA((line,)),
            pltpu.SemaphoreType.DMA((QUAD,)),
            pltpu.SemaphoreType.DMA(((line + 1) * QUAD,)),
        ],
        compiler_params=pltpu.CompilerParams(vmem_limit_bytes=56 * 2**20),
        cost_estimate=BRIEF,
        name="product",
    )(inverse, *candidates, errors)


def weight_kernel(line, scale_ref, *refs):
    pieces, refs = refs[:QUAD], refs[QUAD:]
    master, one, two = refs[:3]
    outs, (held, sem) = refs[3:7], refs[7:]
    _, quarter, _ = my_place()

    @pl.when(pl.program_id(0) == 0)
    def _():
        copies = []
        for d, piece in enumerate(pieces):
            rows = piece.shape[0] // line
            for h in range(line):
                source, target = piece.at[pl.ds(h * rows, rows)], held.at[h, quarter ^ d]
                copies.append(pltpu.make_async_copy(source, target, sem.at[len(copies)]))
        for copy in copies:
            copy.start()
        for copy in copies:
            copy.wait()

    code = held[pl.program_id(0)]
    gradient = decode(code.reshape(code.shape[0] * code.shape[1], code.shape[2]), scale_ref[0]).T
    for out, value in zip(outs, adam_update(master[...], one[...], two[...], gradient)):
        out[...] = value


def weight_update(line, scale, pieces, master, one, two):
    outputs, columns = master.shape
    tile = pl.BlockSpec((outputs, columns // line), lambda h: (0, h))
    return pl.pallas_call(
        functools.partial(weight_kernel, line),
        grid=(line,),
        out_shape=[
            jax.ShapeDtypeStruct(master.shape, t) for t in (jnp.float32, jnp.bfloat16, jnp.bfloat16, jnp.bfloat16)
        ],
        in_specs=[scalar_spec()] + any_specs(len(pieces)) + [tile] * 3,
        out_specs=[tile] * 4,
        scratch_shapes=[
            pltpu.VMEM((line, QUAD, columns // line // QUAD, outputs), jnp.bfloat16),
            pltpu.SemaphoreType.DMA((QUAD * line,)),
        ],
        compiler_params=pltpu.CompilerParams(vmem_limit_bytes=56 * 2**20),
        cost_estimate=BRIEF,
        name="weight_update",
    )(scale, *pieces, master, one, two)


def feedback_kernel(line, odd, n_held, _, scale_ref, *refs):
    pieces, refs = refs[: line // 2], refs[line // 2 :]
    (master, one, two), refs = refs[:3], refs[3 + n_held :]
    outs, (held, sem) = refs[:4], refs[4:]
    layer, quarter, _ = my_place()
    outputs = held.shape[-1]

    @pl.when((pl.program_id(0) == 0) & (pl.program_id(1) == 0))
    def _():
        copies = []
        for i, piece in enumerate(pieces):
            half = (layer ^ (2 * i + odd)) // 2
            for d in range(QUAD):
                source, target = piece.at[:, pl.ds(d * outputs, outputs)], held.at[half, quarter ^ d]
                copies.append(pltpu.make_async_copy(source, target, sem.at[len(copies)]))
        for copy in copies:
            copy.start()
        for copy in copies:
            copy.wait()

    rows = master.shape[1]
    at = pl.ds(pl.multiple_of(pl.program_id(1) * rows, 16), rows)
    for q in range(QUAD):
        lanes = pl.ds(q * outputs, outputs)
        gradient = decode(held[pl.program_id(0), q, at, :], scale_ref[0])
        values = adam_update(master[0, :, lanes], one[0, :, lanes], two[0, :, lanes], gradient)
        for out, value in zip(outs, values):
            out[0, :, lanes] = value


def feedback_update(line, share, odd, scale, pieces, master, one, two, held):
    block, width = master.shape[1], master.shape[2] // share
    rows = 64 if block % 64 == 0 else block

    def place(i, t, first):
        group, s = unslot(2 * i + first[0], share)
        return group, t, s

    tile = pl.BlockSpec((1, rows, width), place)
    first = ((my_place()[0] ^ odd) % 2)[None].astype(jnp.int32)
    return pl.pallas_call(
        functools.partial(feedback_kernel, line, odd, len(held)),
        grid_spec=pltpu.PrefetchScalarGridSpec(
            num_scalar_prefetch=1,
            grid=(line // 2, block // rows),
            in_specs=[scalar_spec()] + any_specs(line // 2) + [tile] * 3 + any_specs(len(held)),
            out_specs=[tile] * 4,
            scratch_shapes=[
                pltpu.VMEM((line // 2, QUAD, block, width // QUAD), jnp.bfloat16),
                pltpu.SemaphoreType.DMA((line // 2 * QUAD,)),
            ],
        ),
        out_shape=[
            jax.ShapeDtypeStruct(master.shape, t) for t in (jnp.float32, jnp.bfloat16, jnp.bfloat16, jnp.bfloat16)
        ],
        input_output_aliases={2 + line // 2 + 3 + i: i for i in range(len(held))},
        compiler_params=pltpu.CompilerParams(vmem_limit_bytes=56 * 2**20),
        cost_estimate=BRIEF,
        name="feedback_update",
    )(first, scale, *pieces, master, one, two, *held)


def make(n_row, n_col):
    line = n_row // QUAD
    share = line // n_col

    def permute(x, move):
        pairs = []
        for r in range(n_row):
            for c in range(n_col):
                to = move(r // QUAD, r % QUAD, c)
                if to is not None:
                    pairs.append((r * n_col + c, (to[0] * QUAD + to[1]) * n_col + to[2]))
        return lax.ppermute(x, ("row", "col"), pairs)

    def flipped_pairs(bit):
        return [(i, i ^ bit) for i in range(n_row * n_col)]

    def along_quad(x, d):
        return permute(x, lambda h, q, c: (h, q ^ d, c))

    def along_col(x, d):
        return permute(x, lambda h, q, c: (h, q, c ^ d))

    def up(x, k):
        return permute(x, lambda h, q, c: (h + 1, q, c) if k <= h < line - 1 else None)

    def down(x, k):
        return permute(x, lambda h, q, c: (h - 1, q, c) if 0 < h < line - k else None)

    layers = [
        [(h * QUAD + q) * n_col + c for c in range(n_col) for q in range(QUAD)] for h in range(line)
    ]

    def shards(
        errors,
        inputs,
        weight,
        weight_moment_one,
        weight_moment_two,
        feedback,
        feedback_moment_one,
        feedback_moment_two,
    ):
        layer, quarter, column = my_place()
        tokens = inputs.shape[0]
        block = inputs.shape[1] // n_row
        outputs = errors.shape[1]

        squares = [jnp.max(jnp.sum(jnp.square(x.astype(jnp.float32) * 2.0**40), axis=0)) for x in (errors, inputs)]
        squares = jnp.stack(squares)
        squares_of_line = ()
        for bit in reversed(range((n_row * n_col).bit_length() - 1)):
            if (1 << bit) < n_col * QUAD and not isinstance(squares_of_line, jax.Array):
                squares_of_line = squares
            others = lax.ppermute(squares, ("row", "col"), flipped_pairs(1 << bit))
            added = jnp.array([(1 << bit) < n_col, (1 << bit) >= n_col])
            squares = jnp.where(added, squares + others, jnp.maximum(squares, others))
        lengths = jnp.sqrt(squares) * 2.0**-40
        bound = lengths[0] * lengths[1] * 1.01
        bound = jnp.where(bound > 0.0, bound, 1.0)
        inverse, scale = (2.0**HEAD / bound)[None], (bound * 2.0**-HEAD)[None]

        if block % 128 == 0:
            own = pack(line, inputs)
        else:
            columns = inputs.reshape(tokens, line, QUAD, block)
            own = [
                lax.dynamic_index_in_dim(columns, quarter ^ d, 2, keepdims=False).reshape(tokens, line * block)
                for d in range(QUAD)
            ]
        own = [own[0]] + [along_quad(own[d], d) for d in range(1, QUAD)]

        def along_line(start):
            ups, downs = [start], [start]
            for k in range(line - 1):
                ups.append(up(ups[-1], k))
                downs.append(down(downs[-1], k))
            return ups[:0:-1] + downs

        near = along_line(jnp.concatenate([own[0], after(own[1], squares_of_line)], axis=0))
        start = jnp.concatenate([after(own[2], near[line - 2], near[line]), own[3]], axis=0)
        far = along_line(start)
        whole_errors = lax.all_gather(
            after(errors, start), ("row", "col"), axis=0, tiled=True, axis_index_groups=layers
        )
        codes = product(line, n_col, tokens, outputs, inverse, (near, far), whole_errors)
        for_feedback = {}
        for j in (*range(0, line, 2), *range(1, line, 2)):
            code = codes[j]
            if j % 2:
                code = after(code, for_feedback[j - 1])
            for_feedback[j] = permute(code, lambda h, q, c: (slot(h, c, share) ^ j, q, h // share))
        for_weight = [along_quad(code, d) if d else code for d, code in enumerate(codes[line:])]

        def update_feedback(odd, held, *others):
            return feedback_update(
                line,
                share,
                odd,
                after(scale, *others),
                [for_feedback[j] for j in range(odd, line, 2)],
                feedback,
                feedback_moment_one,
                feedback_moment_two,
                held,
            )

        new_feedback = update_feedback(0, [])
        new_weight = weight_update(
            line, after(scale, new_feedback[1]), for_weight, weight, weight_moment_one, weight_moment_two
        )
        new_feedback = update_feedback(1, new_feedback, new_weight[1])
        return (*new_weight, *new_feedback)

    return shards


def solution(mesh):
    forward, backward = P("row", "col"), P(None, "row", "col")
    return jax.shard_map(
        make(mesh.shape["row"], mesh.shape["col"]),
        mesh=mesh,
        in_specs=(P("col", "row"), forward, forward, forward, forward, backward, backward, backward),
        out_specs=(forward,) * 4 + (backward,) * 4,
        check_vma=False,
    )
```

time: 429 us -> 322 us (0.75)
  the two profiles are of different devices: /device:TPU:1 before, /device:TPU:20 now
where the time goes in v2:
time: 322 us; the launch traced here: 321 us
  waiting for transfers between devices  167 us (52%)
  Pallas kernels  73.1 us (23%)
  starting transfers between devices  53.6 us (17%)
  between operations  15.7 us (5%)
  other arithmetic  8.46 us (3%)
    ppermute x22, waiting for transfers between devices, permute(): return lax.ppermute(x, ('row', 'col'), pairs)  155 us
    ppermute x22, starting transfers between devices, permute(): return lax.ppermute(x, ('row', 'col'), pairs)  49.7 us
    pallas_call x1, Pallas kernels, product(): pl.pallas_call(functools.partial(product_kernel, line, n_col, tokens, out...  29.2 us
    pallas_call x2, Pallas kernels, feedback_update(): pl.pallas_call(functools.partial(feedback_kernel, line, odd, len(held)),...  24.1 us
    pallas_call x1, Pallas kernels, weight_update(): pl.pallas_call(functools.partial(weight_kernel, line), grid=(line,), out_...  19.5 us
    ppermute x5, waiting for transfers between devices, shards(): others = lax.ppermute(squares, ('row', 'col'), flipped_pairs(1 << bit))  11.8 us
  transfers between devices with their start and end apart: 28, of which 17 were waited for; matrix products, arithmetic and copies ran while one was open for 1% of the time, Pallas kernels for 10%

profile of v2, /device:TPU:20, one launch (start us, length us, event | category | flops | bytes accessed | tf_op | source)
XLA Modules:
  0.0 320.6 jit_solution(2809239854126871)
XLA Ops:
  7.2 2.3 multiply_reduce_fusion.1
  9.6 2.2 multiply_reduce_fusion
  11.7 0.6 reduce_max.18
  12.3 0.6 reduce_max.19
  12.9 1.4 pad_maximum_fusion
  15.1 3.7 %collective-permute-done = f32[2]{0:T(128)S(1)} collective-permute-done((f32[2]{0:T(128)S(1)}, f32[2]{0:T(128)S(1)}, u32[]{:S(2)}, u32[]{:S(2)}) %collective-permute-start) | collective-permute-done | bytes 40 | tf_op jit(solution)/shard_map/ppermute | solution.py:347
  18.8 1.4 maximum_select_fusion.3
  20.1 1.6 collective-permute-start.1
  21.7 2.0 collective-permute-done.1
  23.8 2.4 collective-permute-start.9
  26.1 3.5 %collective-permute-start.6 = (bf16[512,1024]{1,0:T(8,128)(2,1)S(1)}, bf16[512,1024]{1,0:T(8,128)(2,1)}, u32[]{:S(2)}, u32[]{:S(2)}) collective-permute-start(bf16[512,1024]{1,0:T(8,128)(2,1)S(1)} %constant_dynamic-update-slice_fusion.refs_3_), channel_id=1, source_target_pairs={{0,8},{1,9},{2,10},{3,11},{4,12},{5,13},{6,14},{7,15},{8,16},{9,17... | collective-permute-start | bytes 3145736 | tf_op jit(solution)/shard_map/ppermute | solution.py:305
  29.7 1.6 collective-permute-start.12
  31.2 13.4 %collective-permute-done.12 = bf16[256,1024]{1,0:T(8,128)(2,1)S(1)} collective-permute-done((bf16[256,1024]{1,0:T(8,128)(2,1)S(1)}, bf16[256,1024]{1,0:T(8,128)(2,1)S(1)}, u32[]{:S(2)}, u32[]{:S(2)}) %collective-permute-start.12) | collective-permute-done | bytes 524320 | tf_op jit(solution)/shard_map/ppermute | solution.py:305
  44.6 3.6 %collective-permute-done.9.refs_4_ = bf16[512,1024]{1,0:T(8,128)(2,1)S(1)} collective-permute-done((bf16[512,1024]{1,0:T(8,128)(2,1)S(1)}, bf16[512,1024]{1,0:T(8,128)(2,1)S(1)}, u32[]{:S(2)}, u32[]{:S(2)}) %collective-permute-start.9) | collective-permute-done | bytes 1048608 | tf_op jit(solution)/shard_map/ppermute | solution.py:305
  48.2 2.6 collective-permute-done.6.refs_2_
  51.0 2.6 collective-permute-start.17
  53.6 3.3 %collective-permute-start.14 = (bf16[512,1024]{1,0:T(8,128)(2,1)S(1)}, bf16[512,1024]{1,0:T(8,128)(2,1)S(1)}, u32[]{:S(2)}, u32[]{:S(2)}) collective-permute-start(bf16[512,1024]{1,0:T(8,128)(2,1)S(1)} %constant_dynamic-update-slice_fusion.2.refs_10_), channel_id=1, source_target_pairs={{0,8},{1,9},{2,10},{3,11},{4,12},{5,13},{6,14},{7,15},{8,16},{9,17... | collective-permute-start | bytes 3145736 | tf_op jit(solution)/shard_map/ppermute | solution.py:305
  56.9 3.6 %collective-permute-start.10 = (bf16[512,1024]{1,0:T(8,128)(2,1)S(1)}, bf16[512,1024]{1,0:T(8,128)(2,1)}, u32[]{:S(2)}, u32[]{:S(2)}) collective-permute-start(bf16[512,1024]{1,0:T(8,128)(2,1)S(1)} %collective-permute-done.9.refs_4_), channel_id=1, source_target_pairs={{8,0},{9,1},{10,2},{11,3},{12,4},{13,5},{14,6},{15,7},{16,8},{17,9... | collective-permute-start | bytes 3145736 | tf_op jit(solution)/shard_map/ppermute | solution.py:305
  60.4 1.9 collective-permute-start.7
  62.4 16.3 %collective-permute-done.17.refs_11_ = bf16[512,1024]{1,0:T(8,128)(2,1)S(1)} collective-permute-done((bf16[512,1024]{1,0:T(8,128)(2,1)S(1)}, bf16[512,1024]{1,0:T(8,128)(2,1)S(1)}, u32[]{:S(2)}, u32[]{:S(2)}) %collective-permute-start.17) | collective-permute-done | bytes 1048608 | tf_op jit(solution)/shard_map/ppermute | solution.py:305
  78.6 3.8 %collective-permute-start.18 = (bf16[512,1024]{1,0:T(8,128)(2,1)S(1)}, bf16[512,1024]{1,0:T(8,128)(2,1)}, u32[]{:S(2)}, u32[]{:S(2)}) collective-permute-start(bf16[512,1024]{1,0:T(8,128)(2,1)S(1)} %collective-permute-done.17.refs_11_), channel_id=1, source_target_pairs={{8,0},{9,1},{10,2},{11,3},{12,4},{13,5},{14,6},{15,7},{16,8},{17,9... | collective-permute-start | bytes 3145736 | tf_op jit(solution)/shard_map/ppermute | solution.py:305
  82.5 2.2 collective-permute-start.15
  84.7 14.8 %collective-permute-done.10.refs_5_ = bf16[512,1024]{1,0:T(8,128)(2,1)} collective-permute-done((bf16[512,1024]{1,0:T(8,128)(2,1)S(1)}, bf16[512,1024]{1,0:T(8,128)(2,1)}, u32[]{:S(2)}, u32[]{:S(2)}) %collective-permute-start.10) | collective-permute-done | bytes 1048608 | tf_op jit(solution)/shard_map/ppermute | solution.py:305
  99.6 1.7 collective-permute-start.11
  101.2 2.8 collective-permute-done.7.refs_1_
  104.0 4.4 %collective-permute-start.8 = (bf16[512,1024]{1,0:T(8,128)(2,1)}, bf16[512,1024]{1,0:T(8,128)(2,1)}, u32[]{:S(2)}, u32[]{:S(2)}) collective-permute-start(bf16[512,1024]{1,0:T(8,128)(2,1)} %collective-permute-done.7.refs_1_), channel_id=1, source_target_pairs={{16,24},{17,25},{18,26},{19,27},{20,28},{21,29},{22,30},{23,31}} | collective-permute-start | bytes 3145736 | tf_op jit(solution)/shard_map/ppermute | solution.py:305
  108.4 13.5 %collective-permute-done.18.refs_12_ = bf16[512,1024]{1,0:T(8,128)(2,1)} collective-permute-done((bf16[512,1024]{1,0:T(8,128)(2,1)S(1)}, bf16[512,1024]{1,0:T(8,128)(2,1)}, u32[]{:S(2)}, u32[]{:S(2)}) %collective-permute-start.18) | collective-permute-done | bytes 1048608 | tf_op jit(solution)/shard_map/ppermute | solution.py:305
  121.9 1.6 collective-permute-start.19
  123.5 2.6 collective-permute-done.15.refs_8_
  126.1 4.7 %collective-permute-start.16 = (bf16[512,1024]{1,0:T(8,128)(2,1)}, bf16[512,1024]{1,0:T(8,128)(2,1)}, u32[]{:S(2)}, u32[]{:S(2)}) collective-permute-start(bf16[512,1024]{1,0:T(8,128)(2,1)} %collective-permute-done.15.refs_8_), channel_id=1, source_target_pairs={{16,24},{17,25},{18,26},{19,27},{20,28},{21,29},{22,30},{23,31}} | collective-permute-start | bytes 3145736 | tf_op jit(solution)/shard_map/ppermute | solution.py:305
  130.8 1.5 collective-permute-start.2
  132.3 2.0 collective-permute-done.2
  134.3 1.1 collective-permute-done.3
  136.0 3.0 collective-permute-done.4
  141.0 6.9 %collective-permute-done.8.refs_0_ = bf16[512,1024]{1,0:T(8,128)(2,1)} collective-permute-done((bf16[512,1024]{1,0:T(8,128)(2,1)}, bf16[512,1024]{1,0:T(8,128)(2,1)}, u32[]{:S(2)}, u32[]{:S(2)}) %collective-permute-start.8) | collective-permute-done | bytes 1048608 | tf_op jit(solution)/shard_map/ppermute | solution.py:305
  147.9 22.0 %collective-permute-done.16.refs_7_ = bf16[512,1024]{1,0:T(8,128)(2,1)} collective-permute-done((bf16[512,1024]{1,0:T(8,128)(2,1)}, bf16[512,1024]{1,0:T(8,128)(2,1)}, u32[]{:S(2)}, u32[]{:S(2)}) %collective-permute-start.16) | collective-permute-done | bytes 1048608 | tf_op jit(solution)/shard_map/ppermute | solution.py:305
  169.9 29.2 %product.1 = (bf16[256,2048]{1,0:T(8,128)(2,1)}, bf16[256,2048]{1,0:T(8,128)(2,1)}, bf16[256,2048]{1,0:T(8,128)(2,1)}, bf16[256,2048]{1,0:T(8,128)(2,1)}, bf16[1...) custom-call(f32[1]{0:T(128)} %bitcast.5.inverse_ref, ...), custom_call_target="tpu_custom_call" | custom-call | tf_op jit(solution)/shard_map/product/pallas_call | solution.py:165
  199.1 4.3 %collective-permute-start.20 = (bf16[256,2048]{1,0:T(8,128)(2,1)}, bf16[256,2048]{1,0:T(8,128)(2,1)S(1)}, u32[]{:S(2)}, u32[]{:S(2)}) collective-permute-start(bf16[256,2048]{1,0:T(8,128)(2,1)} %get-tuple-element.46), channel_id=1, source_target_pairs={{0,0},{1,24},{2,2},{3,26},{4,4},{5,28},{6,6},{7,30},{8,8},{9,16},{... | collective-permute-start | bytes 3145736 | tf_op jit(solution)/shard_map/ppermute | solution.py:305
  203.5 1.5 collective-permute-start.23
  205.4 43.0 %collective-permute-done.20.refs_0_ = bf16[256,2048]{1,0:T(8,128)(2,1)S(1)} collective-permute-done((bf16[256,2048]{1,0:T(8,128)(2,1)}, bf16[256,2048]{1,0:T(8,128)(2,1)S(1)}, u32[]{:S(2)}, u32[]{:S(2)}) %collective-permute-start.20) | collective-permute-done | bytes 1048608 | tf_op jit(solution)/shard_map/ppermute | solution.py:305
  248.4 1.0 copy-done.9
  249.4 1.9 collective-permute-start.25
  251.2 4.2 %collective-permute-start.26 = (bf16[256,2048]{1,0:T(8,128)(2,1)}, bf16[256,2048]{1,0:T(8,128)(2,1)}, u32[]{:S(2)}, u32[]{:S(2)}) collective-permute-start(bf16[256,2048]{1,0:T(8,128)(2,1)} %get-tuple-element.62), channel_id=1, source_target_pairs={{0,24},{1,0},{2,26},{3,2},{4,28},{5,4},{6,30},{7,6},{8,16},{9,8},{... | collective-permute-start | bytes 3145736 | tf_op jit(solution)/shard_map/ppermute | solution.py:305
  255.4 12.0 %feedback_update.2 = (f32[2,256,4096]{2,1,0:T(8,128)}, bf16[2,256,4096]{2,1,0:T(8,128)(2,1)}, bf16[2,256,4096]{2,1,0:T(8,128)(2,1)}, bf16[2,256,4096]{2,1,0:T(8,128)(2,1)}) custom-call(s32[1]{0:T(128)} %bitcast.4._, f32[1]{0:T(128)} %bitcast.3.scale_ref, bf16[256,2048]{1,0:T(8,128)(2,1)} %copy-done.9, bf16[256,2048]{1,0:T(8,128)(2,1)} %collective-permute-done.21.refs_1_, ...), custom_call_target="tpu_custom_call" | custom-call | tf_op jit(solution)/shard_map/feedback_update/pallas_call | solution.py:272
  267.5 0.9 copy-done.5
  268.8 19.5 %weight_update.1 = (f32[512,4096]{1,0:T(8,128)}, bf16[512,4096]{1,0:T(8,128)(2,1)}, bf16[512,4096]{1,0:T(8,128)(2,1)}, bf16[512,4096]{1,0:T(8,128)(2,1)}) custom-call(f32[1]{0:T(128)} %bitcast.3.scale_ref, bf16[1024,512]{1,0:T(8,128)(2,1)} %get-tuple-element.50.refs_0_, bf16[1024,512]{1,0:T(8,128)(2,1)} %copy-done.5, bf16[1024,512]{1,0:T(8,128)(2,1)} %copy-done.6, ...), custom_call_target="tpu_custom_call" | custom-call | tf_op jit(solution)/shard_map/weight_update/pallas_call | solution.py:214
  288.3 13.3 %collective-permute-done.26.refs_1_ = bf16[256,2048]{1,0:T(8,128)(2,1)} collective-permute-done((bf16[256,2048]{1,0:T(8,128)(2,1)}, bf16[256,2048]{1,0:T(8,128)(2,1)}, u32[]{:S(2)}, u32[]{:S(2)}) %collective-permute-start.26) | collective-permute-done | bytes 1048608 | tf_op jit(solution)/shard_map/ppermute | solution.py:305
  301.6 12.1 %feedback_update.3 = (f32[2,256,4096]{2,1,0:T(8,128)}, bf16[2,256,4096]{2,1,0:T(8,128)(2,1)}, bf16[2,256,4096]{2,1,0:T(8,128)(2,1)}, bf16[2,256,4096]{2,1,0:T(8,128)(2,1)}) custom-call(s32[1]{0:T(128)} %bitcast.6._, f32[1]{0:T(128)} %bitcast.3.scale_ref, ...), custom_call_target="tpu_custom_call", output_to_operand_aliasing={{0}: (7, {}), {1}: (8, {}), {2}: (9, {}), {3}: (10, {})} | custom-call | tf_op jit(solution)/shard_map/feedback_update/pallas_call | solution.py:272
  (53 shorter events, 2.9 us)
Async XLA Ops:
  7.2 11.6 %copy-start.10 = (pred[2]{0:T(512)(128)(4,1)S(1)}, pred[2]{0:T(512)(128)(4,1)}, u32[]{:S(2)}) copy-start(pred[2]{0:T(512)(128)(4,1)} %constant.61.clone) | copy-start | bytes 10
  7.2 7.5 %copy-start = (bf16[256,4096]{1,0:T(8,128)(2,1)S(1)}, bf16[256,4096]{1,0:T(8,128)(2,1)}, u32[]{:S(2)}) copy-start(bf16[256,4096]{1,0:T(8,128)(2,1)} %x_ref.1) | copy-start | bytes 6291460
  7.2 162.7 %all-gather.2.cloned.1.call-start = ((), (), s32[]{:S(2)}) async-start(), calls=%async_computation | async-start | bytes 18874368 | tf_op jit(solution)/shard_map/all_gather | solution.py:375
  14.3 124.7 %copy-start.11 = (pred[2]{0:T(512)(128)(4,1)S(1)}, pred[2]{0:T(512)(128)(4,1)}, u32[]{:S(2)}) copy-start(pred[2]{0:T(512)(128)(4,1)} %constant.62.clone) | copy-start | bytes 10
  14.3 4.5 %collective-permute-start = (f32[2]{0:T(128)S(1)}, f32[2]{0:T(128)S(1)}, u32[]{:S(2)}, u32[]{:S(2)}) collective-permute-start(f32[2]{0:T(128)S(1)} %pad_maximum_fusion), channel_id=1, source_target_pairs={{0,16},{1,17},{2,18},{3,19},{4,20},{5,21},{6,22},{7,23},{8,24},{9,... | collective-permute-start | bytes 32 | tf_op jit(solution)/shard_map/ppermute | solution.py:347
  15.0 8.7 %collective-permute-start.5 = (bf16[256,1024]{1,0:T(8,128)(2,1)S(1)}, bf16[256,1024]{1,0:T(8,128)(2,1)S(1)}, u32[]{:S(2)}, u32[]{:S(2)}) collective-permute-start(bf16[256,1024]{1,0:T(8,128)(2,1)S(1)} %get-tuple-element.40), channel_id=1, source_target_pairs={{0,2},{1,3},{2,0},{3,1},{4,6},{5,7},{6,4},{7,5},{8,10},{9,11},{10,... | collective-permute-start | bytes 1572872 | tf_op jit(solution)/shard_map/ppermute | solution.py:305
  20.1 3.5 %collective-permute-start.1 = (f32[2]{0:T(128)S(1)}, f32[2]{0:T(128)S(1)}, u32[]{:S(2)}, u32[]{:S(2)}) collective-permute-start(f32[2]{0:T(128)S(1)} %maximum_select_fusion.3), channel_id=1, source_target_pairs={{0,8},{1,9},{2,10},{3,11},{4,12},{5,13},{6,14},{7,15},{8,0},{9,1},... | collective-permute-start | bytes 32 | tf_op jit(solution)/shard_map/ppermute | solution.py:347
  23.7 146.1 %copy-start.1 = (bf16[512,1024]{1,0:T(8,128)(2,1)}, bf16[512,1024]{1,0:T(8,128)(2,1)S(1)}, u32[]{:S(2)}) copy-start(bf16[512,1024]{1,0:T(8,128)(2,1)S(1)} %constant_dynamic-update-slice_fusion.refs_3_) | copy-start | bytes 3145732
  23.8 24.5 %collective-permute-start.9 = (bf16[512,1024]{1,0:T(8,128)(2,1)S(1)}, bf16[512,1024]{1,0:T(8,128)(2,1)S(1)}, u32[]{:S(2)}, u32[]{:S(2)}) collective-permute-start(bf16[512,1024]{1,0:T(8,128)(2,1)S(1)} %constant_dynamic-update-slice_fusion.refs_3_), channel_id=1, source_target_pairs={{8,0},{9,1},{10,2},{11,3},{12,4},{13,5},{14,6},{15,7},{16,8},{17,9... | collective-permute-start | bytes 3145736 | tf_op jit(solution)/shard_map/ppermute | solution.py:305
  26.1 24.7 %collective-permute-start.6 = (bf16[512,1024]{1,0:T(8,128)(2,1)S(1)}, bf16[512,1024]{1,0:T(8,128)(2,1)}, u32[]{:S(2)}, u32[]{:S(2)}) collective-permute-start(bf16[512,1024]{1,0:T(8,128)(2,1)S(1)} %constant_dynamic-update-slice_fusion.refs_3_), channel_id=1, source_target_pairs={{0,8},{1,9},{2,10},{3,11},{4,12},{5,13},{6,14},{7,15},{8,16},{9,17... | collective-permute-start | bytes 3145736 | tf_op jit(solution)/shard_map/ppermute | solution.py:305
  29.7 14.9 %collective-permute-start.12 = (bf16[256,1024]{1,0:T(8,128)(2,1)S(1)}, bf16[256,1024]{1,0:T(8,128)(2,1)S(1)}, u32[]{:S(2)}, u32[]{:S(2)}) collective-permute-start(bf16[256,1024]{1,0:T(8,128)(2,1)S(1)} %get-tuple-element.42), channel_id=1, source_target_pairs={{0,4},{1,5},{2,6},{3,7},{4,0},{5,1},{6,2},{7,3},{8,12},{9,13},{10,... | collective-permute-start | bytes 1572872 | tf_op jit(solution)/shard_map/ppermute | solution.py:305
  31.2 19.6 %collective-permute-start.13 = (bf16[256,1024]{1,0:T(8,128)(2,1)S(1)}, bf16[256,1024]{1,0:T(8,128)(2,1)S(1)}, u32[]{:S(2)}, u32[]{:S(2)}) collective-permute-start(bf16[256,1024]{1,0:T(8,128)(2,1)S(1)} %get-tuple-element.44), channel_id=1, source_target_pairs={{0,6},{1,7},{2,4},{3,5},{4,2},{5,3},{6,0},{7,1},{8,14},{9,15},{10,... | collective-permute-start | bytes 1572872 | tf_op jit(solution)/shard_map/ppermute | solution.py:305
  48.2 121.6 %copy-start.3 = (bf16[512,1024]{1,0:T(8,128)(2,1)}, bf16[512,1024]{1,0:T(8,128)(2,1)S(1)}, u32[]{:S(2)}) copy-start(bf16[512,1024]{1,0:T(8,128)(2,1)S(1)} %collective-permute-done.9.refs_4_) | copy-start | bytes 3145732
  50.9 119.0 %copy-start.2 = (bf16[512,1024]{1,0:T(8,128)(2,1)}, bf16[512,1024]{1,0:T(8,128)(2,1)S(1)}, u32[]{:S(2)}) copy-start(bf16[512,1024]{1,0:T(8,128)(2,1)S(1)} %constant_dynamic-update-slice_fusion.2.refs_10_) | copy-start | bytes 3145732
  51.0 27.7 %collective-permute-start.17 = (bf16[512,1024]{1,0:T(8,128)(2,1)S(1)}, bf16[512,1024]{1,0:T(8,128)(2,1)S(1)}, u32[]{:S(2)}, u32[]{:S(2)}) collective-permute-start(bf16[512,1024]{1,0:T(8,128)(2,1)S(1)} %constant_dynamic-update-slice_fusion.2.refs_10_), channel_id=1, source_target_pairs={{8,0},{9,1},{10,2},{11,3},{12,4},{13,5},{14,6},{15,7},{16,8},{17,9... | collective-permute-start | bytes 3145736 | tf_op jit(solution)/shard_map/ppermute | solution.py:305
  53.6 28.9 %collective-permute-start.14 = (bf16[512,1024]{1,0:T(8,128)(2,1)S(1)}, bf16[512,1024]{1,0:T(8,128)(2,1)S(1)}, u32[]{:S(2)}, u32[]{:S(2)}) collective-permute-start(bf16[512,1024]{1,0:T(8,128)(2,1)S(1)} %constant_dynamic-update-slice_fusion.2.refs_10_), channel_id=1, source_target_pairs={{0,8},{1,9},{2,10},{3,11},{4,12},{5,13},{6,14},{7,15},{8,16},{9,17... | collective-permute-start | bytes 3145736 | tf_op jit(solution)/shard_map/ppermute | solution.py:305
  56.9 42.7 %collective-permute-start.10 = (bf16[512,1024]{1,0:T(8,128)(2,1)S(1)}, bf16[512,1024]{1,0:T(8,128)(2,1)}, u32[]{:S(2)}, u32[]{:S(2)}) collective-permute-start(bf16[512,1024]{1,0:T(8,128)(2,1)S(1)} %collective-permute-done.9.refs_4_), channel_id=1, source_target_pairs={{8,0},{9,1},{10,2},{11,3},{12,4},{13,5},{14,6},{15,7},{16,8},{17,9... | collective-permute-start | bytes 3145736 | tf_op jit(solution)/shard_map/ppermute | solution.py:305
  60.4 43.5 %collective-permute-start.7 = (bf16[512,1024]{1,0:T(8,128)(2,1)}, bf16[512,1024]{1,0:T(8,128)(2,1)}, u32[]{:S(2)}, u32[]{:S(2)}) collective-permute-start(bf16[512,1024]{1,0:T(8,128)(2,1)} %collective-permute-done.6.refs_2_), channel_id=1, source_target_pairs={{8,16},{9,17},{10,18},{11,19},{12,20},{13,21},{14,22},{15,23},{16,... | collective-permute-start | bytes 3145736 | tf_op jit(solution)/shard_map/ppermute | solution.py:305
  78.6 20.9 %copy-start.7 = (bf16[512,1024]{1,0:T(8,128)(2,1)}, bf16[512,1024]{1,0:T(8,128)(2,1)S(1)}, u32[]{:S(2)}) copy-start(bf16[512,1024]{1,0:T(8,128)(2,1)S(1)} %collective-permute-done.17.refs_11_) | copy-start | bytes 3145732
  78.6 43.2 %collective-permute-start.18 = (bf16[512,1024]{1,0:T(8,128)(2,1)S(1)}, bf16[512,1024]{1,0:T(8,128)(2,1)}, u32[]{:S(2)}, u32[]{:S(2)}) collective-permute-start(bf16[512,1024]{1,0:T(8,128)(2,1)S(1)} %collective-permute-done.17.refs_11_), channel_id=1, source_target_pairs={{8,0},{9,1},{10,2},{11,3},{12,4},{13,5},{14,6},{15,7},{16,8},{17,9... | collective-permute-start | bytes 3145736 | tf_op jit(solution)/shard_map/ppermute | solution.py:305
  82.5 39.4 %copy-start.8 = (bf16[512,1024]{1,0:T(8,128)(2,1)}, bf16[512,1024]{1,0:T(8,128)(2,1)S(1)}, u32[]{:S(2)}) copy-start(bf16[512,1024]{1,0:T(8,128)(2,1)S(1)} %collective-permute-done.14.refs_9_) | copy-start | bytes 3145732
  82.5 43.6 %collective-permute-start.15 = (bf16[512,1024]{1,0:T(8,128)(2,1)S(1)}, bf16[512,1024]{1,0:T(8,128)(2,1)}, u32[]{:S(2)}, u32[]{:S(2)}) collective-permute-start(bf16[512,1024]{1,0:T(8,128)(2,1)S(1)} %collective-permute-done.14.refs_9_), channel_id=1, source_target_pairs={{8,16},{9,17},{10,18},{11,19},{12,20},{13,21},{14,22},{15,23},{16,... | collective-permute-start | bytes 3145736 | tf_op jit(solution)/shard_map/ppermute | solution.py:305
  99.6 41.4 %collective-permute-start.11 = (bf16[512,1024]{1,0:T(8,128)(2,1)}, bf16[512,1024]{1,0:T(8,128)(2,1)}, u32[]{:S(2)}, u32[]{:S(2)}) collective-permute-start(bf16[512,1024]{1,0:T(8,128)(2,1)} %collective-permute-done.10.refs_5_), channel_id=1, source_target_pairs={{8,0},{9,1},{10,2},{11,3},{12,4},{13,5},{14,6},{15,7}} | collective-permute-start | bytes 3145736 | tf_op jit(solution)/shard_map/ppermute | solution.py:305
  104.0 43.9 %collective-permute-start.8 = (bf16[512,1024]{1,0:T(8,128)(2,1)}, bf16[512,1024]{1,0:T(8,128)(2,1)}, u32[]{:S(2)}, u32[]{:S(2)}) collective-permute-start(bf16[512,1024]{1,0:T(8,128)(2,1)} %collective-permute-done.7.refs_1_), channel_id=1, source_target_pairs={{16,24},{17,25},{18,26},{19,27},{20,28},{21,29},{22,30},{23,31}} | collective-permute-start | bytes 3145736 | tf_op jit(solution)/shard_map/ppermute | solution.py:305
  121.9 26.0 %collective-permute-start.19 = (bf16[512,1024]{1,0:T(8,128)(2,1)}, bf16[512,1024]{1,0:T(8,128)(2,1)}, u32[]{:S(2)}, u32[]{:S(2)}) collective-permute-start(bf16[512,1024]{1,0:T(8,128)(2,1)} %collective-permute-done.18.refs_12_), channel_id=1, source_target_pairs={{8,0},{9,1},{10,2},{11,3},{12,4},{13,5},{14,6},{15,7}} | collective-permute-start | bytes 3145736 | tf_op jit(solution)/shard_map/ppermute | solution.py:305
  126.1 43.8 %collective-permute-start.16 = (bf16[512,1024]{1,0:T(8,128)(2,1)}, bf16[512,1024]{1,0:T(8,128)(2,1)}, u32[]{:S(2)}, u32[]{:S(2)}) collective-permute-start(bf16[512,1024]{1,0:T(8,128)(2,1)} %collective-permute-done.15.refs_8_), channel_id=1, source_target_pairs={{16,24},{17,25},{18,26},{19,27},{20,28},{21,29},{22,30},{23,31}} | collective-permute-start | bytes 3145736 | tf_op jit(solution)/shard_map/ppermute | solution.py:305
  130.8 3.5 %collective-permute-start.2 = (f32[2]{0:T(128)S(1)}, f32[2]{0:T(128)S(1)}, u32[]{:S(2)}, u32[]{:S(2)}) collective-permute-start(f32[2]{0:T(128)S(1)} %maximum_select_fusion.2), channel_id=1, source_target_pairs={{0,4},{1,5},{2,6},{3,7},{4,0},{5,1},{6,2},{7,3},{8,12},{9,13},{10,... | collective-permute-start | bytes 32 | tf_op jit(solution)/shard_map/ppermute | solution.py:347
  134.3 1.1 collective-permute-start.3
  135.5 3.5 %collective-permute-start.4 = (f32[2]{0:T(128)S(1)}, f32[2]{0:T(128)S(1)}, u32[]{:S(2)}, u32[]{:S(2)}) collective-permute-start(f32[2]{0:T(128)S(1)} %maximum_select_fusion), channel_id=1, source_target_pairs={{0,1},{1,0},{2,3},{3,2},{4,5},{5,4},{6,7},{7,6},{8,9},{9,8},{10,11... | collective-permute-start | bytes 32 | tf_op jit(solution)/shard_map/ppermute | solution.py:347
  199.1 49.3 %collective-permute-start.20 = (bf16[256,2048]{1,0:T(8,128)(2,1)}, bf16[256,2048]{1,0:T(8,128)(2,1)S(1)}, u32[]{:S(2)}, u32[]{:S(2)}) collective-permute-start(bf16[256,2048]{1,0:T(8,128)(2,1)} %get-tuple-element.46), channel_id=1, source_target_pairs={{0,0},{1,24},{2,2},{3,26},{4,4},{5,28},{6,6},{7,30},{8,8},{9,16},{... | collective-permute-start | bytes 3145736 | tf_op jit(solution)/shard_map/ppermute | solution.py:305
  203.4 47.8 %collective-permute-start.21 = (bf16[256,2048]{1,0:T(8,128)(2,1)}, bf16[256,2048]{1,0:T(8,128)(2,1)}, u32[]{:S(2)}, u32[]{:S(2)}) collective-permute-start(bf16[256,2048]{1,0:T(8,128)(2,1)} %get-tuple-element.47), channel_id=1, source_target_pairs={{0,16},{1,8},{2,18},{3,10},{4,20},{5,12},{6,22},{7,14},{8,24},{9,0... | collective-permute-start | bytes 3145736 | tf_op jit(solution)/shard_map/ppermute | solution.py:305
  203.5 64.0 %collective-permute-start.22 = (bf16[1024,512]{1,0:T(8,128)(2,1)}, bf16[1024,512]{1,0:T(8,128)(2,1)S(1)}, u32[]{:S(2)}, u32[]{:S(2)}) collective-permute-start(bf16[1024,512]{1,0:T(8,128)(2,1)} %get-tuple-element.51), channel_id=1, source_target_pairs={{0,2},{1,3},{2,0},{3,1},{4,6},{5,7},{6,4},{7,5},{8,10},{9,11},{10,... | collective-permute-start | bytes 3145736 | tf_op jit(solution)/shard_map/ppermute | solution.py:305
  203.5 63.9 %collective-permute-start.23 = (bf16[1024,512]{1,0:T(8,128)(2,1)}, bf16[1024,512]{1,0:T(8,128)(2,1)S(1)}, u32[]{:S(2)}, u32[]{:S(2)}) collective-permute-start(bf16[1024,512]{1,0:T(8,128)(2,1)} %get-tuple-element.52), channel_id=1, source_target_pairs={{0,4},{1,5},{2,6},{3,7},{4,0},{5,1},{6,2},{7,3},{8,12},{9,13},{10,... | collective-permute-start | bytes 3145736 | tf_op jit(solution)/shard_map/ppermute | solution.py:305
  205.1 62.4 %collective-permute-start.24 = (bf16[1024,512]{1,0:T(8,128)(2,1)}, bf16[1024,512]{1,0:T(8,128)(2,1)}, u32[]{:S(2)}, u32[]{:S(2)}) collective-permute-start(bf16[1024,512]{1,0:T(8,128)(2,1)} %get-tuple-element.53), channel_id=1, source_target_pairs={{0,6},{1,7},{2,4},{3,5},{4,2},{5,3},{6,0},{7,1},{8,14},{9,15},{10,... | collective-permute-start | bytes 3145736 | tf_op jit(solution)/shard_map/ppermute | solution.py:305
  248.4 1.0 copy-start.9
  249.4 38.9 %collective-permute-start.25 = (bf16[256,2048]{1,0:T(8,128)(2,1)}, bf16[256,2048]{1,0:T(8,128)(2,1)S(1)}, u32[]{:S(2)}, u32[]{:S(2)}) collective-permute-start(bf16[256,2048]{1,0:T(8,128)(2,1)} %get-tuple-element.60), channel_id=1, source_target_pairs={{0,8},{1,16},{2,10},{3,18},{4,12},{5,20},{6,14},{7,22},{8,0},{9,24... | collective-permute-start | bytes 3145736 | tf_op jit(solution)/shard_map/ppermute | solution.py:305
  251.2 50.4 %collective-permute-start.26 = (bf16[256,2048]{1,0:T(8,128)(2,1)}, bf16[256,2048]{1,0:T(8,128)(2,1)}, u32[]{:S(2)}, u32[]{:S(2)}) collective-permute-start(bf16[256,2048]{1,0:T(8,128)(2,1)} %get-tuple-element.62), channel_id=1, source_target_pairs={{0,24},{1,0},{2,26},{3,2},{4,28},{5,4},{6,30},{7,6},{8,16},{9,8},{... | collective-permute-start | bytes 3145736 | tf_op jit(solution)/shard_map/ppermute | solution.py:305
  267.4 1.0 copy-start.5
  267.5 1.3 copy-start.6
  288.3 13.3 %copy-start.4 = (bf16[256,2048]{1,0:T(8,128)(2,1)}, bf16[256,2048]{1,0:T(8,128)(2,1)S(1)}, u32[]{:S(2)}) copy-start(bf16[256,2048]{1,0:T(8,128)(2,1)S(1)} %collective-permute-done.25.refs_0_) | copy-start | bytes 3145732
Sparse Core Ops, SparseCore 0:
  51.1 89.8 all-gather.1

commit v3 on v2

--- a/solution.py
+++ b/solution.py
@@ -99,36 +99,75 @@
     )(x)
 
 
-def product_kernel(line, n_col, tokens, outputs, depths, inverse_ref, *refs):
+def longest_kernel(errors_ref, inputs_ref, out_ref):
+    for half, ref in enumerate((errors_ref, inputs_ref)):
+        total = jnp.zeros((1, ref.shape[1]), jnp.float32)
+        step = min(256, ref.shape[0])
+        for start in range(0, ref.shape[0], step):
+            x = ref[pl.ds(start, step), :].astype(jnp.float32) * 2.0**40
+            total = total + jnp.sum(x * x, axis=0, keepdims=True)
+        out_ref[pl.ds(half * 4, 4), :] = jnp.broadcast_to(jnp.max(total, axis=1, keepdims=True), (4, 128))
+
+
+def longest(errors, inputs):
+    return pl.pallas_call(
+        longest_kernel,
+        out_shape=jax.ShapeDtypeStruct((8, 128), jnp.float32),
+        in_specs=[pl.BlockSpec(memory_space=pltpu.VMEM)] * 2,
+        out_specs=pl.BlockSpec(memory_space=pltpu.VMEM),
+        compiler_params=pltpu.CompilerParams(vmem_limit_bytes=32 * 2**20),
+        cost_estimate=BRIEF,
+        name="longest",
+    )(errors, inputs)
+
+
+def product_kernel(line, n_col, tokens, outputs, slab, picks, n_old, inverse_ref, *refs):
     share = line // n_col
-    reach = 2 * line - 1
-    candidates, refs = refs[: len(depths) * reach], refs[len(depths) * reach :]
+    candidates, refs = refs[: 2 * line - 1], refs[2 * line - 1 :]
     errors, refs = refs[0], refs[1:]
-    to_line, to_quad, refs = refs[:line], refs[line : line + QUAD], refs[line + QUAD :]
-    held, turned, whole, code, in_sem, error_sem, out_sem = refs
     layer, quarter, column = my_place()
-    depth = QUAD * tokens
-    width = held.shape[1]
-    rows = width // line
+    depth = len(slab) * tokens
+    block = candidates[0].shape[1] // line
+    if picks:
+        so_far, refs = refs[0], refs[1 + n_old :]
+        to_line, to_quad, refs = refs[: len(picks)], refs[len(picks) : len(picks) + QUAD], refs[len(picks) + QUAD :]
+        held, turned, whole, total, code, in_sem, error_sem, total_sem, out_sem = refs
+    else:
+        result, held, turned, whole, total, in_sem, error_sem, out_sem = refs
+    apart = picks and len(picks) < line
+    layers = [slot(layer, column, share) ^ j for j in picks or ()]
+    spans = [pl.ds(pl.multiple_of(to * block, block), block) for to in layers]
 
     for n in range(line):
         source = (column ^ (n // share)) * share + n % share
-        start = n * depth
-        for g, slab in enumerate(depths):
-            for i, candidate in enumerate(candidates[g * reach : (g + 1) * reach]):
-                copy = pltpu.make_async_copy(candidate, held.at[pl.ds(start, slab)], in_sem.at[n])
-                pl.when(source - layer == i - (line - 1))(copy.start)
-            start += slab
+        for i, candidate in enumerate(candidates):
+
+            @pl.when(source - layer == i - (line - 1))
+            def _():
+                rows = pl.ds(n * depth, depth)
+                if apart:
+                    for m, span in enumerate(spans):
+                        part = held.at[rows, pl.ds(m * block, block)]
+                        pltpu.make_async_copy(candidate.at[:, span], part, in_sem.at[n]).start()
+                else:
+                    pltpu.make_async_copy(candidate, held.at[rows], in_sem.at[n]).start()
+
     for q in range(QUAD):
         for n in range(line):
-            for d in range(QUAD):
+            for m, d in enumerate(slab):
                 start = (column ^ (n // share)) * QUAD + (quarter ^ q)
                 start = ((start * share + n % share) * QUAD + (quarter ^ d)) * tokens
                 pltpu.make_async_copy(
                     errors.at[pl.ds(pl.multiple_of(start, tokens), tokens)],
-                    whole.at[pl.ds(n * depth + d * tokens, tokens), pl.ds(q * outputs, outputs)],
+                    whole.at[pl.ds(n * depth + m * tokens, tokens), pl.ds(q * outputs, outputs)],
                     error_sem.at[q],
                 ).start()
+    if apart:
+        for m, span in enumerate(spans):
+            pltpu.make_async_copy(so_far.at[span], total.at[pl.ds(m * block, block)], total_sem).start()
+    elif picks:
+        pltpu.make_async_copy(so_far, total, total_sem).start()
+
     for n in range(line):
         part = held.at[pl.ds(n * depth, depth)]
         pltpu.make_async_copy(part, part, in_sem.at[n]).wait()
@@ -138,18 +177,24 @@
             at = pl.multiple_of(i * 256, 256)
             turned[:, pl.ds(at, 256)] = held[pl.ds(at, 256), :].T
 
+    if picks:
+        pltpu.make_async_copy(total, total, total_sem).wait()
     copies = []
     for q in range(QUAD):
         lanes = pl.ds(q * outputs, outputs)
         part = whole.at[:, lanes]
         pltpu.make_async_copy(part, part, error_sem.at[q]).wait()
         gradient = jnp.dot(turned[...], part[...], preferred_element_type=jnp.float32)
-        code[:, lanes] = encode(gradient, inverse_ref[0])
-        ready = [(code.at[:, lanes], to_quad[q])]
-        for j in range(line):
-            to = slot(layer, column, share) ^ j
-            at = pl.ds(pl.multiple_of(to * rows, 16), rows)
-            ready.append((code.at[at, lanes], to_line[j].at[:, lanes]))
+        if picks:
+            code[:, lanes] = encode(total[:, lanes] + gradient, inverse_ref[0])
+            ready = []
+            for m, (to, span) in enumerate(zip(layers, spans)):
+                rows = pl.ds(m * block, block) if apart else span
+                ready.append((code.at[rows, lanes], to_line[m].at[:, lanes]))
+                ready.append((code.at[rows, lanes], to_quad[q].at[span]))
+        else:
+            total[:, lanes] = gradient
+            ready = [(total.at[:, lanes], result.at[:, lanes])]
         for source, target in ready:
             copies.append(pltpu.make_async_copy(source, target, out_sem.at[len(copies)]))
             copies[-1].start()
@@ -157,30 +202,40 @@
         copy.wait()
 
 
-def product(line, n_col, tokens, outputs, inverse, groups, errors):
-    width = groups[0][0].shape[1]
-    whole = (line * QUAD * tokens, QUAD * outputs)
-    depths = [group[0].shape[0] for group in groups]
-    candidates = [candidate for group in groups for candidate in group]
+def product(line, n_col, tokens, outputs, slab, picks, inverse, candidates, errors, so_far=(), old=()):
+    columns = candidates[0].shape[1]
+    block = columns // line
+    width = len(picks) * block if picks else columns
+    depth = line * len(slab) * tokens
+    if picks:
+        out_shape = [jax.ShapeDtypeStruct((block, QUAD * outputs), jnp.bfloat16)] * len(picks)
+        out_shape += [jax.ShapeDtypeStruct((columns, outputs), jnp.bfloat16)] * QUAD
+        more = [pltpu.VMEM((width, QUAD * outputs), jnp.bfloat16)]
+    else:
+        out_shape = [jax.ShapeDtypeStruct((columns, QUAD * outputs), jnp.float32)]
+        more = []
+    n_in = 1 + len(candidates) + 1 + len(so_far)
     return pl.pallas_call(
-        functools.partial(product_kernel, line, n_col, tokens, outputs, depths),
-        out_shape=[jax.ShapeDtypeStruct((width // line, QUAD * outputs), jnp.bfloat16)] * line
-        + [jax.ShapeDtypeStruct((width, outputs), jnp.bfloat16)] * QUAD,
-        in_specs=[scalar_spec()] + any_specs(len(candidates) + 1),
-        out_specs=any_specs(line + QUAD),
+        functools.partial(product_kernel, line, n_col, tokens, outputs, slab, picks, len(old)),
+        out_shape=out_shape,
+        in_specs=[scalar_spec()] + any_specs(n_in - 1 + len(old)),
+        out_specs=any_specs(len(out_shape)),
         scratch_shapes=[
-            pltpu.VMEM((line * QUAD * tokens, width), jnp.bfloat16),
-            pltpu.VMEM((width, line * QUAD * tokens), jnp.bfloat16),
-            pltpu.VMEM(whole, jnp.bfloat16),
-            pltpu.VMEM((width, QUAD * outputs), jnp.bfloat16),
+            pltpu.VMEM((depth, width), jnp.bfloat16),
+            pltpu.VMEM((width, depth), jnp.bfloat16),
+            pltpu.VMEM((depth, QUAD * outputs), jnp.bfloat16),
+            pltpu.VMEM((width, QUAD * outputs), jnp.float32),
+            *more,
             pltpu.SemaphoreType.DMA((line,)),
             pltpu.SemaphoreType.DMA((QUAD,)),
-            pltpu.SemaphoreType.DMA(((line + 1) * QUAD,)),
+            *([pltpu.SemaphoreType.DMA] if picks else []),
+            pltpu.SemaphoreType.DMA((2 * line * QUAD,)),
         ],
+        input_output_aliases={n_in + i: len(picks) + i for i in range(len(old))},
         compiler_params=pltpu.CompilerParams(vmem_limit_bytes=56 * 2**20),
-        cost_estimate=BRIEF,
+        cost_estimate=pl.CostEstimate(flops=2 * width * depth * QUAD * outputs, bytes_accessed=0, transcendentals=0),
         name="product",
-    )(inverse, *candidates, errors)
+    )(inverse, *candidates, errors, *so_far, *old)
 
 
 def weight_kernel(line, scale_ref, *refs):
@@ -304,9 +359,6 @@
                     pairs.append((r * n_col + c, (to[0] * QUAD + to[1]) * n_col + to[2]))
         return lax.ppermute(x, ("row", "col"), pairs)
 
-    def flipped_pairs(bit):
-        return [(i, i ^ bit) for i in range(n_row * n_col)]
-
     def along_quad(x, d):
         return permute(x, lambda h, q, c: (h, q ^ d, c))
 
@@ -338,16 +390,25 @@
         block = inputs.shape[1] // n_row
         outputs = errors.shape[1]
 
-        squares = [jnp.max(jnp.sum(jnp.square(x.astype(jnp.float32) * 2.0**40), axis=0)) for x in (errors, inputs)]
-        squares = jnp.stack(squares)
-        squares_of_line = ()
-        for bit in reversed(range((n_row * n_col).bit_length() - 1)):
-            if (1 << bit) < n_col * QUAD and not isinstance(squares_of_line, jax.Array):
-                squares_of_line = squares
-            others = lax.ppermute(squares, ("row", "col"), flipped_pairs(1 << bit))
-            added = jnp.array([(1 << bit) < n_col, (1 << bit) >= n_col])
-            squares = jnp.where(added, squares + others, jnp.maximum(squares, others))
-        lengths = jnp.sqrt(squares) * 2.0**-40
+        squares = longest(errors, inputs)
+        of_errors = lax.broadcasted_iota(jnp.int32, squares.shape, 0) < 4
+
+        def combine(mine, others, same_tokens):
+            for other in others:
+                mine = jnp.where(of_errors == same_tokens, jnp.maximum(mine, other), mine + other)
+            return mine
+
+        squares_of_line = combine(
+            squares,
+            [permute(squares, lambda h, q, c: (h ^ d, q, c)) for d in range(1, line)],
+            True,
+        )
+        squares = squares_of_line
+        for d in (1, 2):
+            squares = combine(squares, [along_quad(squares, d)], True)
+        for bit in range((n_col - 1).bit_length()):
+            squares = combine(squares, [along_col(squares, 1 << bit)], False)
+        lengths = jnp.sqrt(jnp.stack([squares[0, 0], squares[4, 0]])) * 2.0**-40
         bound = lengths[0] * lengths[1] * 1.01
         bound = jnp.where(bound > 0.0, bound, 1.0)
         inverse, scale = (2.0**HEAD / bound)[None], (bound * 2.0**-HEAD)[None]
@@ -375,14 +436,19 @@
         whole_errors = lax.all_gather(
             after(errors, start), ("row", "col"), axis=0, tiled=True, axis_index_groups=layers
         )
-        codes = product(line, n_col, tokens, outputs, inverse, (near, far), whole_errors)
-        for_feedback = {}
-        for j in (*range(0, line, 2), *range(1, line, 2)):
-            code = codes[j]
-            if j % 2:
-                code = after(code, for_feedback[j - 1])
-            for_feedback[j] = permute(code, lambda h, q, c: (slot(h, c, share) ^ j, q, h // share))
-        for_weight = [along_quad(code, d) if d else code for d, code in enumerate(codes[line:])]
+        so_far = product(line, n_col, tokens, outputs, (0, 1), (), inverse, near, whole_errors)
+        even, odd = tuple(range(0, line, 2)), tuple(range(1, line, 2))
+        for_feedback, for_weight = {}, ()
+        for picks in (even, odd) if block % 128 == 0 else (even + odd,):
+            codes = product(
+                line, n_col, tokens, outputs, (2, 3), picks, inverse, far, whole_errors, so_far, for_weight
+            )
+            for j, code in zip(picks, codes):
+                if j % 2:
+                    code = after(code, for_feedback[j - 1])
+                for_feedback[j] = permute(code, lambda h, q, c: (slot(h, c, share) ^ j, q, h // share))
+            for_weight = codes[len(picks) :]
+        for_weight = [along_quad(code, d) if d else code for d, code in enumerate(for_weight)]
 
         def update_feedback(odd, held, *others):
             return feedback_update(

time: 322 us -> 303 us (0.941)
  waiting for transfers between devices: 167 us -> 136 us
  Pallas kernels: 73.1 us -> 86.1 us
  other arithmetic: 8.46 us -> 1.67 us
  local copies, waits for them, and re-layouts: 3.03 us -> 7.01 us
    ppermute x22 -> x28, waiting for transfers between devices: 155 us -> 136 us  [permute(): return lax.ppermute(x, ('row', 'col'), pairs)]
    ppermute x5 -> x0, waiting for transfers between devices: 11.8 us -> none  [shards(): others = lax.ppermute(squares, ('row', 'col'), flipped_pairs(1 << bit))]
    pallas_call x1 -> x3, Pallas kernels: 29.2 us -> 40.1 us  [product(): pl.pallas_call(functools.partial(product_kernel, line, n_col, tokens, out...]
    ppermute x22 -> x28, starting transfers between devices: 49.7 us -> 55.6 us  [permute(): return lax.ppermute(x, ('row', 'col'), pairs)]
    reduce_sum x2 -> x0, other arithmetic: 4.5 us -> none  [shards(): jnp.sum(jnp.square(x.astype(jnp.float32) * 2.0 ** 40), axis=0)]
    ppermute x5 -> x0, starting transfers between devices: 3.94 us -> none  [shards(): others = lax.ppermute(squares, ('row', 'col'), flipped_pairs(1 << bit))]
    unnamed x26 -> x24, local copies, waits for them, and re-layouts: 2.37 us -> 5.83 us
  transfers between devices with their start and end apart: 28 -> 29, of which waited for: 17 -> 17; matrix products, arithmetic and copies ran while one was open for 1% -> 1% of each run, Pallas kernels for 10% -> 20%
where the time goes in v3:
time: 303 us; the launch traced here: 302 us
  waiting for transfers between devices  136 us (45%)
  Pallas kernels  86.1 us (28%)
  starting transfers between devices  55.6 us (18%)
  between operations  15.7 us (5%)
  local copies, waits for them, and re-layouts  7.01 us (2%)
    ppermute x28, waiting for transfers between devices, permute(): return lax.ppermute(x, ('row', 'col'), pairs)  136 us
    ppermute x28, starting transfers between devices, permute(): return lax.ppermute(x, ('row', 'col'), pairs)  55.6 us
    pallas_call x3, Pallas kernels, product(): pl.pallas_call(functools.partial(product_kernel, line, n_col, tokens, out...  40.1 us
    pallas_call x2, Pallas kernels, feedback_update(): pl.pallas_call(functools.partial(feedback_kernel, line, odd, len(held)),...  24.2 us
    pallas_call x1, Pallas kernels, weight_update(): pl.pallas_call(functools.partial(weight_kernel, line), grid=(line,), out_...  19.5 us
  transfers between devices with their start and end apart: 29, of which 17 were waited for; matrix products, arithmetic and copies ran while one was open for 1% of the time, Pallas kernels for 20%

profile of v3, /device:TPU:20, one launch (start us, length us, event | category | flops | bytes accessed | tf_op | source)
XLA Modules:
  0.0 302.2 jit_solution(17856309837732171178)
XLA Ops:
  7.2 1.6 copy-done
  9.2 1.6 copy-done.1
  10.8 1.6 copy-done.2
  12.4 2.0 longest.1
  14.7 2.7 collective-permute-start.2
  17.4 1.3 collective-permute-start
  19.1 2.0 collective-permute-done
  21.2 1.9 collective-permute-start.9
  23.1 4.0 %collective-permute-start.8 = (bf16[512,1024]{1,0:T(8,128)(2,1)S(1)}, bf16[512,1024]{1,0:T(8,128)(2,1)}, u32[]{:S(2)}, u32[]{:S(2)}) collective-permute-start(bf16[512,1024]{1,0:T(8,128)(2,1)S(1)} %constant_dynamic-update-slice_fusion.refs_3_), channel_id=1, source_target_pairs={{0,8},{1,9},{2,10},{3,11},{4,12},{5,13},{6,14},{7,15},{8,16},{9,17... | collective-permute-start | bytes 3145736 | tf_op jit(solution)/shard_map/ppermute | solution.py:360
  27.1 1.6 collective-permute-start.6
  28.7 13.4 %collective-permute-done.6 = bf16[256,1024]{1,0:T(8,128)(2,1)S(1)} collective-permute-done((bf16[256,1024]{1,0:T(8,128)(2,1)S(1)}, bf16[256,1024]{1,0:T(8,128)(2,1)S(1)}, u32[]{:S(2)}, u32[]{:S(2)}) %collective-permute-start.6) | collective-permute-done | bytes 524320 | tf_op jit(solution)/shard_map/ppermute | solution.py:360
  42.0 4.9 %collective-permute-done.9.refs_4_ = bf16[512,1024]{1,0:T(8,128)(2,1)S(1)} collective-permute-done((bf16[512,1024]{1,0:T(8,128)(2,1)S(1)}, bf16[512,1024]{1,0:T(8,128)(2,1)S(1)}, u32[]{:S(2)}, u32[]{:S(2)}) %collective-permute-start.9) | collective-permute-done | bytes 1048608 | tf_op jit(solution)/shard_map/ppermute | solution.py:360
  46.9 1.0 copy-done.7
  47.9 1.6 collective-permute-done.8.refs_2_
  49.6 3.6 %collective-permute-start.14 = (bf16[512,1024]{1,0:T(8,128)(2,1)S(1)}, bf16[512,1024]{1,0:T(8,128)(2,1)S(1)}, u32[]{:S(2)}, u32[]{:S(2)}) collective-permute-start(bf16[512,1024]{1,0:T(8,128)(2,1)S(1)} %constant_dynamic-update-slice_fusion.2.refs_3_), channel_id=1, source_target_pairs={{8,0},{9,1},{10,2},{11,3},{12,4},{13,5},{14,6},{15,7},{16,8},{17,9... | collective-permute-start | bytes 3145736 | tf_op jit(solution)/shard_map/ppermute | solution.py:360
  53.3 2.3 collective-permute-start.11
  55.5 4.6 %collective-permute-start.19 = (bf16[512,1024]{1,0:T(8,128)(2,1)}, bf16[512,1024]{1,0:T(8,128)(2,1)}, u32[]{:S(2)}, u32[]{:S(2)}) collective-permute-start(bf16[512,1024]{1,0:T(8,128)(2,1)} %copy-done.7), channel_id=1, source_target_pairs={{8,0},{9,1},{10,2},{11,3},{12,4},{13,5},{14,6},{15,7},{16,8},{17,9... | collective-permute-start | bytes 3145736 | tf_op jit(solution)/shard_map/ppermute | solution.py:360
  60.1 1.9 collective-permute-start.17
  62.0 15.3 %collective-permute-done.14.refs_4_ = bf16[512,1024]{1,0:T(8,128)(2,1)S(1)} collective-permute-done((bf16[512,1024]{1,0:T(8,128)(2,1)S(1)}, bf16[512,1024]{1,0:T(8,128)(2,1)S(1)}, u32[]{:S(2)}, u32[]{:S(2)}) %collective-permute-start.14) | collective-permute-done | bytes 1048608 | tf_op jit(solution)/shard_map/ppermute | solution.py:360
  77.3 4.8 %collective-permute-start.15 = (bf16[512,1024]{1,0:T(8,128)(2,1)S(1)}, bf16[512,1024]{1,0:T(8,128)(2,1)}, u32[]{:S(2)}, u32[]{:S(2)}) collective-permute-start(bf16[512,1024]{1,0:T(8,128)(2,1)S(1)} %collective-permute-done.14.refs_4_), channel_id=1, source_target_pairs={{8,0},{9,1},{10,2},{11,3},{12,4},{13,5},{14,6},{15,7},{16,8},{17,9... | collective-permute-start | bytes 3145736 | tf_op jit(solution)/shard_map/ppermute | solution.py:360
  82.1 1.9 collective-permute-start.12
  84.1 15.2 %collective-permute-done.19.refs_5_ = bf16[512,1024]{1,0:T(8,128)(2,1)} collective-permute-done((bf16[512,1024]{1,0:T(8,128)(2,1)}, bf16[512,1024]{1,0:T(8,128)(2,1)}, u32[]{:S(2)}, u32[]{:S(2)}) %collective-permute-start.19) | collective-permute-done | bytes 1048608 | tf_op jit(solution)/shard_map/ppermute | solution.py:360
  99.3 1.6 collective-permute-start.20
  101.0 2.7 collective-permute-done.17.refs_1_
  103.7 3.3 %collective-permute-start.18 = (bf16[512,1024]{1,0:T(8,128)(2,1)}, bf16[512,1024]{1,0:T(8,128)(2,1)}, u32[]{:S(2)}, u32[]{:S(2)}) collective-permute-start(bf16[512,1024]{1,0:T(8,128)(2,1)} %collective-permute-done.17.refs_1_), channel_id=1, source_target_pairs={{16,24},{17,25},{18,26},{19,27},{20,28},{21,29},{22,30},{23,31}} | collective-permute-start | bytes 3145736 | tf_op jit(solution)/shard_map/ppermute | solution.py:360
  107.1 1.5 collective-permute-start.4
  108.5 2.2 collective-permute-done.4
  111.3 3.2 %collective-permute-done.5 = f32[8,128]{1,0:T(8,128)S(1)} collective-permute-done((f32[8,128]{1,0:T(8,128)S(1)}, f32[8,128]{1,0:T(8,128)S(1)}, u32[]{:S(2)}, u32[]{:S(2)}) %collective-permute-start.5) | collective-permute-done | bytes 4128 | tf_op jit(solution)/shard_map/ppermute | solution.py:360
  114.5 6.3 %collective-permute-done.15.refs_5_ = bf16[512,1024]{1,0:T(8,128)(2,1)} collective-permute-done((bf16[512,1024]{1,0:T(8,128)(2,1)S(1)}, bf16[512,1024]{1,0:T(8,128)(2,1)}, u32[]{:S(2)}, u32[]{:S(2)}) %collective-permute-start.15) | collective-permute-done | bytes 1048608 | tf_op jit(solution)/shard_map/ppermute | solution.py:360
  120.8 1.6 collective-permute-start.16
  122.4 3.2 %collective-permute-done.12.refs_1_ = bf16[512,1024]{1,0:T(8,128)(2,1)} collective-permute-done((bf16[512,1024]{1,0:T(8,128)(2,1)S(1)}, bf16[512,1024]{1,0:T(8,128)(2,1)}, u32[]{:S(2)}, u32[]{:S(2)}) %collective-permute-start.12) | collective-permute-done | bytes 1048608 | tf_op jit(solution)/shard_map/ppermute | solution.py:360
  125.7 3.8 %collective-permute-start.13 = (bf16[512,1024]{1,0:T(8,128)(2,1)}, bf16[512,1024]{1,0:T(8,128)(2,1)}, u32[]{:S(2)}, u32[]{:S(2)}) collective-permute-start(bf16[512,1024]{1,0:T(8,128)(2,1)} %collective-permute-done.12.refs_1_), channel_id=1, source_target_pairs={{16,24},{17,25},{18,26},{19,27},{20,28},{21,29},{22,30},{23,31}} | collective-permute-start | bytes 3145736 | tf_op jit(solution)/shard_map/ppermute | solution.py:360
  129.9 1.4 fusion
  131.3 0.6 fusion.2
  133.2 13.3 %collective-permute-done.18.refs_0_ = bf16[512,1024]{1,0:T(8,128)(2,1)} collective-permute-done((bf16[512,1024]{1,0:T(8,128)(2,1)}, bf16[512,1024]{1,0:T(8,128)(2,1)}, u32[]{:S(2)}, u32[]{:S(2)}) %collective-permute-start.18) | collective-permute-done | bytes 1048608 | tf_op jit(solution)/shard_map/ppermute | solution.py:360
  146.5 15.6 %product.3.refs_8_ = f32[1024,2048]{1,0:T(8,128)} custom-call(f32[1]{0:T(128)} %bitcast.5.inverse_ref, bf16[512,1024]{1,0:T(8,128)(2,1)} %collective-permute-done.18.refs_0_, bf16[512,1024]{1,0:T(8,128)(2,1)} %collective-permute-done.17.refs_1_, bf16[512,1024]{1,0:T(8,128)(2,1)} %collective-permute-done.8.refs_2_, bf16[512,1024]{1,0:T(8,128)(2,1)} %copy-done.6, ...), custom_call_target="tpu_custom_call" | custom-call | flops 8589934592 | tf_op jit(solution)/shard_map/product/pallas_call | solution.py:218
  162.2 6.4 %collective-permute-done.13.refs_0_ = bf16[512,1024]{1,0:T(8,128)(2,1)} collective-permute-done((bf16[512,1024]{1,0:T(8,128)(2,1)}, bf16[512,1024]{1,0:T(8,128)(2,1)}, u32[]{:S(2)}, u32[]{:S(2)}) %collective-permute-start.13) | collective-permute-done | bytes 1048608 | tf_op jit(solution)/shard_map/ppermute | solution.py:360
  168.5 12.2 %product.4 = (bf16[256,2048]{1,0:T(8,128)(2,1)}, bf16[256,2048]{1,0:T(8,128)(2,1)}, bf16[1024,512]{1,0:T(8,128)(2,1)}, bf16[1024,512]{1,0:T(8,128)(2,1)}, bf16[1...) custom-call(f32[1]{0:T(128)} %bitcast.5.inverse_ref, bf16[512,1024]{1,0:T(8,128)(2,1)} %collective-permute-done.13.refs_0_, ...), custom_call_target="tpu_custom_call" | custom-call | flops 4294967296 | tf_op jit(solution)/shard_map/product/pallas_call | solution.py:218
  180.7 4.4 %collective-permute-start.21 = (bf16[256,2048]{1,0:T(8,128)(2,1)}, bf16[256,2048]{1,0:T(8,128)(2,1)S(1)}, u32[]{:S(2)}, u32[]{:S(2)}) collective-permute-start(bf16[256,2048]{1,0:T(8,128)(2,1)} %get-tuple-element.50), channel_id=1, source_target_pairs={{0,0},{1,24},{2,2},{3,26},{4,4},{5,28},{6,6},{7,30},{8,8},{9,16},{... | collective-permute-start | bytes 3145736 | tf_op jit(solution)/shard_map/ppermute | solution.py:360
  185.4 12.3 %product.5 = (bf16[256,2048]{1,0:T(8,128)(2,1)}, bf16[256,2048]{1,0:T(8,128)(2,1)}, bf16[1024,512]{1,0:T(8,128)(2,1)}, bf16[1024,512]{1,0:T(8,128)(2,1)}, bf16[1...) custom-call(f32[1]{0:T(128)} %bitcast.5.inverse_ref, ...), custom_call_target="tpu_custom_call", output_to_operand_aliasing={{2}: (10, {}), {3}: (11, {}), {4}: (12, {}), {5}: (13, {})} | custom-call | flops 4294967296 | tf_op jit(solution)/shard_map/product/pallas_call | solution.py:218
  197.7 1.6 collective-permute-start.24
  199.6 30.5 %collective-permute-done.21.refs_0_ = bf16[256,2048]{1,0:T(8,128)(2,1)S(1)} collective-permute-done((bf16[256,2048]{1,0:T(8,128)(2,1)}, bf16[256,2048]{1,0:T(8,128)(2,1)S(1)}, u32[]{:S(2)}, u32[]{:S(2)}) %collective-permute-start.21) | collective-permute-done | bytes 1048608 | tf_op jit(solution)/shard_map/ppermute | solution.py:360
  230.1 1.9 collective-permute-start.26
  232.0 3.7 %collective-permute-start.27 = (bf16[256,2048]{1,0:T(8,128)(2,1)}, bf16[256,2048]{1,0:T(8,128)(2,1)}, u32[]{:S(2)}, u32[]{:S(2)}) collective-permute-start(bf16[256,2048]{1,0:T(8,128)(2,1)} %get-tuple-element.70), channel_id=1, source_target_pairs={{0,24},{1,0},{2,26},{3,2},{4,28},{5,4},{6,30},{7,6},{8,16},{9,8},{... | collective-permute-start | bytes 3145736 | tf_op jit(solution)/shard_map/ppermute | solution.py:360
  235.8 12.1 %feedback_update.2 = (f32[2,256,4096]{2,1,0:T(8,128)}, bf16[2,256,4096]{2,1,0:T(8,128)(2,1)}, bf16[2,256,4096]{2,1,0:T(8,128)(2,1)}, bf16[2,256,4096]{2,1,0:T(8,128)(2,1)}) custom-call(s32[1]{0:T(128)} %bitcast.4._, f32[1]{0:T(128)} %bitcast.3.scale_ref, bf16[256,2048]{1,0:T(8,128)(2,1)} %copy-done.8, bf16[256,2048]{1,0:T(8,128)(2,1)} %copy-done.9, ...), custom_call_target="tpu_custom_call" | custom-call | tf_op jit(solution)/shard_map/feedback_update/pallas_call | solution.py:327
  247.9 19.5 %weight_update.1 = (f32[512,4096]{1,0:T(8,128)}, bf16[512,4096]{1,0:T(8,128)(2,1)}, bf16[512,4096]{1,0:T(8,128)(2,1)}, bf16[512,4096]{1,0:T(8,128)(2,1)}) custom-call(f32[1]{0:T(128)} %bitcast.3.scale_ref, bf16[1024,512]{1,0:T(8,128)(2,1)} %get-tuple-element.58.refs_0_, bf16[1024,512]{1,0:T(8,128)(2,1)} %collective-permute-done.23.refs_1_, ...), custom_call_target="tpu_custom_call" | custom-call | tf_op jit(solution)/shard_map/weight_update/pallas_call | solution.py:269
  267.5 15.8 %collective-permute-done.27.refs_1_ = bf16[256,2048]{1,0:T(8,128)(2,1)} collective-permute-done((bf16[256,2048]{1,0:T(8,128)(2,1)}, bf16[256,2048]{1,0:T(8,128)(2,1)}, u32[]{:S(2)}, u32[]{:S(2)}) %collective-permute-start.27) | collective-permute-done | bytes 1048608 | tf_op jit(solution)/shard_map/ppermute | solution.py:360
  283.3 12.1 %feedback_update.3 = (f32[2,256,4096]{2,1,0:T(8,128)}, bf16[2,256,4096]{2,1,0:T(8,128)(2,1)}, bf16[2,256,4096]{2,1,0:T(8,128)(2,1)}, bf16[2,256,4096]{2,1,0:T(8,128)(2,1)}) custom-call(s32[1]{0:T(128)} %bitcast.6._, f32[1]{0:T(128)} %bitcast.3.scale_ref, ...), custom_call_target="tpu_custom_call", output_to_operand_aliasing={{0}: (7, {}), {1}: (8, {}), {2}: (9, {}), {3}: (10, {})} | custom-call | tf_op jit(solution)/shard_map/feedback_update/pallas_call | solution.py:327
  (54 shorter events, 3.2 us)
Async XLA Ops:
  7.2 139.3 %all-gather.2.cloned.1.call-start = ((), (), s32[]{:S(2)}) async-start(), calls=%async_computation | async-start | bytes 18874368 | tf_op jit(solution)/shard_map/all_gather | solution.py:436
  7.2 1.6 copy-start
  9.1 12.0 %collective-permute-start.7 = (bf16[256,1024]{1,0:T(8,128)(2,1)S(1)}, bf16[256,1024]{1,0:T(8,128)(2,1)S(1)}, u32[]{:S(2)}, u32[]{:S(2)}) collective-permute-start(bf16[256,1024]{1,0:T(8,128)(2,1)S(1)} %get-tuple-element.45), channel_id=1, source_target_pairs={{0,2},{1,3},{2,0},{3,1},{4,6},{5,7},{6,4},{7,5},{8,10},{9,11},{10,... | collective-permute-start | bytes 1572872 | tf_op jit(solution)/shard_map/ppermute | solution.py:360
  9.2 1.6 copy-start.1
  10.8 1.6 copy-start.2
  14.4 4.5 %collective-permute-start.1 = (f32[8,128]{1,0:T(8,128)S(1)}, f32[8,128]{1,0:T(8,128)S(1)}, u32[]{:S(2)}, u32[]{:S(2)}) collective-permute-start(f32[8,128]{1,0:T(8,128)S(1)} %longest.1), channel_id=1, source_target_pairs={{0,16},{1,17},{2,18},{3,19},{4,20},{5,21},{6,22},{7,23},{8,24},{9,... | collective-permute-start | bytes 12296 | tf_op jit(solution)/shard_map/ppermute | solution.py:360
  14.7 4.3 %collective-permute-start.2 = (f32[8,128]{1,0:T(8,128)S(1)}, f32[8,128]{1,0:T(8,128)S(1)}, u32[]{:S(2)}, u32[]{:S(2)}) collective-permute-start(f32[8,128]{1,0:T(8,128)S(1)} %longest.1), channel_id=1, source_target_pairs={{0,24},{1,25},{2,26},{3,27},{4,28},{5,29},{6,30},{7,31},{8,16},{9,... | collective-permute-start | bytes 12296 | tf_op jit(solution)/shard_map/ppermute | solution.py:360
  17.4 3.6 %collective-permute-start = (f32[8,128]{1,0:T(8,128)S(1)}, f32[8,128]{1,0:T(8,128)S(1)}, u32[]{:S(2)}, u32[]{:S(2)}) collective-permute-start(f32[8,128]{1,0:T(8,128)S(1)} %longest.1), channel_id=1, source_target_pairs={{0,8},{1,9},{2,10},{3,11},{4,12},{5,13},{6,14},{7,15},{8,0},{9,1},... | collective-permute-start | bytes 12296 | tf_op jit(solution)/shard_map/ppermute | solution.py:360
  21.2 28.4 %copy-start.6 = (bf16[512,1024]{1,0:T(8,128)(2,1)}, bf16[512,1024]{1,0:T(8,128)(2,1)S(1)}, u32[]{:S(2)}) copy-start(bf16[512,1024]{1,0:T(8,128)(2,1)S(1)} %constant_dynamic-update-slice_fusion.refs_3_) | copy-start | bytes 3145732
  21.2 25.7 %collective-permute-start.9 = (bf16[512,1024]{1,0:T(8,128)(2,1)S(1)}, bf16[512,1024]{1,0:T(8,128)(2,1)S(1)}, u32[]{:S(2)}, u32[]{:S(2)}) collective-permute-start(bf16[512,1024]{1,0:T(8,128)(2,1)S(1)} %constant_dynamic-update-slice_fusion.refs_3_), channel_id=1, source_target_pairs={{8,0},{9,1},{10,2},{11,3},{12,4},{13,5},{14,6},{15,7},{16,8},{17,9... | collective-permute-start | bytes 3145736 | tf_op jit(solution)/shard_map/ppermute | solution.py:360
  23.1 26.4 %collective-permute-start.8 = (bf16[512,1024]{1,0:T(8,128)(2,1)S(1)}, bf16[512,1024]{1,0:T(8,128)(2,1)}, u32[]{:S(2)}, u32[]{:S(2)}) collective-permute-start(bf16[512,1024]{1,0:T(8,128)(2,1)S(1)} %constant_dynamic-update-slice_fusion.refs_3_), channel_id=1, source_target_pairs={{0,8},{1,9},{2,10},{3,11},{4,12},{5,13},{6,14},{7,15},{8,16},{9,17... | collective-permute-start | bytes 3145736 | tf_op jit(solution)/shard_map/ppermute | solution.py:360
  27.1 14.9 %collective-permute-start.6 = (bf16[256,1024]{1,0:T(8,128)(2,1)S(1)}, bf16[256,1024]{1,0:T(8,128)(2,1)S(1)}, u32[]{:S(2)}, u32[]{:S(2)}) collective-permute-start(bf16[256,1024]{1,0:T(8,128)(2,1)S(1)} %get-tuple-element.43), channel_id=1, source_target_pairs={{0,4},{1,5},{2,6},{3,7},{4,0},{5,1},{6,2},{7,3},{8,12},{9,13},{10,... | collective-permute-start | bytes 1572872 | tf_op jit(solution)/shard_map/ppermute | solution.py:360
  28.6 20.9 %collective-permute-start.10 = (bf16[256,1024]{1,0:T(8,128)(2,1)S(1)}, bf16[256,1024]{1,0:T(8,128)(2,1)S(1)}, u32[]{:S(2)}, u32[]{:S(2)}) collective-permute-start(bf16[256,1024]{1,0:T(8,128)(2,1)S(1)} %get-tuple-element.48), channel_id=1, source_target_pairs={{0,6},{1,7},{2,4},{3,5},{4,2},{5,3},{6,0},{7,1},{8,14},{9,15},{10,... | collective-permute-start | bytes 1572872 | tf_op jit(solution)/shard_map/ppermute | solution.py:360
  46.9 1.0 copy-start.7
  49.6 112.6 %copy-start.3 = (bf16[512,1024]{1,0:T(8,128)(2,1)}, bf16[512,1024]{1,0:T(8,128)(2,1)S(1)}, u32[]{:S(2)}) copy-start(bf16[512,1024]{1,0:T(8,128)(2,1)S(1)} %constant_dynamic-update-slice_fusion.2.refs_3_) | copy-start | bytes 3145732
  49.6 27.7 %collective-permute-start.14 = (bf16[512,1024]{1,0:T(8,128)(2,1)S(1)}, bf16[512,1024]{1,0:T(8,128)(2,1)S(1)}, u32[]{:S(2)}, u32[]{:S(2)}) collective-permute-start(bf16[512,1024]{1,0:T(8,128)(2,1)S(1)} %constant_dynamic-update-slice_fusion.2.refs_3_), channel_id=1, source_target_pairs={{8,0},{9,1},{10,2},{11,3},{12,4},{13,5},{14,6},{15,7},{16,8},{17,9... | collective-permute-start | bytes 3145736 | tf_op jit(solution)/shard_map/ppermute | solution.py:360
  53.3 28.9 %collective-permute-start.11 = (bf16[512,1024]{1,0:T(8,128)(2,1)S(1)}, bf16[512,1024]{1,0:T(8,128)(2,1)S(1)}, u32[]{:S(2)}, u32[]{:S(2)}) collective-permute-start(bf16[512,1024]{1,0:T(8,128)(2,1)S(1)} %constant_dynamic-update-slice_fusion.2.refs_3_), channel_id=1, source_target_pairs={{0,8},{1,9},{2,10},{3,11},{4,12},{5,13},{6,14},{7,15},{8,16},{9,17... | collective-permute-start | bytes 3145736 | tf_op jit(solution)/shard_map/ppermute | solution.py:360
  55.5 43.8 %collective-permute-start.19 = (bf16[512,1024]{1,0:T(8,128)(2,1)}, bf16[512,1024]{1,0:T(8,128)(2,1)}, u32[]{:S(2)}, u32[]{:S(2)}) collective-permute-start(bf16[512,1024]{1,0:T(8,128)(2,1)} %copy-done.7), channel_id=1, source_target_pairs={{8,0},{9,1},{10,2},{11,3},{12,4},{13,5},{14,6},{15,7},{16,8},{17,9... | collective-permute-start | bytes 3145736 | tf_op jit(solution)/shard_map/ppermute | solution.py:360
  60.1 43.6 %collective-permute-start.17 = (bf16[512,1024]{1,0:T(8,128)(2,1)}, bf16[512,1024]{1,0:T(8,128)(2,1)}, u32[]{:S(2)}, u32[]{:S(2)}) collective-permute-start(bf16[512,1024]{1,0:T(8,128)(2,1)} %collective-permute-done.8.refs_2_), channel_id=1, source_target_pairs={{8,16},{9,17},{10,18},{11,19},{12,20},{13,21},{14,22},{15,23},{16,... | collective-permute-start | bytes 3145736 | tf_op jit(solution)/shard_map/ppermute | solution.py:360
  77.3 84.8 %copy-start.4 = (bf16[512,1024]{1,0:T(8,128)(2,1)}, bf16[512,1024]{1,0:T(8,128)(2,1)S(1)}, u32[]{:S(2)}) copy-start(bf16[512,1024]{1,0:T(8,128)(2,1)S(1)} %collective-permute-done.14.refs_4_) | copy-start | bytes 3145732
  77.3 43.5 %collective-permute-start.15 = (bf16[512,1024]{1,0:T(8,128)(2,1)S(1)}, bf16[512,1024]{1,0:T(8,128)(2,1)}, u32[]{:S(2)}, u32[]{:S(2)}) collective-permute-start(bf16[512,1024]{1,0:T(8,128)(2,1)S(1)} %collective-permute-done.14.refs_4_), channel_id=1, source_target_pairs={{8,0},{9,1},{10,2},{11,3},{12,4},{13,5},{14,6},{15,7},{16,8},{17,9... | collective-permute-start | bytes 3145736 | tf_op jit(solution)/shard_map/ppermute | solution.py:360
  82.1 80.0 %copy-start.5 = (bf16[512,1024]{1,0:T(8,128)(2,1)}, bf16[512,1024]{1,0:T(8,128)(2,1)S(1)}, u32[]{:S(2)}) copy-start(bf16[512,1024]{1,0:T(8,128)(2,1)S(1)} %collective-permute-done.11.refs_2_) | copy-start | bytes 3145732
  82.1 43.5 %collective-permute-start.12 = (bf16[512,1024]{1,0:T(8,128)(2,1)S(1)}, bf16[512,1024]{1,0:T(8,128)(2,1)}, u32[]{:S(2)}, u32[]{:S(2)}) collective-permute-start(bf16[512,1024]{1,0:T(8,128)(2,1)S(1)} %collective-permute-done.11.refs_2_), channel_id=1, source_target_pairs={{8,16},{9,17},{10,18},{11,19},{12,20},{13,21},{14,22},{15,23},{16,... | collective-permute-start | bytes 3145736 | tf_op jit(solution)/shard_map/ppermute | solution.py:360
  84.0 22.9 %collective-permute-start.3 = (f32[8,128]{1,0:T(8,128)S(1)}, f32[8,128]{1,0:T(8,128)S(1)}, u32[]{:S(2)}, u32[]{:S(2)}) collective-permute-start(f32[8,128]{1,0:T(8,128)S(1)} %add_select_fusion.3), channel_id=1, source_target_pairs={{0,2},{1,3},{2,0},{3,1},{4,6},{5,7},{6,4},{7,5},{8,10},{9,11},{10,... | collective-permute-start | bytes 12296 | tf_op jit(solution)/shard_map/ppermute | solution.py:360
  99.3 33.9 %collective-permute-start.20 = (bf16[512,1024]{1,0:T(8,128)(2,1)}, bf16[512,1024]{1,0:T(8,128)(2,1)}, u32[]{:S(2)}, u32[]{:S(2)}) collective-permute-start(bf16[512,1024]{1,0:T(8,128)(2,1)} %collective-permute-done.19.refs_5_), channel_id=1, source_target_pairs={{8,0},{9,1},{10,2},{11,3},{12,4},{13,5},{14,6},{15,7}} | collective-permute-start | bytes 3145736 | tf_op jit(solution)/shard_map/ppermute | solution.py:360
  103.7 42.8 %collective-permute-start.18 = (bf16[512,1024]{1,0:T(8,128)(2,1)}, bf16[512,1024]{1,0:T(8,128)(2,1)}, u32[]{:S(2)}, u32[]{:S(2)}) collective-permute-start(bf16[512,1024]{1,0:T(8,128)(2,1)} %collective-permute-done.17.refs_1_), channel_id=1, source_target_pairs={{16,24},{17,25},{18,26},{19,27},{20,28},{21,29},{22,30},{23,31}} | collective-permute-start | bytes 3145736 | tf_op jit(solution)/shard_map/ppermute | solution.py:360
  107.1 3.7 %collective-permute-start.4 = (f32[8,128]{1,0:T(8,128)S(1)}, f32[8,128]{1,0:T(8,128)S(1)}, u32[]{:S(2)}, u32[]{:S(2)}) collective-permute-start(f32[8,128]{1,0:T(8,128)S(1)} %add_select_fusion.2), channel_id=1, source_target_pairs={{0,4},{1,5},{2,6},{3,7},{4,0},{5,1},{6,2},{7,3},{8,12},{9,13},{10,... | collective-permute-start | bytes 12296 | tf_op jit(solution)/shard_map/ppermute | solution.py:360
  110.8 3.7 %collective-permute-start.5 = (f32[8,128]{1,0:T(8,128)S(1)}, f32[8,128]{1,0:T(8,128)S(1)}, u32[]{:S(2)}, u32[]{:S(2)}) collective-permute-start(f32[8,128]{1,0:T(8,128)S(1)} %add_select_fusion.1), channel_id=1, source_target_pairs={{0,1},{1,0},{2,3},{3,2},{4,5},{5,4},{6,7},{7,6},{8,9},{9,8},{10,11... | collective-permute-start | bytes 12296 | tf_op jit(solution)/shard_map/ppermute | solution.py:360
  120.8 41.4 %collective-permute-start.16 = (bf16[512,1024]{1,0:T(8,128)(2,1)}, bf16[512,1024]{1,0:T(8,128)(2,1)}, u32[]{:S(2)}, u32[]{:S(2)}) collective-permute-start(bf16[512,1024]{1,0:T(8,128)(2,1)} %collective-permute-done.15.refs_5_), channel_id=1, source_target_pairs={{8,0},{9,1},{10,2},{11,3},{12,4},{13,5},{14,6},{15,7}} | collective-permute-start | bytes 3145736 | tf_op jit(solution)/shard_map/ppermute | solution.py:360
  125.7 42.9 %collective-permute-start.13 = (bf16[512,1024]{1,0:T(8,128)(2,1)}, bf16[512,1024]{1,0:T(8,128)(2,1)}, u32[]{:S(2)}, u32[]{:S(2)}) collective-permute-start(bf16[512,1024]{1,0:T(8,128)(2,1)} %collective-permute-done.12.refs_1_), channel_id=1, source_target_pairs={{16,24},{17,25},{18,26},{19,27},{20,28},{21,29},{22,30},{23,31}} | collective-permute-start | bytes 3145736 | tf_op jit(solution)/shard_map/ppermute | solution.py:360
  180.7 49.4 %collective-permute-start.21 = (bf16[256,2048]{1,0:T(8,128)(2,1)}, bf16[256,2048]{1,0:T(8,128)(2,1)S(1)}, u32[]{:S(2)}, u32[]{:S(2)}) collective-permute-start(bf16[256,2048]{1,0:T(8,128)(2,1)} %get-tuple-element.50), channel_id=1, source_target_pairs={{0,0},{1,24},{2,2},{3,26},{4,4},{5,28},{6,6},{7,30},{8,8},{9,16},{... | collective-permute-start | bytes 3145736 | tf_op jit(solution)/shard_map/ppermute | solution.py:360
  185.1 46.9 %collective-permute-start.22 = (bf16[256,2048]{1,0:T(8,128)(2,1)}, bf16[256,2048]{1,0:T(8,128)(2,1)S(1)}, u32[]{:S(2)}, u32[]{:S(2)}) collective-permute-start(bf16[256,2048]{1,0:T(8,128)(2,1)} %get-tuple-element.51), channel_id=1, source_target_pairs={{0,16},{1,8},{2,18},{3,10},{4,20},{5,12},{6,22},{7,14},{8,24},{9,0... | collective-permute-start | bytes 3145736 | tf_op jit(solution)/shard_map/ppermute | solution.py:360
  197.7 50.2 %collective-permute-start.23 = (bf16[1024,512]{1,0:T(8,128)(2,1)}, bf16[1024,512]{1,0:T(8,128)(2,1)}, u32[]{:S(2)}, u32[]{:S(2)}) collective-permute-start(bf16[1024,512]{1,0:T(8,128)(2,1)} %get-tuple-element.59), channel_id=1, source_target_pairs={{0,2},{1,3},{2,0},{3,1},{4,6},{5,7},{6,4},{7,5},{8,10},{9,11},{10,... | collective-permute-start | bytes 3145736 | tf_op jit(solution)/shard_map/ppermute | solution.py:360
  197.7 50.1 %collective-permute-start.24 = (bf16[1024,512]{1,0:T(8,128)(2,1)}, bf16[1024,512]{1,0:T(8,128)(2,1)}, u32[]{:S(2)}, u32[]{:S(2)}) collective-permute-start(bf16[1024,512]{1,0:T(8,128)(2,1)} %get-tuple-element.60), channel_id=1, source_target_pairs={{0,4},{1,5},{2,6},{3,7},{4,0},{5,1},{6,2},{7,3},{8,12},{9,13},{10,... | collective-permute-start | bytes 3145736 | tf_op jit(solution)/shard_map/ppermute | solution.py:360
  199.3 48.6 %collective-permute-start.25 = (bf16[1024,512]{1,0:T(8,128)(2,1)}, bf16[1024,512]{1,0:T(8,128)(2,1)}, u32[]{:S(2)}, u32[]{:S(2)}) collective-permute-start(bf16[1024,512]{1,0:T(8,128)(2,1)} %get-tuple-element.61), channel_id=1, source_target_pairs={{0,6},{1,7},{2,4},{3,5},{4,2},{5,3},{6,0},{7,1},{8,14},{9,15},{10,... | collective-permute-start | bytes 3145736 | tf_op jit(solution)/shard_map/ppermute | solution.py:360
  230.1 5.6 %copy-start.8 = (bf16[256,2048]{1,0:T(8,128)(2,1)}, bf16[256,2048]{1,0:T(8,128)(2,1)S(1)}, u32[]{:S(2)}) copy-start(bf16[256,2048]{1,0:T(8,128)(2,1)S(1)} %collective-permute-done.21.refs_0_) | copy-start | bytes 3145732
  230.1 37.3 %collective-permute-start.26 = (bf16[256,2048]{1,0:T(8,128)(2,1)}, bf16[256,2048]{1,0:T(8,128)(2,1)S(1)}, u32[]{:S(2)}, u32[]{:S(2)}) collective-permute-start(bf16[256,2048]{1,0:T(8,128)(2,1)} %get-tuple-element.68), channel_id=1, source_target_pairs={{0,8},{1,16},{2,10},{3,18},{4,12},{5,20},{6,14},{7,22},{8,0},{9,24... | collective-permute-start | bytes 3145736 | tf_op jit(solution)/shard_map/ppermute | solution.py:360
  232.0 3.7 %copy-start.9 = (bf16[256,2048]{1,0:T(8,128)(2,1)}, bf16[256,2048]{1,0:T(8,128)(2,1)S(1)}, u32[]{:S(2)}) copy-start(bf16[256,2048]{1,0:T(8,128)(2,1)S(1)} %collective-permute-done.22.refs_1_) | copy-start | bytes 3145732
  232.0 51.3 %collective-permute-start.27 = (bf16[256,2048]{1,0:T(8,128)(2,1)}, bf16[256,2048]{1,0:T(8,128)(2,1)}, u32[]{:S(2)}, u32[]{:S(2)}) collective-permute-start(bf16[256,2048]{1,0:T(8,128)(2,1)} %get-tuple-element.70), channel_id=1, source_target_pairs={{0,24},{1,0},{2,26},{3,2},{4,28},{5,4},{6,30},{7,6},{8,16},{9,8},{... | collective-permute-start | bytes 3145736 | tf_op jit(solution)/shard_map/ppermute | solution.py:360
  267.4 15.8 %copy-start.10 = (bf16[256,2048]{1,0:T(8,128)(2,1)}, bf16[256,2048]{1,0:T(8,128)(2,1)S(1)}, u32[]{:S(2)}) copy-start(bf16[256,2048]{1,0:T(8,128)(2,1)S(1)} %collective-permute-done.26.refs_0_) | copy-start | bytes 3145732
Sparse Core Ops, SparseCore 0:
  49.7 90.0 all-gather.1

commit v4 on v3

--- a/solution.py
+++ b/solution.py
@@ -121,8 +121,10 @@
     )(errors, inputs)
 
 
-def product_kernel(line, n_col, tokens, outputs, slab, picks, n_old, inverse_ref, *refs):
+def product_kernel(line, n_col, tokens, outputs, slab, picks, n_old, *refs):
     share = line // n_col
+    if picks:
+        inverse_ref, refs = refs[0], refs[1:]
     candidates, refs = refs[: 2 * line - 1], refs[2 * line - 1 :]
     errors, refs = refs[0], refs[1:]
     layer, quarter, column = my_place()
@@ -214,11 +216,12 @@
     else:
         out_shape = [jax.ShapeDtypeStruct((columns, QUAD * outputs), jnp.float32)]
         more = []
-    n_in = 1 + len(candidates) + 1 + len(so_far)
+    scalars = [inverse] if picks else []
+    n_in = len(scalars) + len(candidates) + 1 + len(so_far)
     return pl.pallas_call(
         functools.partial(product_kernel, line, n_col, tokens, outputs, slab, picks, len(old)),
         out_shape=out_shape,
-        in_specs=[scalar_spec()] + any_specs(n_in - 1 + len(old)),
+        in_specs=[scalar_spec()] * len(scalars) + any_specs(n_in - len(scalars) + len(old)),
         out_specs=any_specs(len(out_shape)),
         scratch_shapes=[
             pltpu.VMEM((depth, width), jnp.bfloat16),
@@ -235,7 +238,7 @@
         compiler_params=pltpu.CompilerParams(vmem_limit_bytes=56 * 2**20),
         cost_estimate=pl.CostEstimate(flops=2 * width * depth * QUAD * outputs, bytes_accessed=0, transcendentals=0),
         name="product",
-    )(inverse, *candidates, errors, *so_far, *old)
+    )(*scalars, *candidates, errors, *so_far, *old)
 
 
 def weight_kernel(line, scale_ref, *refs):
@@ -316,7 +319,7 @@
 
 def feedback_update(line, share, odd, scale, pieces, master, one, two, held):
     block, width = master.shape[1], master.shape[2] // share
-    rows = 64 if block % 64 == 0 else block
+    rows = 128 if block % 128 == 0 else block
 
     def place(i, t, first):
         group, s = unslot(2 * i + first[0], share)
@@ -390,29 +393,6 @@
         block = inputs.shape[1] // n_row
         outputs = errors.shape[1]
 
-        squares = longest(errors, inputs)
-        of_errors = lax.broadcasted_iota(jnp.int32, squares.shape, 0) < 4
-
-        def combine(mine, others, same_tokens):
-            for other in others:
-                mine = jnp.where(of_errors == same_tokens, jnp.maximum(mine, other), mine + other)
-            return mine
-
-        squares_of_line = combine(
-            squares,
-            [permute(squares, lambda h, q, c: (h ^ d, q, c)) for d in range(1, line)],
-            True,
-        )
-        squares = squares_of_line
-        for d in (1, 2):
-            squares = combine(squares, [along_quad(squares, d)], True)
-        for bit in range((n_col - 1).bit_length()):
-            squares = combine(squares, [along_col(squares, 1 << bit)], False)
-        lengths = jnp.sqrt(jnp.stack([squares[0, 0], squares[4, 0]])) * 2.0**-40
-        bound = lengths[0] * lengths[1] * 1.01
-        bound = jnp.where(bound > 0.0, bound, 1.0)
-        inverse, scale = (2.0**HEAD / bound)[None], (bound * 2.0**-HEAD)[None]
-
         if block % 128 == 0:
             own = pack(line, inputs)
         else:
@@ -430,13 +410,33 @@
                 downs.append(down(downs[-1], k))
             return ups[:0:-1] + downs
 
-        near = along_line(jnp.concatenate([own[0], after(own[1], squares_of_line)], axis=0))
-        start = jnp.concatenate([after(own[2], near[line - 2], near[line]), own[3]], axis=0)
+        near = along_line(jnp.concatenate(own[:2], axis=0))
+
+        squares = after(longest(errors, inputs), near[line - 2], near[line])
+        of_errors = lax.broadcasted_iota(jnp.int32, squares.shape, 0) < 4
+
+        def combine(mine, others, same_tokens):
+            for other in others:
+                mine = jnp.where(of_errors == same_tokens, jnp.maximum(mine, other), mine + other)
+            return mine
+
+        for bit in range((n_col - 1).bit_length()):
+            squares = combine(squares, [along_col(squares, 1 << bit)], False)
+        start = jnp.concatenate([after(own[2], squares), own[3]], axis=0)
         far = along_line(start)
+        for d in (1, 2):
+            squares = combine(squares, [along_quad(squares, d)], True)
+        squares = after(squares, near[0], near[-1])
+        others = [permute(squares, lambda h, q, c: (h ^ d, q, c)) for d in range(1, line)]
+        squares = combine(squares, others, True)
+        lengths = jnp.sqrt(jnp.stack([squares[0, 0], squares[4, 0]])) * 2.0**-40
+        bound = lengths[0] * lengths[1] * 1.01
+        bound = jnp.where(bound > 0.0, bound, 1.0)
+        inverse, scale = (2.0**HEAD / bound)[None], (bound * 2.0**-HEAD)[None]
         whole_errors = lax.all_gather(
             after(errors, start), ("row", "col"), axis=0, tiled=True, axis_index_groups=layers
         )
-        so_far = product(line, n_col, tokens, outputs, (0, 1), (), inverse, near, whole_errors)
+        so_far = product(line, n_col, tokens, outputs, (0, 1), (), None, near, whole_errors)
         even, odd = tuple(range(0, line, 2)), tuple(range(1, line, 2))
         for_feedback, for_weight = {}, ()
         for picks in (even, odd) if block % 128 == 0 else (even + odd,):

time: 303 us -> 291 us (0.960)
  waiting for transfers between devices: 136 us -> 125 us
  starting transfers between devices: 55.6 us -> 60.7 us
  local copies, waits for them, and re-layouts: 7.01 us -> 2.9 us
    ppermute x28, waiting for transfers between devices: 136 us -> 125 us  [permute(): return lax.ppermute(x, ('row', 'col'), pairs)]
    ppermute x28, starting transfers between devices: 55.6 us -> 60.6 us  [permute(): return lax.ppermute(x, ('row', 'col'), pairs)]
    unnamed x24 -> x30, local copies, waits for them, and re-layouts: 5.83 us -> 1.71 us
  transfers between devices with their start and end apart: 29 -> 29, of which waited for: 17 -> 14; matrix products, arithmetic and copies ran while one was open for 1% -> 1% of each run, Pallas kernels for 20% -> 21%
where the time goes in v4:
time: 291 us; the launch traced here: 290 us
  waiting for transfers between devices  125 us (43%)
  Pallas kernels  84.7 us (29%)
  starting transfers between devices  60.7 us (21%)
  between operations  15.7 us (5%)
    ppermute x28, waiting for transfers between devices, permute(): return lax.ppermute(x, ('row', 'col'), pairs)  125 us
    ppermute x28, starting transfers between devices, permute(): return lax.ppermute(x, ('row', 'col'), pairs)  60.6 us
    pallas_call x3, Pallas kernels, product(): pl.pallas_call(functools.partial(product_kernel, line, n_col, tokens, out...  40.2 us
    pallas_call x2, Pallas kernels, feedback_update(): pl.pallas_call(functools.partial(feedback_kernel, line, odd, len(held)),...  22.7 us
    pallas_call x1, Pallas kernels, weight_update(): pl.pallas_call(functools.partial(weight_kernel, line), grid=(line,), out_...  19.5 us
  transfers between devices with their start and end apart: 29, of which 14 were waited for; matrix products, arithmetic and copies ran while one was open for 1% of the time, Pallas kernels for 21%

profile of v4, /device:TPU:20, one launch (start us, length us, event | category | flops | bytes accessed | tf_op | source)
XLA Modules:
  0.0 290.2 jit_solution(2946803311145705828)
XLA Ops:
  7.2 1.6 copy-done
  9.2 1.9 collective-permute-done
  11.1 2.4 collective-permute-start.2
  13.5 4.5 %collective-permute-start.1 = (bf16[512,1024]{1,0:T(8,128)(2,1)S(1)}, bf16[512,1024]{1,0:T(8,128)(2,1)}, u32[]{:S(2)}, u32[]{:S(2)}) collective-permute-start(bf16[512,1024]{1,0:T(8,128)(2,1)S(1)} %constant_dynamic-update-slice_fusion.refs_3_), channel_id=1, source_target_pairs={{0,8},{1,9},{2,10},{3,11},{4,12},{5,13},{6,14},{7,15},{8,16},{9,17... | collective-permute-start | bytes 3145736 | tf_op jit(solution)/shard_map/ppermute | solution.py:363
  18.0 1.6 collective-permute-start.13
  19.5 2.0 longest.1
  21.5 16.8 %collective-permute-done.2.refs_4_ = bf16[512,1024]{1,0:T(8,128)(2,1)} collective-permute-done((bf16[512,1024]{1,0:T(8,128)(2,1)S(1)}, bf16[512,1024]{1,0:T(8,128)(2,1)}, u32[]{:S(2)}, u32[]{:S(2)}) %collective-permute-start.2) | collective-permute-done | bytes 1048608 | tf_op jit(solution)/shard_map/ppermute | solution.py:363
  38.3 2.1 collective-permute-done.1.refs_2_
  40.4 0.5 collective-permute-start.3
  40.9 3.1 %collective-permute-done.3 = f32[8,128]{1,0:T(8,128)S(1)} collective-permute-done((f32[8,128]{1,0:T(8,128)S(1)}, f32[8,128]{1,0:T(8,128)S(1)}, u32[]{:S(2)}, u32[]{:S(2)}) %collective-permute-start.3) | collective-permute-done | bytes 4128 | tf_op jit(solution)/shard_map/ppermute | solution.py:363
  44.2 2.4 collective-permute-start.8
  46.7 2.8 collective-permute-start.6
  49.4 3.1 %collective-permute-start.18 = (bf16[512,1024]{1,0:T(8,128)(2,1)S(1)}, bf16[512,1024]{1,0:T(8,128)(2,1)S(1)}, u32[]{:S(2)}, u32[]{:S(2)}) collective-permute-start(bf16[512,1024]{1,0:T(8,128)(2,1)S(1)} %constant_dynamic-update-slice_fusion.2.refs_4_), channel_id=1, source_target_pairs={{8,0},{9,1},{10,2},{11,3},{12,4},{13,5},{14,6},{15,7},{16,8},{17,9... | collective-permute-start | bytes 3145736 | tf_op jit(solution)/shard_map/ppermute | solution.py:363
  52.6 2.8 collective-permute-start.15
  55.4 15.2 %collective-permute-done.8.refs_5_ = bf16[512,1024]{1,0:T(8,128)(2,1)S(1)} collective-permute-done((bf16[512,1024]{1,0:T(8,128)(2,1)}, bf16[512,1024]{1,0:T(8,128)(2,1)S(1)}, u32[]{:S(2)}, u32[]{:S(2)}) %collective-permute-start.8) | collective-permute-done | bytes 1048608 | tf_op jit(solution)/shard_map/ppermute | solution.py:363
  70.5 0.7 collective-permute-start.9
  71.2 3.6 %collective-permute-done.6.refs_1_ = bf16[512,1024]{1,0:T(8,128)(2,1)S(1)} collective-permute-done((bf16[512,1024]{1,0:T(8,128)(2,1)}, bf16[512,1024]{1,0:T(8,128)(2,1)S(1)}, u32[]{:S(2)}, u32[]{:S(2)}) %collective-permute-start.6) | collective-permute-done | bytes 1048608 | tf_op jit(solution)/shard_map/ppermute | solution.py:363
  74.9 2.8 collective-permute-start.7
  77.7 12.0 %collective-permute-done.18.refs_5_ = bf16[512,1024]{1,0:T(8,128)(2,1)S(1)} collective-permute-done((bf16[512,1024]{1,0:T(8,128)(2,1)S(1)}, bf16[512,1024]{1,0:T(8,128)(2,1)S(1)}, u32[]{:S(2)}, u32[]{:S(2)}) %collective-permute-start.18) | collective-permute-done | bytes 1048608 | tf_op jit(solution)/shard_map/ppermute | solution.py:363
  89.7 6.1 %collective-permute-start.19 = (bf16[512,1024]{1,0:T(8,128)(2,1)S(1)}, bf16[512,1024]{1,0:T(8,128)(2,1)}, u32[]{:S(2)}, u32[]{:S(2)}) collective-permute-start(bf16[512,1024]{1,0:T(8,128)(2,1)S(1)} %collective-permute-done.18.refs_5_), channel_id=1, source_target_pairs={{8,0},{9,1},{10,2},{11,3},{12,4},{13,5},{14,6},{15,7},{16,8},{17,9... | collective-permute-start | bytes 3145736 | tf_op jit(solution)/shard_map/ppermute | solution.py:363
  95.8 4.3 %collective-permute-start.16 = (bf16[512,1024]{1,0:T(8,128)(2,1)S(1)}, bf16[512,1024]{1,0:T(8,128)(2,1)}, u32[]{:S(2)}, u32[]{:S(2)}) collective-permute-start(bf16[512,1024]{1,0:T(8,128)(2,1)S(1)} %collective-permute-done.15.refs_3_), channel_id=1, source_target_pairs={{8,16},{9,17},{10,18},{11,19},{12,20},{13,21},{14,22},{15,23},{16,... | collective-permute-start | bytes 3145736 | tf_op jit(solution)/shard_map/ppermute | solution.py:363
  100.2 1.1 collective-permute-done.4
  101.4 1.5 collective-permute-start.5
  102.9 2.2 collective-permute-done.5
  105.2 13.1 %collective-permute-done.7.refs_0_ = bf16[512,1024]{1,0:T(8,128)(2,1)S(1)} collective-permute-done((bf16[512,1024]{1,0:T(8,128)(2,1)S(1)}, bf16[512,1024]{1,0:T(8,128)(2,1)S(1)}, u32[]{:S(2)}, u32[]{:S(2)}) %collective-permute-start.7) | collective-permute-done | bytes 1048608 | tf_op jit(solution)/shard_map/ppermute | solution.py:363
  118.3 3.9 %collective-permute-start.12 = (f32[8,128]{1,0:T(8,128)S(1)}, f32[8,128]{1,0:T(8,128)S(1)}, u32[]{:S(2)}, u32[]{:S(2)}) collective-permute-start(f32[8,128]{1,0:T(8,128)S(1)} %add_select_fusion.1), channel_id=1, source_target_pairs={{0,24},{1,25},{2,26},{3,27},{4,28},{5,29},{6,30},{7,31},{8,16},{9,... | collective-permute-start | bytes 12296 | tf_op jit(solution)/shard_map/ppermute | solution.py:363
  122.2 0.4 collective-permute-start.10
  122.7 1.6 collective-permute-start.20
  124.3 13.4 %collective-permute-done.16.refs_2_ = bf16[512,1024]{1,0:T(8,128)(2,1)} collective-permute-done((bf16[512,1024]{1,0:T(8,128)(2,1)S(1)}, bf16[512,1024]{1,0:T(8,128)(2,1)}, u32[]{:S(2)}, u32[]{:S(2)}) %collective-permute-start.16) | collective-permute-done | bytes 1048608 | tf_op jit(solution)/shard_map/ppermute | solution.py:363
  137.7 5.5 %collective-permute-start.17 = (bf16[512,1024]{1,0:T(8,128)(2,1)}, bf16[512,1024]{1,0:T(8,128)(2,1)}, u32[]{:S(2)}, u32[]{:S(2)}) collective-permute-start(bf16[512,1024]{1,0:T(8,128)(2,1)} %collective-permute-done.16.refs_2_), channel_id=1, source_target_pairs={{16,24},{17,25},{18,26},{19,27},{20,28},{21,29},{22,30},{23,31}} | collective-permute-start | bytes 3145736 | tf_op jit(solution)/shard_map/ppermute | solution.py:363
  143.3 0.5 fusion.1
  143.8 1.3 fusion
  145.2 0.6 fusion.2
  147.1 15.7 %product.3.refs_9_ = f32[1024,2048]{1,0:T(8,128)} custom-call(bf16[512,1024]{1,0:T(8,128)(2,1)} %copy-done.13, bf16[512,1024]{1,0:T(8,128)(2,1)} %copy-done.11, bf16[512,1024]{1,0:T(8,128)(2,1)} %collective-permute-done.1.refs_2_, bf16[512,1024]{1,0:T(8,128)(2,1)} %copy-done.6, bf16[512,1024]{1,0:T(8,128)(2,1)} %collective-permute-done.2.refs_4_, ...), custom_call_target="tpu_custom_call" | custom-call | flops 8589934592 | tf_op jit(solution)/shard_map/product/pallas_call | solution.py:221
  162.8 12.2 %product.4 = (bf16[256,2048]{1,0:T(8,128)(2,1)}, bf16[256,2048]{1,0:T(8,128)(2,1)}, bf16[1024,512]{1,0:T(8,128)(2,1)}, bf16[1024,512]{1,0:T(8,128)(2,1)}, bf16[1...) custom-call(f32[1]{0:T(128)} %bitcast.5.refs_0_, bf16[512,1024]{1,0:T(8,128)(2,1)} %collective-permute-done.17.refs_1_, ...), custom_call_target="tpu_custom_call" | custom-call | flops 4294967296 | tf_op jit(solution)/shard_map/product/pallas_call | solution.py:221
  175.1 3.4 %collective-permute-start.21 = (bf16[256,2048]{1,0:T(8,128)(2,1)}, bf16[256,2048]{1,0:T(8,128)(2,1)S(1)}, u32[]{:S(2)}, u32[]{:S(2)}) collective-permute-start(bf16[256,2048]{1,0:T(8,128)(2,1)} %get-tuple-element.52), channel_id=1, source_target_pairs={{0,0},{1,24},{2,2},{3,26},{4,4},{5,28},{6,6},{7,30},{8,8},{9,16},{... | collective-permute-start | bytes 3145736 | tf_op jit(solution)/shard_map/ppermute | solution.py:363
  178.5 0.8 collective-permute-start.22
  179.4 12.3 %product.5 = (bf16[256,2048]{1,0:T(8,128)(2,1)}, bf16[256,2048]{1,0:T(8,128)(2,1)}, bf16[1024,512]{1,0:T(8,128)(2,1)}, bf16[1024,512]{1,0:T(8,128)(2,1)}, bf16[1...) custom-call(f32[1]{0:T(128)} %bitcast.5.refs_0_, ...), custom_call_target="tpu_custom_call", output_to_operand_aliasing={{2}: (10, {}), {3}: (11, {}), {4}: (12, {}), {5}: (13, {})} | custom-call | flops 4294967296 | tf_op jit(solution)/shard_map/product/pallas_call | solution.py:221
  191.7 1.6 collective-permute-start.24
  193.3 0.3 collective-permute-start.25
  193.6 26.2 %collective-permute-done.21.refs_0_ = bf16[256,2048]{1,0:T(8,128)(2,1)S(1)} collective-permute-done((bf16[256,2048]{1,0:T(8,128)(2,1)}, bf16[256,2048]{1,0:T(8,128)(2,1)S(1)}, u32[]{:S(2)}, u32[]{:S(2)}) %collective-permute-start.21) | collective-permute-done | bytes 1048608 | tf_op jit(solution)/shard_map/ppermute | solution.py:363
  219.8 1.9 collective-permute-start.26
  221.7 5.5 %collective-permute-start.27 = (bf16[256,2048]{1,0:T(8,128)(2,1)}, bf16[256,2048]{1,0:T(8,128)(2,1)}, u32[]{:S(2)}, u32[]{:S(2)}) collective-permute-start(bf16[256,2048]{1,0:T(8,128)(2,1)} %get-tuple-element.72), channel_id=1, source_target_pairs={{0,24},{1,0},{2,26},{3,2},{4,28},{5,4},{6,30},{7,6},{8,16},{9,8},{... | collective-permute-start | bytes 3145736 | tf_op jit(solution)/shard_map/ppermute | solution.py:363
  227.2 11.4 %feedback_update.2 = (f32[2,256,4096]{2,1,0:T(8,128)}, bf16[2,256,4096]{2,1,0:T(8,128)(2,1)}, bf16[2,256,4096]{2,1,0:T(8,128)(2,1)}, bf16[2,256,4096]{2,1,0:T(8,128)(2,1)}) custom-call(s32[1]{0:T(128)} %bitcast.4._, f32[1]{0:T(128)} %bitcast.3.scale_ref, bf16[256,2048]{1,0:T(8,128)(2,1)} %copy-done.7, bf16[256,2048]{1,0:T(8,128)(2,1)} %copy-done.8, ...), custom_call_target="tpu_custom_call" | custom-call | tf_op jit(solution)/shard_map/feedback_update/pallas_call | solution.py:330
  238.6 1.0 collective-permute-done.25.refs_3_
  239.6 19.5 %weight_update.1 = (f32[512,4096]{1,0:T(8,128)}, bf16[512,4096]{1,0:T(8,128)(2,1)}, bf16[512,4096]{1,0:T(8,128)(2,1)}, bf16[512,4096]{1,0:T(8,128)(2,1)}) custom-call(f32[1]{0:T(128)} %bitcast.3.scale_ref, bf16[1024,512]{1,0:T(8,128)(2,1)} %get-tuple-element.60.refs_0_, bf16[1024,512]{1,0:T(8,128)(2,1)} %collective-permute-done.23.refs_1_, ...), custom_call_target="tpu_custom_call" | custom-call | tf_op jit(solution)/shard_map/weight_update/pallas_call | solution.py:272
  259.2 12.8 %collective-permute-done.27.refs_1_ = bf16[256,2048]{1,0:T(8,128)(2,1)} collective-permute-done((bf16[256,2048]{1,0:T(8,128)(2,1)}, bf16[256,2048]{1,0:T(8,128)(2,1)}, u32[]{:S(2)}, u32[]{:S(2)}) %collective-permute-start.27) | collective-permute-done | bytes 1048608 | tf_op jit(solution)/shard_map/ppermute | solution.py:363
  272.0 11.4 %feedback_update.3 = (f32[2,256,4096]{2,1,0:T(8,128)}, bf16[2,256,4096]{2,1,0:T(8,128)(2,1)}, bf16[2,256,4096]{2,1,0:T(8,128)(2,1)}, bf16[2,256,4096]{2,1,0:T(8,128)(2,1)}) custom-call(s32[1]{0:T(128)} %bitcast.6._, f32[1]{0:T(128)} %bitcast.3.scale_ref, ...), custom_call_target="tpu_custom_call", output_to_operand_aliasing={{0}: (7, {}), {1}: (8, {}), {2}: (9, {}), {3}: (10, {})} | custom-call | tf_op jit(solution)/shard_map/feedback_update/pallas_call | solution.py:330
  (60 shorter events, 1.1 us)
Async XLA Ops:
  7.2 139.9 %all-gather.2.cloned.1.call-start = ((), (), s32[]{:S(2)}) async-start(), calls=%async_computation | async-start | bytes 18874368 | tf_op jit(solution)/shard_map/all_gather | solution.py:436
  7.2 1.6 copy-start
  8.8 10.7 %copy-start.1 = (bf16[256,4096]{1,0:T(8,128)(2,1)S(1)}, bf16[256,4096]{1,0:T(8,128)(2,1)}, u32[]{:S(2)}) copy-start(bf16[256,4096]{1,0:T(8,128)(2,1)} %x_ref.1) | copy-start | bytes 6291460
  8.8 10.7 %copy-start.2 = (bf16[2048,512]{1,0:T(8,128)(2,1)S(1)}, bf16[2048,512]{1,0:T(8,128)(2,1)}, u32[]{:S(2)}) copy-start(bf16[2048,512]{1,0:T(8,128)(2,1)} %errors_ref.1) | copy-start | bytes 6291460
  9.1 2.0 collective-permute-start
  11.1 33.0 %copy-start.6 = (bf16[512,1024]{1,0:T(8,128)(2,1)}, bf16[512,1024]{1,0:T(8,128)(2,1)S(1)}, u32[]{:S(2)}) copy-start(bf16[512,1024]{1,0:T(8,128)(2,1)S(1)} %constant_dynamic-update-slice_fusion.refs_3_) | copy-start | bytes 3145732
  11.1 27.2 %collective-permute-start.2 = (bf16[512,1024]{1,0:T(8,128)(2,1)S(1)}, bf16[512,1024]{1,0:T(8,128)(2,1)}, u32[]{:S(2)}, u32[]{:S(2)}) collective-permute-start(bf16[512,1024]{1,0:T(8,128)(2,1)S(1)} %constant_dynamic-update-slice_fusion.refs_3_), channel_id=1, source_target_pairs={{8,0},{9,1},{10,2},{11,3},{12,4},{13,5},{14,6},{15,7},{16,8},{17,9... | collective-permute-start | bytes 3145736 | tf_op jit(solution)/shard_map/ppermute | solution.py:363
  13.5 26.9 %collective-permute-start.1 = (bf16[512,1024]{1,0:T(8,128)(2,1)S(1)}, bf16[512,1024]{1,0:T(8,128)(2,1)}, u32[]{:S(2)}, u32[]{:S(2)}) collective-permute-start(bf16[512,1024]{1,0:T(8,128)(2,1)S(1)} %constant_dynamic-update-slice_fusion.refs_3_), channel_id=1, source_target_pairs={{0,8},{1,9},{2,10},{3,11},{4,12},{5,13},{6,14},{7,15},{8,16},{9,17... | collective-permute-start | bytes 3145736 | tf_op jit(solution)/shard_map/ppermute | solution.py:363
  18.0 26.1 %collective-permute-start.13 = (bf16[256,1024]{1,0:T(8,128)(2,1)S(1)}, bf16[256,1024]{1,0:T(8,128)(2,1)S(1)}, u32[]{:S(2)}, u32[]{:S(2)}) collective-permute-start(bf16[256,1024]{1,0:T(8,128)(2,1)S(1)} %get-tuple-element.48), channel_id=1, source_target_pairs={{0,4},{1,5},{2,6},{3,7},{4,0},{5,1},{6,2},{7,3},{8,12},{9,13},{10,... | collective-permute-start | bytes 1572872 | tf_op jit(solution)/shard_map/ppermute | solution.py:363
  19.5 24.6 %collective-permute-start.14 = (bf16[256,1024]{1,0:T(8,128)(2,1)S(1)}, bf16[256,1024]{1,0:T(8,128)(2,1)S(1)}, u32[]{:S(2)}, u32[]{:S(2)}) collective-permute-start(bf16[256,1024]{1,0:T(8,128)(2,1)S(1)} %get-tuple-element.50), channel_id=1, source_target_pairs={{0,6},{1,7},{2,4},{3,5},{4,2},{5,3},{6,0},{7,1},{8,14},{9,15},{10,... | collective-permute-start | bytes 1572872 | tf_op jit(solution)/shard_map/ppermute | solution.py:363
  40.4 3.6 %collective-permute-start.3 = (f32[8,128]{1,0:T(8,128)S(1)}, f32[8,128]{1,0:T(8,128)S(1)}, u32[]{:S(2)}, u32[]{:S(2)}) collective-permute-start(f32[8,128]{1,0:T(8,128)S(1)} %longest.1), channel_id=1, source_target_pairs={{0,1},{1,0},{2,3},{3,2},{4,5},{5,4},{6,7},{7,6},{8,9},{9,8},{10,11... | collective-permute-start | bytes 12296 | tf_op jit(solution)/shard_map/ppermute | solution.py:363
  44.2 118.6 %copy-start.3 = (bf16[512,1024]{1,0:T(8,128)(2,1)}, bf16[512,1024]{1,0:T(8,128)(2,1)S(1)}, u32[]{:S(2)}) copy-start(bf16[512,1024]{1,0:T(8,128)(2,1)S(1)} %constant_dynamic-update-slice_fusion.2.refs_4_) | copy-start | bytes 3145732
  44.2 26.3 %collective-permute-start.8 = (bf16[512,1024]{1,0:T(8,128)(2,1)}, bf16[512,1024]{1,0:T(8,128)(2,1)S(1)}, u32[]{:S(2)}, u32[]{:S(2)}) collective-permute-start(bf16[512,1024]{1,0:T(8,128)(2,1)} %collective-permute-done.2.refs_4_), channel_id=1, source_target_pairs={{8,0},{9,1},{10,2},{11,3},{12,4},{13,5},{14,6},{15,7},{16,8},{17,9... | collective-permute-start | bytes 3145736 | tf_op jit(solution)/shard_map/ppermute | solution.py:363
  46.7 28.2 %collective-permute-start.6 = (bf16[512,1024]{1,0:T(8,128)(2,1)}, bf16[512,1024]{1,0:T(8,128)(2,1)S(1)}, u32[]{:S(2)}, u32[]{:S(2)}) collective-permute-start(bf16[512,1024]{1,0:T(8,128)(2,1)} %collective-permute-done.1.refs_2_), channel_id=1, source_target_pairs={{8,16},{9,17},{10,18},{11,19},{12,20},{13,21},{14,22},{15,23},{16,... | collective-permute-start | bytes 3145736 | tf_op jit(solution)/shard_map/ppermute | solution.py:363
  49.4 40.2 %collective-permute-start.18 = (bf16[512,1024]{1,0:T(8,128)(2,1)S(1)}, bf16[512,1024]{1,0:T(8,128)(2,1)S(1)}, u32[]{:S(2)}, u32[]{:S(2)}) collective-permute-start(bf16[512,1024]{1,0:T(8,128)(2,1)S(1)} %constant_dynamic-update-slice_fusion.2.refs_4_), channel_id=1, source_target_pairs={{8,0},{9,1},{10,2},{11,3},{12,4},{13,5},{14,6},{15,7},{16,8},{17,9... | collective-permute-start | bytes 3145736 | tf_op jit(solution)/shard_map/ppermute | solution.py:363
  52.6 43.2 %collective-permute-start.15 = (bf16[512,1024]{1,0:T(8,128)(2,1)S(1)}, bf16[512,1024]{1,0:T(8,128)(2,1)S(1)}, u32[]{:S(2)}, u32[]{:S(2)}) collective-permute-start(bf16[512,1024]{1,0:T(8,128)(2,1)S(1)} %constant_dynamic-update-slice_fusion.2.refs_4_), channel_id=1, source_target_pairs={{0,8},{1,9},{2,10},{3,11},{4,12},{5,13},{6,14},{7,15},{8,16},{9,17... | collective-permute-start | bytes 3145736 | tf_op jit(solution)/shard_map/ppermute | solution.py:363
  70.5 67.2 %copy-start.10 = (bf16[512,1024]{1,0:T(8,128)(2,1)}, bf16[512,1024]{1,0:T(8,128)(2,1)S(1)}, u32[]{:S(2)}) copy-start(bf16[512,1024]{1,0:T(8,128)(2,1)S(1)} %collective-permute-done.8.refs_5_) | copy-start | bytes 3145732
  70.5 34.6 %collective-permute-start.9 = (bf16[512,1024]{1,0:T(8,128)(2,1)S(1)}, bf16[512,1024]{1,0:T(8,128)(2,1)S(1)}, u32[]{:S(2)}, u32[]{:S(2)}) collective-permute-start(bf16[512,1024]{1,0:T(8,128)(2,1)S(1)} %collective-permute-done.8.refs_5_), channel_id=1, source_target_pairs={{8,0},{9,1},{10,2},{11,3},{12,4},{13,5},{14,6},{15,7}} | collective-permute-start | bytes 3145736 | tf_op jit(solution)/shard_map/ppermute | solution.py:363
  74.9 68.3 %copy-start.11 = (bf16[512,1024]{1,0:T(8,128)(2,1)}, bf16[512,1024]{1,0:T(8,128)(2,1)S(1)}, u32[]{:S(2)}) copy-start(bf16[512,1024]{1,0:T(8,128)(2,1)S(1)} %collective-permute-done.6.refs_1_) | copy-start | bytes 3145732
  74.9 43.4 %collective-permute-start.7 = (bf16[512,1024]{1,0:T(8,128)(2,1)S(1)}, bf16[512,1024]{1,0:T(8,128)(2,1)S(1)}, u32[]{:S(2)}, u32[]{:S(2)}) collective-permute-start(bf16[512,1024]{1,0:T(8,128)(2,1)S(1)} %collective-permute-done.6.refs_1_), channel_id=1, source_target_pairs={{16,24},{17,25},{18,26},{19,27},{20,28},{21,29},{22,30},{23,31}} | collective-permute-start | bytes 3145736 | tf_op jit(solution)/shard_map/ppermute | solution.py:363
  89.7 73.1 %copy-start.4 = (bf16[512,1024]{1,0:T(8,128)(2,1)}, bf16[512,1024]{1,0:T(8,128)(2,1)S(1)}, u32[]{:S(2)}) copy-start(bf16[512,1024]{1,0:T(8,128)(2,1)S(1)} %collective-permute-done.18.refs_5_) | copy-start | bytes 3145732
  89.7 33.0 %collective-permute-start.19 = (bf16[512,1024]{1,0:T(8,128)(2,1)S(1)}, bf16[512,1024]{1,0:T(8,128)(2,1)}, u32[]{:S(2)}, u32[]{:S(2)}) collective-permute-start(bf16[512,1024]{1,0:T(8,128)(2,1)S(1)} %collective-permute-done.18.refs_5_), channel_id=1, source_target_pairs={{8,0},{9,1},{10,2},{11,3},{12,4},{13,5},{14,6},{15,7},{16,8},{17,9... | collective-permute-start | bytes 3145736 | tf_op jit(solution)/shard_map/ppermute | solution.py:363
  95.8 67.0 %copy-start.5 = (bf16[512,1024]{1,0:T(8,128)(2,1)}, bf16[512,1024]{1,0:T(8,128)(2,1)S(1)}, u32[]{:S(2)}) copy-start(bf16[512,1024]{1,0:T(8,128)(2,1)S(1)} %collective-permute-done.15.refs_3_) | copy-start | bytes 3145732
  95.8 41.9 %collective-permute-start.16 = (bf16[512,1024]{1,0:T(8,128)(2,1)S(1)}, bf16[512,1024]{1,0:T(8,128)(2,1)}, u32[]{:S(2)}, u32[]{:S(2)}) collective-permute-start(bf16[512,1024]{1,0:T(8,128)(2,1)S(1)} %collective-permute-done.15.refs_3_), channel_id=1, source_target_pairs={{8,16},{9,17},{10,18},{11,19},{12,20},{13,21},{14,22},{15,23},{16,... | collective-permute-start | bytes 3145736 | tf_op jit(solution)/shard_map/ppermute | solution.py:363
  100.1 1.2 collective-permute-start.4
  101.4 3.7 %collective-permute-start.5 = (f32[8,128]{1,0:T(8,128)S(1)}, f32[8,128]{1,0:T(8,128)S(1)}, u32[]{:S(2)}, u32[]{:S(2)}) collective-permute-start(f32[8,128]{1,0:T(8,128)S(1)} %add_select_fusion.2), channel_id=1, source_target_pairs={{0,4},{1,5},{2,6},{3,7},{4,0},{5,1},{6,2},{7,3},{8,12},{9,13},{10,... | collective-permute-start | bytes 12296 | tf_op jit(solution)/shard_map/ppermute | solution.py:363
  105.2 38.0 %copy-start.12 = (bf16[512,1024]{1,0:T(8,128)(2,1)}, bf16[512,1024]{1,0:T(8,128)(2,1)S(1)}, u32[]{:S(2)}) copy-start(bf16[512,1024]{1,0:T(8,128)(2,1)S(1)} %collective-permute-done.9.refs_6_) | copy-start | bytes 3145732
  118.3 24.9 %copy-start.13 = (bf16[512,1024]{1,0:T(8,128)(2,1)}, bf16[512,1024]{1,0:T(8,128)(2,1)S(1)}, u32[]{:S(2)}) copy-start(bf16[512,1024]{1,0:T(8,128)(2,1)S(1)} %collective-permute-done.7.refs_0_) | copy-start | bytes 3145732
  118.3 24.9 %collective-permute-start.11 = (f32[8,128]{1,0:T(8,128)S(1)}, f32[8,128]{1,0:T(8,128)S(1)}, u32[]{:S(2)}, u32[]{:S(2)}) collective-permute-start(f32[8,128]{1,0:T(8,128)S(1)} %add_select_fusion.1), channel_id=1, source_target_pairs={{0,16},{1,17},{2,18},{3,19},{4,20},{5,21},{6,22},{7,23},{8,24},{9,... | collective-permute-start | bytes 12296 | tf_op jit(solution)/shard_map/ppermute | solution.py:363
  118.3 24.9 %collective-permute-start.12 = (f32[8,128]{1,0:T(8,128)S(1)}, f32[8,128]{1,0:T(8,128)S(1)}, u32[]{:S(2)}, u32[]{:S(2)}) collective-permute-start(f32[8,128]{1,0:T(8,128)S(1)} %add_select_fusion.1), channel_id=1, source_target_pairs={{0,24},{1,25},{2,26},{3,27},{4,28},{5,29},{6,30},{7,31},{8,16},{9,... | collective-permute-start | bytes 12296 | tf_op jit(solution)/shard_map/ppermute | solution.py:363
  122.2 21.0 %collective-permute-start.10 = (f32[8,128]{1,0:T(8,128)S(1)}, f32[8,128]{1,0:T(8,128)S(1)}, u32[]{:S(2)}, u32[]{:S(2)}) collective-permute-start(f32[8,128]{1,0:T(8,128)S(1)} %add_select_fusion.1), channel_id=1, source_target_pairs={{0,8},{1,9},{2,10},{3,11},{4,12},{5,13},{6,14},{7,15},{8,0},{9,1},... | collective-permute-start | bytes 12296 | tf_op jit(solution)/shard_map/ppermute | solution.py:363
  122.7 40.1 %collective-permute-start.20 = (bf16[512,1024]{1,0:T(8,128)(2,1)}, bf16[512,1024]{1,0:T(8,128)(2,1)}, u32[]{:S(2)}, u32[]{:S(2)}) collective-permute-start(bf16[512,1024]{1,0:T(8,128)(2,1)} %collective-permute-done.19.refs_6_), channel_id=1, source_target_pairs={{8,0},{9,1},{10,2},{11,3},{12,4},{13,5},{14,6},{15,7}} | collective-permute-start | bytes 3145736 | tf_op jit(solution)/shard_map/ppermute | solution.py:363
  137.7 25.1 %collective-permute-start.17 = (bf16[512,1024]{1,0:T(8,128)(2,1)}, bf16[512,1024]{1,0:T(8,128)(2,1)}, u32[]{:S(2)}, u32[]{:S(2)}) collective-permute-start(bf16[512,1024]{1,0:T(8,128)(2,1)} %collective-permute-done.16.refs_2_), channel_id=1, source_target_pairs={{16,24},{17,25},{18,26},{19,27},{20,28},{21,29},{22,30},{23,31}} | collective-permute-start | bytes 3145736 | tf_op jit(solution)/shard_map/ppermute | solution.py:363
  175.1 44.7 %collective-permute-start.21 = (bf16[256,2048]{1,0:T(8,128)(2,1)}, bf16[256,2048]{1,0:T(8,128)(2,1)S(1)}, u32[]{:S(2)}, u32[]{:S(2)}) collective-permute-start(bf16[256,2048]{1,0:T(8,128)(2,1)} %get-tuple-element.52), channel_id=1, source_target_pairs={{0,0},{1,24},{2,2},{3,26},{4,4},{5,28},{6,6},{7,30},{8,8},{9,16},{... | collective-permute-start | bytes 3145736 | tf_op jit(solution)/shard_map/ppermute | solution.py:363
  178.5 43.2 %collective-permute-start.22 = (bf16[256,2048]{1,0:T(8,128)(2,1)}, bf16[256,2048]{1,0:T(8,128)(2,1)S(1)}, u32[]{:S(2)}, u32[]{:S(2)}) collective-permute-start(bf16[256,2048]{1,0:T(8,128)(2,1)} %get-tuple-element.53), channel_id=1, source_target_pairs={{0,16},{1,8},{2,18},{3,10},{4,20},{5,12},{6,22},{7,14},{8,24},{9,0... | collective-permute-start | bytes 3145736 | tf_op jit(solution)/shard_map/ppermute | solution.py:363
  191.6 46.9 %collective-permute-start.23 = (bf16[1024,512]{1,0:T(8,128)(2,1)}, bf16[1024,512]{1,0:T(8,128)(2,1)}, u32[]{:S(2)}, u32[]{:S(2)}) collective-permute-start(bf16[1024,512]{1,0:T(8,128)(2,1)} %get-tuple-element.61), channel_id=1, source_target_pairs={{0,2},{1,3},{2,0},{3,1},{4,6},{5,7},{6,4},{7,5},{8,10},{9,11},{10,... | collective-permute-start | bytes 3145736 | tf_op jit(solution)/shard_map/ppermute | solution.py:363
  191.7 46.9 %collective-permute-start.24 = (bf16[1024,512]{1,0:T(8,128)(2,1)}, bf16[1024,512]{1,0:T(8,128)(2,1)}, u32[]{:S(2)}, u32[]{:S(2)}) collective-permute-start(bf16[1024,512]{1,0:T(8,128)(2,1)} %get-tuple-element.62), channel_id=1, source_target_pairs={{0,4},{1,5},{2,6},{3,7},{4,0},{5,1},{6,2},{7,3},{8,12},{9,13},{10,... | collective-permute-start | bytes 3145736 | tf_op jit(solution)/shard_map/ppermute | solution.py:363
  193.3 46.3 %collective-permute-start.25 = (bf16[1024,512]{1,0:T(8,128)(2,1)}, bf16[1024,512]{1,0:T(8,128)(2,1)}, u32[]{:S(2)}, u32[]{:S(2)}) collective-permute-start(bf16[1024,512]{1,0:T(8,128)(2,1)} %get-tuple-element.63), channel_id=1, source_target_pairs={{0,6},{1,7},{2,4},{3,5},{4,2},{5,3},{6,0},{7,1},{8,14},{9,15},{10,... | collective-permute-start | bytes 3145736 | tf_op jit(solution)/shard_map/ppermute | solution.py:363
  219.8 7.4 %copy-start.7 = (bf16[256,2048]{1,0:T(8,128)(2,1)}, bf16[256,2048]{1,0:T(8,128)(2,1)S(1)}, u32[]{:S(2)}) copy-start(bf16[256,2048]{1,0:T(8,128)(2,1)S(1)} %collective-permute-done.21.refs_0_) | copy-start | bytes 3145732
  219.8 39.3 %collective-permute-start.26 = (bf16[256,2048]{1,0:T(8,128)(2,1)}, bf16[256,2048]{1,0:T(8,128)(2,1)S(1)}, u32[]{:S(2)}, u32[]{:S(2)}) collective-permute-start(bf16[256,2048]{1,0:T(8,128)(2,1)} %get-tuple-element.70), channel_id=1, source_target_pairs={{0,8},{1,16},{2,10},{3,18},{4,12},{5,20},{6,14},{7,22},{8,0},{9,24... | collective-permute-start | bytes 3145736 | tf_op jit(solution)/shard_map/ppermute | solution.py:363
  221.7 5.5 %copy-start.8 = (bf16[256,2048]{1,0:T(8,128)(2,1)}, bf16[256,2048]{1,0:T(8,128)(2,1)S(1)}, u32[]{:S(2)}) copy-start(bf16[256,2048]{1,0:T(8,128)(2,1)S(1)} %collective-permute-done.22.refs_1_) | copy-start | bytes 3145732
  221.7 50.3 %collective-permute-start.27 = (bf16[256,2048]{1,0:T(8,128)(2,1)}, bf16[256,2048]{1,0:T(8,128)(2,1)}, u32[]{:S(2)}, u32[]{:S(2)}) collective-permute-start(bf16[256,2048]{1,0:T(8,128)(2,1)} %get-tuple-element.72), channel_id=1, source_target_pairs={{0,24},{1,0},{2,26},{3,2},{4,28},{5,4},{6,30},{7,6},{8,16},{9,8},{... | collective-permute-start | bytes 3145736 | tf_op jit(solution)/shard_map/ppermute | solution.py:363
  259.2 12.8 %copy-start.9 = (bf16[256,2048]{1,0:T(8,128)(2,1)}, bf16[256,2048]{1,0:T(8,128)(2,1)S(1)}, u32[]{:S(2)}) copy-start(bf16[256,2048]{1,0:T(8,128)(2,1)S(1)} %collective-permute-done.26.refs_0_) | copy-start | bytes 3145732
Sparse Core Ops, SparseCore 0:
  44.4 91.1 all-gather.1

commit v5 on v4

--- a/solution.py
+++ b/solution.py
@@ -236,7 +236,9 @@
         ],
         input_output_aliases={n_in + i: len(picks) + i for i in range(len(old))},
         compiler_params=pltpu.CompilerParams(vmem_limit_bytes=56 * 2**20),
-        cost_estimate=pl.CostEstimate(flops=2 * width * depth * QUAD * outputs, bytes_accessed=0, transcendentals=0),
+        cost_estimate=pl.CostEstimate(
+            flops=(2 if picks else 40) * width * depth * QUAD * outputs, bytes_accessed=0, transcendentals=0
+        ),
         name="product",
     )(*scalars, *candidates, errors, *so_far, *old)
 

time: 291 us -> 290 us (level)
  no operation moved by 1% of the time
where the time goes in v5:
time: 290 us; the launch traced here: 289 us
  waiting for transfers between devices  126 us (43%)
  Pallas kernels  84.7 us (29%)
  starting transfers between devices  57.9 us (20%)
  between operations  15.7 us (5%)
  local copies, waits for them, and re-layouts  2.9 us (1%)
    ppermute x28, waiting for transfers between devices, permute(): return lax.ppermute(x, ('row', 'col'), pairs)  126 us
    ppermute x28, starting transfers between devices, permute(): return lax.ppermute(x, ('row', 'col'), pairs)  57.8 us
    pallas_call x3, Pallas kernels, product(): pl.pallas_call(functools.partial(product_kernel, line, n_col, tokens, out...  40.2 us
    pallas_call x2, Pallas kernels, feedback_update(): pl.pallas_call(functools.partial(feedback_kernel, line, odd, len(held)),...  22.7 us
    pallas_call x1, Pallas kernels, weight_update(): pl.pallas_call(functools.partial(weight_kernel, line), grid=(line,), out_...  19.5 us
  transfers between devices with their start and end apart: 29, of which 14 were waited for; matrix products, arithmetic and copies ran while one was open for 1% of the time, Pallas kernels for 21%

profile of v5, /device:TPU:20, one launch (start us, length us, event | category | flops | bytes accessed | tf_op | source)
XLA Modules:
  0.0 289.1 jit_solution(422703518342305442)
XLA Ops:
  7.2 1.6 copy-done
  9.2 1.9 collective-permute-done
  11.1 2.4 collective-permute-start.2
  13.5 3.5 %collective-permute-start.1 = (bf16[512,1024]{1,0:T(8,128)(2,1)S(1)}, bf16[512,1024]{1,0:T(8,128)(2,1)S(1)}, u32[]{:S(2)}, u32[]{:S(2)}) collective-permute-start(bf16[512,1024]{1,0:T(8,128)(2,1)S(1)} %constant_dynamic-update-slice_fusion.refs_3_), channel_id=1, source_target_pairs={{0,8},{1,9},{2,10},{3,11},{4,12},{5,13},{6,14},{7,15},{8,16},{9,17... | collective-permute-start | bytes 3145736 | tf_op jit(solution)/shard_map/ppermute | solution.py:365
  17.1 1.6 collective-permute-start.13
  18.6 1.9 longest.1
  20.6 17.7 %collective-permute-done.2.refs_4_ = bf16[512,1024]{1,0:T(8,128)(2,1)S(1)} collective-permute-done((bf16[512,1024]{1,0:T(8,128)(2,1)S(1)}, bf16[512,1024]{1,0:T(8,128)(2,1)S(1)}, u32[]{:S(2)}, u32[]{:S(2)}) %collective-permute-start.2) | collective-permute-done | bytes 1048608 | tf_op jit(solution)/shard_map/ppermute | solution.py:365
  38.2 2.1 collective-permute-done.1.refs_2_
  40.3 0.5 collective-permute-start.3
  40.8 3.1 %collective-permute-done.3 = f32[8,128]{1,0:T(8,128)S(1)} collective-permute-done((f32[8,128]{1,0:T(8,128)S(1)}, f32[8,128]{1,0:T(8,128)S(1)}, u32[]{:S(2)}, u32[]{:S(2)}) %collective-permute-start.3) | collective-permute-done | bytes 4128 | tf_op jit(solution)/shard_map/ppermute | solution.py:365
  44.1 2.4 collective-permute-start.8
  46.6 1.9 collective-permute-start.6
  48.5 4.0 %collective-permute-start.18 = (bf16[512,1024]{1,0:T(8,128)(2,1)S(1)}, bf16[512,1024]{1,0:T(8,128)(2,1)S(1)}, u32[]{:S(2)}, u32[]{:S(2)}) collective-permute-start(bf16[512,1024]{1,0:T(8,128)(2,1)S(1)} %constant_dynamic-update-slice_fusion.2.refs_4_), channel_id=1, source_target_pairs={{8,0},{9,1},{10,2},{11,3},{12,4},{13,5},{14,6},{15,7},{16,8},{17,9... | collective-permute-start | bytes 3145736 | tf_op jit(solution)/shard_map/ppermute | solution.py:365
  52.5 1.9 collective-permute-start.15
  54.4 15.7 %collective-permute-done.8.refs_5_ = bf16[512,1024]{1,0:T(8,128)(2,1)S(1)} collective-permute-done((bf16[512,1024]{1,0:T(8,128)(2,1)S(1)}, bf16[512,1024]{1,0:T(8,128)(2,1)S(1)}, u32[]{:S(2)}, u32[]{:S(2)}) %collective-permute-start.8) | collective-permute-done | bytes 1048608 | tf_op jit(solution)/shard_map/ppermute | solution.py:365
  70.1 0.7 collective-permute-start.9
  70.8 3.9 %collective-permute-done.6.refs_1_ = bf16[512,1024]{1,0:T(8,128)(2,1)S(1)} collective-permute-done((bf16[512,1024]{1,0:T(8,128)(2,1)}, bf16[512,1024]{1,0:T(8,128)(2,1)S(1)}, u32[]{:S(2)}, u32[]{:S(2)}) %collective-permute-start.6) | collective-permute-done | bytes 1048608 | tf_op jit(solution)/shard_map/ppermute | solution.py:365
  74.8 2.0 collective-permute-start.7
  76.8 12.6 %collective-permute-done.18.refs_5_ = bf16[512,1024]{1,0:T(8,128)(2,1)S(1)} collective-permute-done((bf16[512,1024]{1,0:T(8,128)(2,1)S(1)}, bf16[512,1024]{1,0:T(8,128)(2,1)S(1)}, u32[]{:S(2)}, u32[]{:S(2)}) %collective-permute-start.18) | collective-permute-done | bytes 1048608 | tf_op jit(solution)/shard_map/ppermute | solution.py:365
  89.4 6.1 %collective-permute-start.19 = (bf16[512,1024]{1,0:T(8,128)(2,1)S(1)}, bf16[512,1024]{1,0:T(8,128)(2,1)}, u32[]{:S(2)}, u32[]{:S(2)}) collective-permute-start(bf16[512,1024]{1,0:T(8,128)(2,1)S(1)} %collective-permute-done.18.refs_5_), channel_id=1, source_target_pairs={{8,0},{9,1},{10,2},{11,3},{12,4},{13,5},{14,6},{15,7},{16,8},{17,9... | collective-permute-start | bytes 3145736 | tf_op jit(solution)/shard_map/ppermute | solution.py:365
  95.5 3.7 %collective-permute-start.16 = (bf16[512,1024]{1,0:T(8,128)(2,1)S(1)}, bf16[512,1024]{1,0:T(8,128)(2,1)}, u32[]{:S(2)}, u32[]{:S(2)}) collective-permute-start(bf16[512,1024]{1,0:T(8,128)(2,1)S(1)} %collective-permute-done.15.refs_3_), channel_id=1, source_target_pairs={{8,16},{9,17},{10,18},{11,19},{12,20},{13,21},{14,22},{15,23},{16,... | collective-permute-start | bytes 3145736 | tf_op jit(solution)/shard_map/ppermute | solution.py:365
  99.3 1.1 collective-permute-done.4
  100.5 1.5 collective-permute-start.5
  102.0 2.2 collective-permute-done.5
  104.2 13.1 %collective-permute-done.7.refs_0_ = bf16[512,1024]{1,0:T(8,128)(2,1)S(1)} collective-permute-done((bf16[512,1024]{1,0:T(8,128)(2,1)S(1)}, bf16[512,1024]{1,0:T(8,128)(2,1)S(1)}, u32[]{:S(2)}, u32[]{:S(2)}) %collective-permute-start.7) | collective-permute-done | bytes 1048608 | tf_op jit(solution)/shard_map/ppermute | solution.py:365
  117.3 3.9 %collective-permute-start.12 = (f32[8,128]{1,0:T(8,128)S(1)}, f32[8,128]{1,0:T(8,128)S(1)}, u32[]{:S(2)}, u32[]{:S(2)}) collective-permute-start(f32[8,128]{1,0:T(8,128)S(1)} %add_select_fusion.1), channel_id=1, source_target_pairs={{0,24},{1,25},{2,26},{3,27},{4,28},{5,29},{6,30},{7,31},{8,16},{9,... | collective-permute-start | bytes 12296 | tf_op jit(solution)/shard_map/ppermute | solution.py:365
  121.3 0.4 collective-permute-start.10
  121.7 1.7 collective-permute-start.20
  123.4 13.3 %collective-permute-done.16.refs_2_ = bf16[512,1024]{1,0:T(8,128)(2,1)} collective-permute-done((bf16[512,1024]{1,0:T(8,128)(2,1)S(1)}, bf16[512,1024]{1,0:T(8,128)(2,1)}, u32[]{:S(2)}, u32[]{:S(2)}) %collective-permute-start.16) | collective-permute-done | bytes 1048608 | tf_op jit(solution)/shard_map/ppermute | solution.py:365
  136.7 5.5 %collective-permute-start.17 = (bf16[512,1024]{1,0:T(8,128)(2,1)}, bf16[512,1024]{1,0:T(8,128)(2,1)}, u32[]{:S(2)}, u32[]{:S(2)}) collective-permute-start(bf16[512,1024]{1,0:T(8,128)(2,1)} %collective-permute-done.16.refs_2_), channel_id=1, source_target_pairs={{16,24},{17,25},{18,26},{19,27},{20,28},{21,29},{22,30},{23,31}} | collective-permute-start | bytes 3145736 | tf_op jit(solution)/shard_map/ppermute | solution.py:365
  142.3 0.5 fusion.1
  142.8 1.3 fusion
  144.1 0.6 fusion.2
  146.0 15.7 %product.3.refs_9_ = f32[1024,2048]{1,0:T(8,128)} custom-call(bf16[512,1024]{1,0:T(8,128)(2,1)} %copy-done.15, bf16[512,1024]{1,0:T(8,128)(2,1)} %copy-done.13, bf16[512,1024]{1,0:T(8,128)(2,1)} %copy-done.11, bf16[512,1024]{1,0:T(8,128)(2,1)} %copy-done.9, bf16[512,1024]{1,0:T(8,128)(2,1)} %copy-done.10, bf16[512,1024]{1,0:T(8,128)(2,1)} %copy-done.12, ...), custom_call_target="tpu_custom_call" | custom-call | flops 171798691840 | tf_op jit(solution)/shard_map/product/pallas_call | solution.py:221
  161.7 12.2 %product.4 = (bf16[256,2048]{1,0:T(8,128)(2,1)}, bf16[256,2048]{1,0:T(8,128)(2,1)}, bf16[1024,512]{1,0:T(8,128)(2,1)}, bf16[1024,512]{1,0:T(8,128)(2,1)}, bf16[1...) custom-call(f32[1]{0:T(128)} %bitcast.5.refs_0_, bf16[512,1024]{1,0:T(8,128)(2,1)} %collective-permute-done.17.refs_1_, ...), custom_call_target="tpu_custom_call" | custom-call | flops 4294967296 | tf_op jit(solution)/shard_map/product/pallas_call | solution.py:221
  174.0 3.6 %collective-permute-start.21 = (bf16[256,2048]{1,0:T(8,128)(2,1)}, bf16[256,2048]{1,0:T(8,128)(2,1)S(1)}, u32[]{:S(2)}, u32[]{:S(2)}) collective-permute-start(bf16[256,2048]{1,0:T(8,128)(2,1)} %get-tuple-element.52), channel_id=1, source_target_pairs={{0,0},{1,24},{2,2},{3,26},{4,4},{5,28},{6,6},{7,30},{8,8},{9,16},{... | collective-permute-start | bytes 3145736 | tf_op jit(solution)/shard_map/ppermute | solution.py:365
  177.6 0.8 collective-permute-start.22
  178.4 12.3 %product.5 = (bf16[256,2048]{1,0:T(8,128)(2,1)}, bf16[256,2048]{1,0:T(8,128)(2,1)}, bf16[1024,512]{1,0:T(8,128)(2,1)}, bf16[1024,512]{1,0:T(8,128)(2,1)}, bf16[1...) custom-call(f32[1]{0:T(128)} %bitcast.5.refs_0_, ...), custom_call_target="tpu_custom_call", output_to_operand_aliasing={{2}: (10, {}), {3}: (11, {}), {4}: (12, {}), {5}: (13, {})} | custom-call | flops 4294967296 | tf_op jit(solution)/shard_map/product/pallas_call | solution.py:221
  190.8 1.4 collective-permute-start.24
  192.2 0.5 collective-permute-start.25
  192.7 26.2 %collective-permute-done.21.refs_0_ = bf16[256,2048]{1,0:T(8,128)(2,1)S(1)} collective-permute-done((bf16[256,2048]{1,0:T(8,128)(2,1)}, bf16[256,2048]{1,0:T(8,128)(2,1)S(1)}, u32[]{:S(2)}, u32[]{:S(2)}) %collective-permute-start.21) | collective-permute-done | bytes 1048608 | tf_op jit(solution)/shard_map/ppermute | solution.py:365
  218.9 1.9 collective-permute-start.26
  220.8 5.7 %collective-permute-start.27 = (bf16[256,2048]{1,0:T(8,128)(2,1)}, bf16[256,2048]{1,0:T(8,128)(2,1)}, u32[]{:S(2)}, u32[]{:S(2)}) collective-permute-start(bf16[256,2048]{1,0:T(8,128)(2,1)} %get-tuple-element.72), channel_id=1, source_target_pairs={{0,24},{1,0},{2,26},{3,2},{4,28},{5,4},{6,30},{7,6},{8,16},{9,8},{... | collective-permute-start | bytes 3145736 | tf_op jit(solution)/shard_map/ppermute | solution.py:365
  226.5 11.4 %feedback_update.2 = (f32[2,256,4096]{2,1,0:T(8,128)}, bf16[2,256,4096]{2,1,0:T(8,128)(2,1)}, bf16[2,256,4096]{2,1,0:T(8,128)(2,1)}, bf16[2,256,4096]{2,1,0:T(8,128)(2,1)}) custom-call(s32[1]{0:T(128)} %bitcast.4._, f32[1]{0:T(128)} %bitcast.3.scale_ref, bf16[256,2048]{1,0:T(8,128)(2,1)} %copy-done.6, bf16[256,2048]{1,0:T(8,128)(2,1)} %copy-done.7, ...), custom_call_target="tpu_custom_call" | custom-call | tf_op jit(solution)/shard_map/feedback_update/pallas_call | solution.py:332
  237.9 0.8 collective-permute-done.25.refs_3_
  238.7 19.5 %weight_update.1 = (f32[512,4096]{1,0:T(8,128)}, bf16[512,4096]{1,0:T(8,128)(2,1)}, bf16[512,4096]{1,0:T(8,128)(2,1)}, bf16[512,4096]{1,0:T(8,128)(2,1)}) custom-call(f32[1]{0:T(128)} %bitcast.3.scale_ref, bf16[1024,512]{1,0:T(8,128)(2,1)} %get-tuple-element.60.refs_0_, bf16[1024,512]{1,0:T(8,128)(2,1)} %collective-permute-done.23.refs_1_, ...), custom_call_target="tpu_custom_call" | custom-call | tf_op jit(solution)/shard_map/weight_update/pallas_call | solution.py:274
  258.3 12.6 %collective-permute-done.27.refs_1_ = bf16[256,2048]{1,0:T(8,128)(2,1)} collective-permute-done((bf16[256,2048]{1,0:T(8,128)(2,1)}, bf16[256,2048]{1,0:T(8,128)(2,1)}, u32[]{:S(2)}, u32[]{:S(2)}) %collective-permute-start.27) | collective-permute-done | bytes 1048608 | tf_op jit(solution)/shard_map/ppermute | solution.py:365
  270.8 11.4 %feedback_update.3 = (f32[2,256,4096]{2,1,0:T(8,128)}, bf16[2,256,4096]{2,1,0:T(8,128)(2,1)}, bf16[2,256,4096]{2,1,0:T(8,128)(2,1)}, bf16[2,256,4096]{2,1,0:T(8,128)(2,1)}) custom-call(s32[1]{0:T(128)} %bitcast.6._, f32[1]{0:T(128)} %bitcast.3.scale_ref, ...), custom_call_target="tpu_custom_call", output_to_operand_aliasing={{0}: (7, {}), {1}: (8, {}), {2}: (9, {}), {3}: (10, {})} | custom-call | tf_op jit(solution)/shard_map/feedback_update/pallas_call | solution.py:332
  (64 shorter events, 1.1 us)
Async XLA Ops:
  7.2 138.9 %all-gather.2.cloned.1.call-start = ((), (), s32[]{:S(2)}) async-start(), calls=%async_computation | async-start | bytes 18874368 | tf_op jit(solution)/shard_map/all_gather | solution.py:438
  7.2 1.6 copy-start
  8.8 9.8 %copy-start.1 = (bf16[256,4096]{1,0:T(8,128)(2,1)S(1)}, bf16[256,4096]{1,0:T(8,128)(2,1)}, u32[]{:S(2)}) copy-start(bf16[256,4096]{1,0:T(8,128)(2,1)} %x_ref.1) | copy-start | bytes 6291460
  8.8 9.8 %copy-start.2 = (bf16[2048,512]{1,0:T(8,128)(2,1)S(1)}, bf16[2048,512]{1,0:T(8,128)(2,1)}, u32[]{:S(2)}) copy-start(bf16[2048,512]{1,0:T(8,128)(2,1)} %errors_ref.1) | copy-start | bytes 6291460
  9.1 2.0 collective-permute-start
  11.1 33.0 %copy-start.9 = (bf16[512,1024]{1,0:T(8,128)(2,1)}, bf16[512,1024]{1,0:T(8,128)(2,1)S(1)}, u32[]{:S(2)}) copy-start(bf16[512,1024]{1,0:T(8,128)(2,1)S(1)} %constant_dynamic-update-slice_fusion.refs_3_) | copy-start | bytes 3145732
  11.1 27.1 %collective-permute-start.2 = (bf16[512,1024]{1,0:T(8,128)(2,1)S(1)}, bf16[512,1024]{1,0:T(8,128)(2,1)S(1)}, u32[]{:S(2)}, u32[]{:S(2)}) collective-permute-start(bf16[512,1024]{1,0:T(8,128)(2,1)S(1)} %constant_dynamic-update-slice_fusion.refs_3_), channel_id=1, source_target_pairs={{8,0},{9,1},{10,2},{11,3},{12,4},{13,5},{14,6},{15,7},{16,8},{17,9... | collective-permute-start | bytes 3145736 | tf_op jit(solution)/shard_map/ppermute | solution.py:365
  13.5 26.8 %collective-permute-start.1 = (bf16[512,1024]{1,0:T(8,128)(2,1)S(1)}, bf16[512,1024]{1,0:T(8,128)(2,1)S(1)}, u32[]{:S(2)}, u32[]{:S(2)}) collective-permute-start(bf16[512,1024]{1,0:T(8,128)(2,1)S(1)} %constant_dynamic-update-slice_fusion.refs_3_), channel_id=1, source_target_pairs={{0,8},{1,9},{2,10},{3,11},{4,12},{5,13},{6,14},{7,15},{8,16},{9,17... | collective-permute-start | bytes 3145736 | tf_op jit(solution)/shard_map/ppermute | solution.py:365
  17.1 26.9 %collective-permute-start.13 = (bf16[256,1024]{1,0:T(8,128)(2,1)S(1)}, bf16[256,1024]{1,0:T(8,128)(2,1)S(1)}, u32[]{:S(2)}, u32[]{:S(2)}) collective-permute-start(bf16[256,1024]{1,0:T(8,128)(2,1)S(1)} %get-tuple-element.48), channel_id=1, source_target_pairs={{0,4},{1,5},{2,6},{3,7},{4,0},{5,1},{6,2},{7,3},{8,12},{9,13},{10,... | collective-permute-start | bytes 1572872 | tf_op jit(solution)/shard_map/ppermute | solution.py:365
  18.6 25.4 %collective-permute-start.14 = (bf16[256,1024]{1,0:T(8,128)(2,1)S(1)}, bf16[256,1024]{1,0:T(8,128)(2,1)S(1)}, u32[]{:S(2)}, u32[]{:S(2)}) collective-permute-start(bf16[256,1024]{1,0:T(8,128)(2,1)S(1)} %get-tuple-element.50), channel_id=1, source_target_pairs={{0,6},{1,7},{2,4},{3,5},{4,2},{5,3},{6,0},{7,1},{8,14},{9,15},{10,... | collective-permute-start | bytes 1572872 | tf_op jit(solution)/shard_map/ppermute | solution.py:365
  38.2 107.8 %copy-start.10 = (bf16[512,1024]{1,0:T(8,128)(2,1)}, bf16[512,1024]{1,0:T(8,128)(2,1)S(1)}, u32[]{:S(2)}) copy-start(bf16[512,1024]{1,0:T(8,128)(2,1)S(1)} %collective-permute-done.2.refs_4_) | copy-start | bytes 3145732
  40.3 3.7 %copy-start.11 = (bf16[512,1024]{1,0:T(8,128)(2,1)}, bf16[512,1024]{1,0:T(8,128)(2,1)S(1)}, u32[]{:S(2)}) copy-start(bf16[512,1024]{1,0:T(8,128)(2,1)S(1)} %collective-permute-done.1.refs_2_) | copy-start | bytes 3145732
  40.3 3.6 %collective-permute-start.3 = (f32[8,128]{1,0:T(8,128)S(1)}, f32[8,128]{1,0:T(8,128)S(1)}, u32[]{:S(2)}, u32[]{:S(2)}) collective-permute-start(f32[8,128]{1,0:T(8,128)S(1)} %longest.1), channel_id=1, source_target_pairs={{0,1},{1,0},{2,3},{3,2},{4,5},{5,4},{6,7},{7,6},{8,9},{9,8},{10,11... | collective-permute-start | bytes 12296 | tf_op jit(solution)/shard_map/ppermute | solution.py:365
  44.1 117.6 %copy-start.3 = (bf16[512,1024]{1,0:T(8,128)(2,1)}, bf16[512,1024]{1,0:T(8,128)(2,1)S(1)}, u32[]{:S(2)}) copy-start(bf16[512,1024]{1,0:T(8,128)(2,1)S(1)} %constant_dynamic-update-slice_fusion.2.refs_4_) | copy-start | bytes 3145732
  44.1 26.0 %collective-permute-start.8 = (bf16[512,1024]{1,0:T(8,128)(2,1)S(1)}, bf16[512,1024]{1,0:T(8,128)(2,1)S(1)}, u32[]{:S(2)}, u32[]{:S(2)}) collective-permute-start(bf16[512,1024]{1,0:T(8,128)(2,1)S(1)} %collective-permute-done.2.refs_4_), channel_id=1, source_target_pairs={{8,0},{9,1},{10,2},{11,3},{12,4},{13,5},{14,6},{15,7},{16,8},{17,9... | collective-permute-start | bytes 3145736 | tf_op jit(solution)/shard_map/ppermute | solution.py:365
  46.6 28.2 %collective-permute-start.6 = (bf16[512,1024]{1,0:T(8,128)(2,1)}, bf16[512,1024]{1,0:T(8,128)(2,1)S(1)}, u32[]{:S(2)}, u32[]{:S(2)}) collective-permute-start(bf16[512,1024]{1,0:T(8,128)(2,1)} %copy-done.11), channel_id=1, source_target_pairs={{8,16},{9,17},{10,18},{11,19},{12,20},{13,21},{14,22},{15,23},{16,... | collective-permute-start | bytes 3145736 | tf_op jit(solution)/shard_map/ppermute | solution.py:365
  48.5 40.9 %collective-permute-start.18 = (bf16[512,1024]{1,0:T(8,128)(2,1)S(1)}, bf16[512,1024]{1,0:T(8,128)(2,1)S(1)}, u32[]{:S(2)}, u32[]{:S(2)}) collective-permute-start(bf16[512,1024]{1,0:T(8,128)(2,1)S(1)} %constant_dynamic-update-slice_fusion.2.refs_4_), channel_id=1, source_target_pairs={{8,0},{9,1},{10,2},{11,3},{12,4},{13,5},{14,6},{15,7},{16,8},{17,9... | collective-permute-start | bytes 3145736 | tf_op jit(solution)/shard_map/ppermute | solution.py:365
  52.5 43.0 %collective-permute-start.15 = (bf16[512,1024]{1,0:T(8,128)(2,1)S(1)}, bf16[512,1024]{1,0:T(8,128)(2,1)S(1)}, u32[]{:S(2)}, u32[]{:S(2)}) collective-permute-start(bf16[512,1024]{1,0:T(8,128)(2,1)S(1)} %constant_dynamic-update-slice_fusion.2.refs_4_), channel_id=1, source_target_pairs={{0,8},{1,9},{2,10},{3,11},{4,12},{5,13},{6,14},{7,15},{8,16},{9,17... | collective-permute-start | bytes 3145736 | tf_op jit(solution)/shard_map/ppermute | solution.py:365
  70.1 47.2 %copy-start.12 = (bf16[512,1024]{1,0:T(8,128)(2,1)}, bf16[512,1024]{1,0:T(8,128)(2,1)S(1)}, u32[]{:S(2)}) copy-start(bf16[512,1024]{1,0:T(8,128)(2,1)S(1)} %collective-permute-done.8.refs_5_) | copy-start | bytes 3145732
  70.1 34.1 %collective-permute-start.9 = (bf16[512,1024]{1,0:T(8,128)(2,1)S(1)}, bf16[512,1024]{1,0:T(8,128)(2,1)S(1)}, u32[]{:S(2)}, u32[]{:S(2)}) collective-permute-start(bf16[512,1024]{1,0:T(8,128)(2,1)S(1)} %collective-permute-done.8.refs_5_), channel_id=1, source_target_pairs={{8,0},{9,1},{10,2},{11,3},{12,4},{13,5},{14,6},{15,7}} | collective-permute-start | bytes 3145736 | tf_op jit(solution)/shard_map/ppermute | solution.py:365
  74.8 69.9 %copy-start.13 = (bf16[512,1024]{1,0:T(8,128)(2,1)}, bf16[512,1024]{1,0:T(8,128)(2,1)S(1)}, u32[]{:S(2)}) copy-start(bf16[512,1024]{1,0:T(8,128)(2,1)S(1)} %collective-permute-done.6.refs_1_) | copy-start | bytes 3145732
  74.8 42.6 %collective-permute-start.7 = (bf16[512,1024]{1,0:T(8,128)(2,1)S(1)}, bf16[512,1024]{1,0:T(8,128)(2,1)S(1)}, u32[]{:S(2)}, u32[]{:S(2)}) collective-permute-start(bf16[512,1024]{1,0:T(8,128)(2,1)S(1)} %collective-permute-done.6.refs_1_), channel_id=1, source_target_pairs={{16,24},{17,25},{18,26},{19,27},{20,28},{21,29},{22,30},{23,31}} | collective-permute-start | bytes 3145736 | tf_op jit(solution)/shard_map/ppermute | solution.py:365
  89.4 6.1 %copy-start.4 = (bf16[512,1024]{1,0:T(8,128)(2,1)}, bf16[512,1024]{1,0:T(8,128)(2,1)S(1)}, u32[]{:S(2)}) copy-start(bf16[512,1024]{1,0:T(8,128)(2,1)S(1)} %collective-permute-done.18.refs_5_) | copy-start | bytes 3145732
  89.4 32.4 %collective-permute-start.19 = (bf16[512,1024]{1,0:T(8,128)(2,1)S(1)}, bf16[512,1024]{1,0:T(8,128)(2,1)}, u32[]{:S(2)}, u32[]{:S(2)}) collective-permute-start(bf16[512,1024]{1,0:T(8,128)(2,1)S(1)} %collective-permute-done.18.refs_5_), channel_id=1, source_target_pairs={{8,0},{9,1},{10,2},{11,3},{12,4},{13,5},{14,6},{15,7},{16,8},{17,9... | collective-permute-start | bytes 3145736 | tf_op jit(solution)/shard_map/ppermute | solution.py:365
  95.5 26.3 %copy-start.5 = (bf16[512,1024]{1,0:T(8,128)(2,1)}, bf16[512,1024]{1,0:T(8,128)(2,1)S(1)}, u32[]{:S(2)}) copy-start(bf16[512,1024]{1,0:T(8,128)(2,1)S(1)} %collective-permute-done.15.refs_3_) | copy-start | bytes 3145732
  95.5 41.3 %collective-permute-start.16 = (bf16[512,1024]{1,0:T(8,128)(2,1)S(1)}, bf16[512,1024]{1,0:T(8,128)(2,1)}, u32[]{:S(2)}, u32[]{:S(2)}) collective-permute-start(bf16[512,1024]{1,0:T(8,128)(2,1)S(1)} %collective-permute-done.15.refs_3_), channel_id=1, source_target_pairs={{8,16},{9,17},{10,18},{11,19},{12,20},{13,21},{14,22},{15,23},{16,... | collective-permute-start | bytes 3145736 | tf_op jit(solution)/shard_map/ppermute | solution.py:365
  99.2 1.2 collective-permute-start.4
  100.5 3.7 %collective-permute-start.5 = (f32[8,128]{1,0:T(8,128)S(1)}, f32[8,128]{1,0:T(8,128)S(1)}, u32[]{:S(2)}, u32[]{:S(2)}) collective-permute-start(f32[8,128]{1,0:T(8,128)S(1)} %add_select_fusion.2), channel_id=1, source_target_pairs={{0,4},{1,5},{2,6},{3,7},{4,0},{5,1},{6,2},{7,3},{8,12},{9,13},{10,... | collective-permute-start | bytes 12296 | tf_op jit(solution)/shard_map/ppermute | solution.py:365
  104.2 40.5 %copy-start.14 = (bf16[512,1024]{1,0:T(8,128)(2,1)}, bf16[512,1024]{1,0:T(8,128)(2,1)S(1)}, u32[]{:S(2)}) copy-start(bf16[512,1024]{1,0:T(8,128)(2,1)S(1)} %collective-permute-done.9.refs_6_) | copy-start | bytes 3145732
  117.3 27.4 %copy-start.15 = (bf16[512,1024]{1,0:T(8,128)(2,1)}, bf16[512,1024]{1,0:T(8,128)(2,1)S(1)}, u32[]{:S(2)}) copy-start(bf16[512,1024]{1,0:T(8,128)(2,1)S(1)} %collective-permute-done.7.refs_0_) | copy-start | bytes 3145732
  117.3 24.9 %collective-permute-start.11 = (f32[8,128]{1,0:T(8,128)S(1)}, f32[8,128]{1,0:T(8,128)S(1)}, u32[]{:S(2)}, u32[]{:S(2)}) collective-permute-start(f32[8,128]{1,0:T(8,128)S(1)} %add_select_fusion.1), channel_id=1, source_target_pairs={{0,16},{1,17},{2,18},{3,19},{4,20},{5,21},{6,22},{7,23},{8,24},{9,... | collective-permute-start | bytes 12296 | tf_op jit(solution)/shard_map/ppermute | solution.py:365
  117.3 24.9 %collective-permute-start.12 = (f32[8,128]{1,0:T(8,128)S(1)}, f32[8,128]{1,0:T(8,128)S(1)}, u32[]{:S(2)}, u32[]{:S(2)}) collective-permute-start(f32[8,128]{1,0:T(8,128)S(1)} %add_select_fusion.1), channel_id=1, source_target_pairs={{0,24},{1,25},{2,26},{3,27},{4,28},{5,29},{6,30},{7,31},{8,16},{9,... | collective-permute-start | bytes 12296 | tf_op jit(solution)/shard_map/ppermute | solution.py:365
  121.3 20.9 %collective-permute-start.10 = (f32[8,128]{1,0:T(8,128)S(1)}, f32[8,128]{1,0:T(8,128)S(1)}, u32[]{:S(2)}, u32[]{:S(2)}) collective-permute-start(f32[8,128]{1,0:T(8,128)S(1)} %add_select_fusion.1), channel_id=1, source_target_pairs={{0,8},{1,9},{2,10},{3,11},{4,12},{5,13},{6,14},{7,15},{8,0},{9,1},... | collective-permute-start | bytes 12296 | tf_op jit(solution)/shard_map/ppermute | solution.py:365
  121.7 40.0 %collective-permute-start.20 = (bf16[512,1024]{1,0:T(8,128)(2,1)}, bf16[512,1024]{1,0:T(8,128)(2,1)}, u32[]{:S(2)}, u32[]{:S(2)}) collective-permute-start(bf16[512,1024]{1,0:T(8,128)(2,1)} %collective-permute-done.19.refs_6_), channel_id=1, source_target_pairs={{8,0},{9,1},{10,2},{11,3},{12,4},{13,5},{14,6},{15,7}} | collective-permute-start | bytes 3145736 | tf_op jit(solution)/shard_map/ppermute | solution.py:365
  136.7 25.0 %collective-permute-start.17 = (bf16[512,1024]{1,0:T(8,128)(2,1)}, bf16[512,1024]{1,0:T(8,128)(2,1)}, u32[]{:S(2)}, u32[]{:S(2)}) collective-permute-start(bf16[512,1024]{1,0:T(8,128)(2,1)} %collective-permute-done.16.refs_2_), channel_id=1, source_target_pairs={{16,24},{17,25},{18,26},{19,27},{20,28},{21,29},{22,30},{23,31}} | collective-permute-start | bytes 3145736 | tf_op jit(solution)/shard_map/ppermute | solution.py:365
  174.0 44.9 %collective-permute-start.21 = (bf16[256,2048]{1,0:T(8,128)(2,1)}, bf16[256,2048]{1,0:T(8,128)(2,1)S(1)}, u32[]{:S(2)}, u32[]{:S(2)}) collective-permute-start(bf16[256,2048]{1,0:T(8,128)(2,1)} %get-tuple-element.52), channel_id=1, source_target_pairs={{0,0},{1,24},{2,2},{3,26},{4,4},{5,28},{6,6},{7,30},{8,8},{9,16},{... | collective-permute-start | bytes 3145736 | tf_op jit(solution)/shard_map/ppermute | solution.py:365
  177.6 43.2 %collective-permute-start.22 = (bf16[256,2048]{1,0:T(8,128)(2,1)}, bf16[256,2048]{1,0:T(8,128)(2,1)S(1)}, u32[]{:S(2)}, u32[]{:S(2)}) collective-permute-start(bf16[256,2048]{1,0:T(8,128)(2,1)} %get-tuple-element.53), channel_id=1, source_target_pairs={{0,16},{1,8},{2,18},{3,10},{4,20},{5,12},{6,22},{7,14},{8,24},{9,0... | collective-permute-start | bytes 3145736 | tf_op jit(solution)/shard_map/ppermute | solution.py:365
  190.7 47.1 %collective-permute-start.23 = (bf16[1024,512]{1,0:T(8,128)(2,1)}, bf16[1024,512]{1,0:T(8,128)(2,1)}, u32[]{:S(2)}, u32[]{:S(2)}) collective-permute-start(bf16[1024,512]{1,0:T(8,128)(2,1)} %get-tuple-element.61), channel_id=1, source_target_pairs={{0,2},{1,3},{2,0},{3,1},{4,6},{5,7},{6,4},{7,5},{8,10},{9,11},{10,... | collective-permute-start | bytes 3145736 | tf_op jit(solution)/shard_map/ppermute | solution.py:365
  190.8 47.1 %collective-permute-start.24 = (bf16[1024,512]{1,0:T(8,128)(2,1)}, bf16[1024,512]{1,0:T(8,128)(2,1)}, u32[]{:S(2)}, u32[]{:S(2)}) collective-permute-start(bf16[1024,512]{1,0:T(8,128)(2,1)} %get-tuple-element.62), channel_id=1, source_target_pairs={{0,4},{1,5},{2,6},{3,7},{4,0},{5,1},{6,2},{7,3},{8,12},{9,13},{10,... | collective-permute-start | bytes 3145736 | tf_op jit(solution)/shard_map/ppermute | solution.py:365
  192.2 46.5 %collective-permute-start.25 = (bf16[1024,512]{1,0:T(8,128)(2,1)}, bf16[1024,512]{1,0:T(8,128)(2,1)}, u32[]{:S(2)}, u32[]{:S(2)}) collective-permute-start(bf16[1024,512]{1,0:T(8,128)(2,1)} %get-tuple-element.63), channel_id=1, source_target_pairs={{0,6},{1,7},{2,4},{3,5},{4,2},{5,3},{6,0},{7,1},{8,14},{9,15},{10,... | collective-permute-start | bytes 3145736 | tf_op jit(solution)/shard_map/ppermute | solution.py:365
  218.9 7.6 %copy-start.6 = (bf16[256,2048]{1,0:T(8,128)(2,1)}, bf16[256,2048]{1,0:T(8,128)(2,1)S(1)}, u32[]{:S(2)}) copy-start(bf16[256,2048]{1,0:T(8,128)(2,1)S(1)} %collective-permute-done.21.refs_0_) | copy-start | bytes 3145732
  218.9 39.4 %collective-permute-start.26 = (bf16[256,2048]{1,0:T(8,128)(2,1)}, bf16[256,2048]{1,0:T(8,128)(2,1)S(1)}, u32[]{:S(2)}, u32[]{:S(2)}) collective-permute-start(bf16[256,2048]{1,0:T(8,128)(2,1)} %get-tuple-element.70), channel_id=1, source_target_pairs={{0,8},{1,16},{2,10},{3,18},{4,12},{5,20},{6,14},{7,22},{8,0},{9,24... | collective-permute-start | bytes 3145736 | tf_op jit(solution)/shard_map/ppermute | solution.py:365
  220.8 5.7 %copy-start.7 = (bf16[256,2048]{1,0:T(8,128)(2,1)}, bf16[256,2048]{1,0:T(8,128)(2,1)S(1)}, u32[]{:S(2)}) copy-start(bf16[256,2048]{1,0:T(8,128)(2,1)S(1)} %collective-permute-done.22.refs_1_) | copy-start | bytes 3145732
  220.8 50.1 %collective-permute-start.27 = (bf16[256,2048]{1,0:T(8,128)(2,1)}, bf16[256,2048]{1,0:T(8,128)(2,1)}, u32[]{:S(2)}, u32[]{:S(2)}) collective-permute-start(bf16[256,2048]{1,0:T(8,128)(2,1)} %get-tuple-element.72), channel_id=1, source_target_pairs={{0,24},{1,0},{2,26},{3,2},{4,28},{5,4},{6,30},{7,6},{8,16},{9,8},{... | collective-permute-start | bytes 3145736 | tf_op jit(solution)/shard_map/ppermute | solution.py:365
  258.3 12.6 %copy-start.8 = (bf16[256,2048]{1,0:T(8,128)(2,1)}, bf16[256,2048]{1,0:T(8,128)(2,1)S(1)}, u32[]{:S(2)}) copy-start(bf16[256,2048]{1,0:T(8,128)(2,1)S(1)} %collective-permute-done.26.refs_0_) | copy-start | bytes 3145732
Sparse Core Ops, SparseCore 0:
  44.3 90.2 all-gather.1
